TPU v7x, 32 devices: a whole 2x2x4 slice. The times are simulated.
32 devices in a mesh: blk: 8 (over y, x, core), mpo: 4 (over z).
Axes of the slice: x: 2, y: 2, z: 4, core: 2. Of those that a mesh axis runs over, the one named last changes fastest.
Arguments:
- theta: float32 [16, 128, 16, 128], P('blk'), may hold values from -6 to 6
- block_dims: int32 [16, 2], P('blk'), may hold values from 32 to 128, as said below
- pair_mask: int32 [24, 16], P(None, 'blk'), may hold values 0 or 1
- term_charge: int32 [24], replicated, may hold values from -1 to 1
- left_env: float32 [24, 16, 128, 128], P('mpo', 'blk'), may hold values from -0.5 to 0.5
- right_env: float32 [24, 16, 128, 128], P('mpo', 'blk'), may hold values from -0.5 to 0.5
- site_one: float32 [24, 4, 4], replicated, may hold values from -0.625 to 0.625
- site_two: float32 [24, 4, 4], replicated, may hold values from -3 to 3
Outputs:
- hpsi: float32 [16, 128, 16, 128], P('blk', 'mpo')
Inputs may be any that keep to these rules, and one draw needn't show every extreme that they name: `block_dims`: kept dimensions of each sector; rows and columns of a block beyond them are empty. The first sector keeps 128 on both sides.
All inputs are finite; a program needn't handle non-finite values. No bound on the sum of `pair_mask` on one device may be relied on, other than what follows from the above.
Results may differ from a plain program's by a relative error of at most 0.0003.
Values sent between devices are 32-bit elements; how exact they have to be, the bound alone decides.
No kernel may reach another device: no remote copies, remote signals or barrier semaphores. Data moves between devices by JAX's collectives and lax.ppermute only.
A program may use at most 64 MiB of HBM per device.

v0:
```python
import jax
import jax.numpy as jnp
from jax import lax
from jax.sharding import PartitionSpec as P


def extended(cells, sides, width):
    for axis, dim in sides:
        count = lax.axis_size(axis)
        ends = count - 1
        head = lax.slice_in_dim(cells, 0, width, axis=dim)
        tail = lax.slice_in_dim(cells, cells.shape[dim] - width, cells.shape[dim], axis=dim)
        cells = jnp.concatenate(
            [
                lax.ppermute(tail, axis, [(i, (i + 1) % count) for i in range(ends)]),
                cells,
                lax.ppermute(head, axis, [((i + 1) % count, i) for i in range(ends)]),
            ],
            axis=dim,
        )
    return cells


def sector_mask(block_dims, bond_cap):
    positions = jnp.arange(bond_cap, dtype=jnp.int32)
    left_ok = positions[None, :] < block_dims[:, 0:1]
    right_ok = positions[None, :] < block_dims[:, 1:2]
    return (left_ok[:, :, None] & right_ok[:, None, :]).astype(jnp.float32)


def make_pair(first_op, second_op):
    states = first_op.shape[0]
    return (first_op[:, None, :, None] * second_op[None, :, None, :]).reshape(
        states * states, states * states
    )


def apply_term(left_rows, source, site_pair, right_block):
    highest = lax.Precision.HIGHEST
    row_count = left_rows.shape[0]
    moved = jnp.dot(
        left_rows,
        source.reshape(source.shape[0], -1),
        precision=highest,
        preferred_element_type=jnp.float32,
    )
    moved = moved.reshape(row_count, source.shape[1], source.shape[2])
    mixed = jnp.einsum("pq,aqd->apd", site_pair, moved, precision=highest)
    return jnp.einsum("apd,bd->apb", mixed, right_block, precision=highest)


def all_sectors(running, padded, left_all, right_all, charge, site_pair, allowed):
    sectors = left_all.shape[0]
    source_index = jnp.arange(sectors, dtype=jnp.int32) + 1 - charge

    def per_sector(left_rows, index, right_block):
        source = lax.dynamic_index_in_dim(padded, index, 0, keepdims=False)
        return apply_term(left_rows, source, site_pair, right_block)

    terms = jax.vmap(per_sector)(left_all, source_index, right_all)
    return running + allowed.astype(jnp.float32)[:, None, None, None] * terms


def body(theta, block_dims, pair_mask, term_charge, left_env, right_env, site_one, site_two):
    bond_cap = theta.shape[1]
    group_index = lax.axis_index("mpo")
    group_count = lax.axis_size("mpo")
    row_count = bond_cap // group_count
    first_row = group_index * row_count
    block_mask = sector_mask(block_dims, bond_cap)
    masked = theta * block_mask[:, :, None, :]
    padded = extended(masked, (("blk", 0),), 1)
    row_mask = lax.dynamic_slice_in_dim(block_mask, first_row, row_count, 1)
    term_count = left_env.shape[0]
    first_term = group_index * term_count

    def local_term(w, running):
        term_index = first_term + w
        charge = lax.dynamic_index_in_dim(term_charge, term_index, 0, keepdims=False)
        allowed = lax.dynamic_index_in_dim(pair_mask, term_index, 0, keepdims=False)
        first_op = lax.dynamic_index_in_dim(site_one, term_index, 0, keepdims=False)
        second_op = lax.dynamic_index_in_dim(site_two, term_index, 0, keepdims=False)
        left_all = lax.dynamic_index_in_dim(left_env, w, 0, keepdims=False)
        right_all = lax.dynamic_index_in_dim(right_env, w, 0, keepdims=False)
        return all_sectors(
            running, padded, left_all, right_all, charge, make_pair(first_op, second_op), allowed
        )

    partial_value = lax.fori_loop(0, term_count, local_term, jnp.zeros(theta.shape, jnp.float32))
    mine = lax.psum_scatter(partial_value, "mpo", scatter_dimension=1, tiled=True)
    return mine * row_mask[:, :, None, :]


def solution(mesh):
    placed = (
        P("blk", None, None, None),
        P("blk", None),
        P(None, "blk"),
        P(),
        P("mpo", "blk", None, None),
        P("mpo", "blk", None, None),
        P(),
        P(),
    )
    return jax.shard_map(
        body, mesh=mesh, in_specs=placed, out_specs=P("blk", "mpo", None, None), check_vma=False
    )
```

profile of v0, /device:TPU:3, one launch (start us, length us, event | category | flops | bytes accessed | tf_op | source)
XLA Modules:
  0.0 207.9 jit_solution(10617488448867002309)
XLA Ops:
  7.7 2.2 %copy_multiply_fusion = f32[2,128,16,128]{3,1,2,0:T(8,128)S(1)} fusion(f32[2,128,16,128]{3,2,1,0:T(8,128)} %param.10, f32[2,128,128]{2,1,0:T(8,128)S(1)} %and_convert_fusion), kind=kLoop, calls=%fused_computation.27 | loop fusion | flops 524288 | bytes 4325376 | tf_op jit(solution)/shard_map/mul | solution.py:71
  11.1 3.7 %collective-permute-start = (f32[1,128,16,128]{3,1,2,0:T(8,128)}, f32[1,128,16,128]{3,1,2,0:T(8,128)}, u32[]{:S(2)}, u32[]{:S(2)}) collective-permute-start(f32[1,128,16,128]{3,1,2,0:T(8,128)} %get-tuple-element.262), channel_id=1, source_target_pairs={{0,4},{4,8},{8,12},{12,16},{16,20},{20,24},{24,28},{1,5},{5,9},{9,... | collective-permute-start | bytes 3145736 | tf_op jit(solution)/shard_map/ppermute | solution.py:15
  14.8 1.9 collective-permute-start.1
  17.1 18.4 %collective-permute-done = f32[1,128,16,128]{3,1,2,0:T(8,128)} collective-permute-done((f32[1,128,16,128]{3,1,2,0:T(8,128)}, f32[1,128,16,128]{3,1,2,0:T(8,128)}, u32[]{:S(2)}, u32[]{:S(2)}) %collective-permute-start) | collective-permute-done | bytes 1048608 | tf_op jit(solution)/shard_map/ppermute | solution.py:15
  35.5 4.3 %collective-permute-done.1 = f32[1,128,16,128]{3,1,2,0:T(8,128)} collective-permute-done((f32[1,128,16,128]{3,1,2,0:T(8,128)S(1)}, f32[1,128,16,128]{3,1,2,0:T(8,128)}, u32[]{:S(2)}, u32[]{:S(2)}) %collective-permute-start.1) | collective-permute-done | bytes 1048608 | tf_op jit(solution)/shard_map/ppermute | solution.py:17
  39.7 3.9 %pad_maximum_fusion = f32[4,128,16,128]{3,1,2,0:T(8,128)} fusion(f32[1,128,16,128]{3,1,2,0:T(8,128)} %collective-permute-done.1, f32[2,128,16,128]{3,1,2,0:T(8,128)S(1)} %copy_multiply_fusion, f32[1,128,16,128]{3,1,2,0:T(8,128)} %collective-permute-done), kind=kLoop, calls=%fused_computation.25 | loop fusion | flops 2097152 | bytes 8388608 | tf_op jit(solution)/shard_map/concatenate | solution.py:13
  43.6 106.1 %while.14 = (s32[]{:T(128)}, f32[2,128,16,128]{3,1,2,0:T(8,128)}, s32[]{:T(128)}, s32[24,2]{1,0:T(8,128)S(1)}, f32[6,2,128,128]{3,2,1,0:T(8,128)}, /*index=5*/s3...) while((s32[]{:T(128)}, f32[2,128,16,128]{3,1,2,0:T(8,128)}, ...), condition=%wide.region_1.2_spmd.clone, body=%wide.region_0.1_spmd.clone.sunk | while | flops 1712849152 | bytes 44307156 | solution.py:89
  44.9 2.9 %gather_fusion = f32[2,128,16,128]{3,1,2,0:T(8,128)S(1)} fusion(f32[4,128,16,128]{3,1,2,0:T(8,128)} %get-tuple-element.363, s32[2]{0:T(128)S(1)} %fusion.38), kind=kCustom, calls=%fused_computation.clone.clone.1 | custom fusion | bytes 4194336 | tf_op jit(solution)/shard_map/while/body/eval_jaxpr/vmap(jit(dynamic_index_in_dim))/gather | solution.py:57
  49.6 3.6 %fusion.39 = f32[2,128,2048]{2,1,0:T(8,128)S(1)} fusion(f32[2,128,2048]{1,2,0:T(8,128)} %bitcast.73, f32[6,2,128,128]{3,2,1,0:T(8,128)} %get-tuple-element.361, s32[]{:T(128)S(6)} %copy.54), kind=kOutput, calls=%fused_computation.8.clone.1 | convolution fusion | flops 805306368 | bytes 4325380 | tf_op jit(solution)/shard_map/while/body/eval_jaxpr/vmap()/dot_general | solution.py:41
  53.6 1.9 fusion.40
  55.6 4.4 %select_add_fusion.2 = f32[2,128,16,128]{3,1,2,0:T(8,128)S(1)} fusion(f32[2,128,16,128]{3,1,2,0:T(8,128)S(1)} %copy-done, f32[2,128,16,128]{3,2,1,0:T(8,128)S(1)} %fusion.40, f32[2]{0:T(128)S(1)} %fusion.41, pred[]{:T(512)S(6)} %compare.3, f32[6,2,128,128]{3,2,1,0:T(8,128)} %get-tuple-element.366, s32[]{:T(128)S(6)} %copy.54), kind=kOutput, calls=%fused_computation.5.clone.1 | convolution fusion | flops 806879232 | bytes 6422541 | tf_op jit(solution)/shard_map/while/body/eval_jaxpr/vmap(apd,bd->apb)/dot_general | solution.py:49
  62.6 2.9 %gather_fusion = f32[2,128,16,128]{3,1,2,0:T(8,128)S(1)} fusion(f32[4,128,16,128]{3,1,2,0:T(8,128)} %get-tuple-element.363, s32[2]{0:T(128)S(1)} %fusion.38), kind=kCustom, calls=%fused_computation.clone.clone.1 | custom fusion | bytes 4194336 | tf_op jit(solution)/shard_map/while/body/eval_jaxpr/vmap(jit(dynamic_index_in_dim))/gather | solution.py:57
  67.3 3.6 %fusion.39 = f32[2,128,2048]{2,1,0:T(8,128)S(1)} fusion(f32[2,128,2048]{1,2,0:T(8,128)} %bitcast.73, f32[6,2,128,128]{3,2,1,0:T(8,128)} %get-tuple-element.361, s32[]{:T(128)S(6)} %copy.54), kind=kOutput, calls=%fused_computation.8.clone.1 | convolution fusion | flops 805306368 | bytes 4325380 | tf_op jit(solution)/shard_map/while/body/eval_jaxpr/vmap()/dot_general | solution.py:41
  71.3 1.9 fusion.40
  73.2 4.4 %select_add_fusion.2 = f32[2,128,16,128]{3,1,2,0:T(8,128)S(1)} fusion(f32[2,128,16,128]{3,1,2,0:T(8,128)S(1)} %copy-done, f32[2,128,16,128]{3,2,1,0:T(8,128)S(1)} %fusion.40, f32[2]{0:T(128)S(1)} %fusion.41, pred[]{:T(512)S(6)} %compare.3, f32[6,2,128,128]{3,2,1,0:T(8,128)} %get-tuple-element.366, s32[]{:T(128)S(6)} %copy.54), kind=kOutput, calls=%fused_computation.5.clone.1 | convolution fusion | flops 806879232 | bytes 6422541 | tf_op jit(solution)/shard_map/while/body/eval_jaxpr/vmap(apd,bd->apb)/dot_general | solution.py:49
  80.3 2.9 %gather_fusion = f32[2,128,16,128]{3,1,2,0:T(8,128)S(1)} fusion(f32[4,128,16,128]{3,1,2,0:T(8,128)} %get-tuple-element.363, s32[2]{0:T(128)S(1)} %fusion.38), kind=kCustom, calls=%fused_computation.clone.clone.1 | custom fusion | bytes 4194336 | tf_op jit(solution)/shard_map/while/body/eval_jaxpr/vmap(jit(dynamic_index_in_dim))/gather | solution.py:57
  85.0 3.6 %fusion.39 = f32[2,128,2048]{2,1,0:T(8,128)S(1)} fusion(f32[2,128,2048]{1,2,0:T(8,128)} %bitcast.73, f32[6,2,128,128]{3,2,1,0:T(8,128)} %get-tuple-element.361, s32[]{:T(128)S(6)} %copy.54), kind=kOutput, calls=%fused_computation.8.clone.1 | convolution fusion | flops 805306368 | bytes 4325380 | tf_op jit(solution)/shard_map/while/body/eval_jaxpr/vmap()/dot_general | solution.py:41
  90.9 4.4 %select_add_fusion.2 = f32[2,128,16,128]{3,1,2,0:T(8,128)S(1)} fusion(f32[2,128,16,128]{3,1,2,0:T(8,128)S(1)} %copy-done, f32[2,128,16,128]{3,2,1,0:T(8,128)S(1)} %fusion.40, f32[2]{0:T(128)S(1)} %fusion.41, pred[]{:T(512)S(6)} %compare.3, f32[6,2,128,128]{3,2,1,0:T(8,128)} %get-tuple-element.366, s32[]{:T(128)S(6)} %copy.54), kind=kOutput, calls=%fused_computation.5.clone.1 | convolution fusion | flops 806879232 | bytes 6422541 | tf_op jit(solution)/shard_map/while/body/eval_jaxpr/vmap(apd,bd->apb)/dot_general | solution.py:49
  97.9 2.9 %gather_fusion = f32[2,128,16,128]{3,1,2,0:T(8,128)S(1)} fusion(f32[4,128,16,128]{3,1,2,0:T(8,128)} %get-tuple-element.363, s32[2]{0:T(128)S(1)} %fusion.38), kind=kCustom, calls=%fused_computation.clone.clone.1 | custom fusion | bytes 4194336 | tf_op jit(solution)/shard_map/while/body/eval_jaxpr/vmap(jit(dynamic_index_in_dim))/gather | solution.py:57
  102.7 3.6 %fusion.39 = f32[2,128,2048]{2,1,0:T(8,128)S(1)} fusion(f32[2,128,2048]{1,2,0:T(8,128)} %bitcast.73, f32[6,2,128,128]{3,2,1,0:T(8,128)} %get-tuple-element.361, s32[]{:T(128)S(6)} %copy.54), kind=kOutput, calls=%fused_computation.8.clone.1 | convolution fusion | flops 805306368 | bytes 4325380 | tf_op jit(solution)/shard_map/while/body/eval_jaxpr/vmap()/dot_general | solution.py:41
  106.7 1.9 fusion.40
  108.6 4.4 %select_add_fusion.2 = f32[2,128,16,128]{3,1,2,0:T(8,128)S(1)} fusion(f32[2,128,16,128]{3,1,2,0:T(8,128)S(1)} %copy-done, f32[2,128,16,128]{3,2,1,0:T(8,128)S(1)} %fusion.40, f32[2]{0:T(128)S(1)} %fusion.41, pred[]{:T(512)S(6)} %compare.3, f32[6,2,128,128]{3,2,1,0:T(8,128)} %get-tuple-element.366, s32[]{:T(128)S(6)} %copy.54), kind=kOutput, calls=%fused_computation.5.clone.1 | convolution fusion | flops 806879232 | bytes 6422541 | tf_op jit(solution)/shard_map/while/body/eval_jaxpr/vmap(apd,bd->apb)/dot_general | solution.py:49
  115.6 2.9 %gather_fusion = f32[2,128,16,128]{3,1,2,0:T(8,128)S(1)} fusion(f32[4,128,16,128]{3,1,2,0:T(8,128)} %get-tuple-element.363, s32[2]{0:T(128)S(1)} %fusion.38), kind=kCustom, calls=%fused_computation.clone.clone.1 | custom fusion | bytes 4194336 | tf_op jit(solution)/shard_map/while/body/eval_jaxpr/vmap(jit(dynamic_index_in_dim))/gather | solution.py:57
  120.3 3.6 %fusion.39 = f32[2,128,2048]{2,1,0:T(8,128)S(1)} fusion(f32[2,128,2048]{1,2,0:T(8,128)} %bitcast.73, f32[6,2,128,128]{3,2,1,0:T(8,128)} %get-tuple-element.361, s32[]{:T(128)S(6)} %copy.54), kind=kOutput, calls=%fused_computation.8.clone.1 | convolution fusion | flops 805306368 | bytes 4325380 | tf_op jit(solution)/shard_map/while/body/eval_jaxpr/vmap()/dot_general | solution.py:41
  124.3 1.9 fusion.40
  126.3 4.4 %select_add_fusion.2 = f32[2,128,16,128]{3,1,2,0:T(8,128)S(1)} fusion(f32[2,128,16,128]{3,1,2,0:T(8,128)S(1)} %copy-done, f32[2,128,16,128]{3,2,1,0:T(8,128)S(1)} %fusion.40, f32[2]{0:T(128)S(1)} %fusion.41, pred[]{:T(512)S(6)} %compare.3, f32[6,2,128,128]{3,2,1,0:T(8,128)} %get-tuple-element.366, s32[]{:T(128)S(6)} %copy.54), kind=kOutput, calls=%fused_computation.5.clone.1 | convolution fusion | flops 806879232 | bytes 6422541 | tf_op jit(solution)/shard_map/while/body/eval_jaxpr/vmap(apd,bd->apb)/dot_general | solution.py:49
  133.3 2.9 %gather_fusion = f32[2,128,16,128]{3,1,2,0:T(8,128)S(1)} fusion(f32[4,128,16,128]{3,1,2,0:T(8,128)} %get-tuple-element.363, s32[2]{0:T(128)S(1)} %fusion.38), kind=kCustom, calls=%fused_computation.clone.clone.1 | custom fusion | bytes 4194336 | tf_op jit(solution)/shard_map/while/body/eval_jaxpr/vmap(jit(dynamic_index_in_dim))/gather | solution.py:57
  138.0 3.6 %fusion.39 = f32[2,128,2048]{2,1,0:T(8,128)S(1)} fusion(f32[2,128,2048]{1,2,0:T(8,128)} %bitcast.73, f32[6,2,128,128]{3,2,1,0:T(8,128)} %get-tuple-element.361, s32[]{:T(128)S(6)} %copy.54), kind=kOutput, calls=%fused_computation.8.clone.1 | convolution fusion | flops 805306368 | bytes 4325380 | tf_op jit(solution)/shard_map/while/body/eval_jaxpr/vmap()/dot_general | solution.py:41
  143.9 4.4 %select_add_fusion.2 = f32[2,128,16,128]{3,1,2,0:T(8,128)S(1)} fusion(f32[2,128,16,128]{3,1,2,0:T(8,128)S(1)} %copy-done, f32[2,128,16,128]{3,2,1,0:T(8,128)S(1)} %fusion.40, f32[2]{0:T(128)S(1)} %fusion.41, pred[]{:T(512)S(6)} %compare.3, f32[6,2,128,128]{3,2,1,0:T(8,128)} %get-tuple-element.366, s32[]{:T(128)S(6)} %copy.54), kind=kOutput, calls=%fused_computation.5.clone.1 | convolution fusion | flops 806879232 | bytes 6422541 | tf_op jit(solution)/shard_map/while/body/eval_jaxpr/vmap(apd,bd->apb)/dot_general | solution.py:49
  149.6 2.8 %copy.32 = f32[2,128,16,128]{3,2,0,1:T(8,128)S(1)} copy(f32[2,128,16,128]{3,1,2,0:T(8,128)} %get-tuple-element.174) | data formatting | bytes 4194304
  152.5 3.0 %copy.45 = f32[16,8,32,128]{3,1,2,0:T(8,128)} copy(f32[16,8,32,128]{3,2,1,0:T(8,128)S(1)} %bitcast.76) | data formatting | bytes 4194304
  155.5 43.6 %reduce-scatter.5.cloned.1.call-done = f32[32,4096]{1,0:T(8,128)} async-done(((f32[128,4096]{1,0:T(8,128)}), f32[32,4096]{1,0:T(8,128)}) %reduce-scatter.5.cloned.1.call-update) | async-done | bytes 524304
  (95 shorter events, 37.6 us)
Async XLA Ops:
  6.5 192.5 %reduce-scatter.5.cloned.1.call-start = ((), (), s32[]{:S(2)}) async-start(), calls=%async_computation.1 | async-start | bytes 2621440
  9.9 6.8 %copy-start.4 = (s32[24,2]{0,1:T(2,128)S(1)}, s32[24,2]{0,1:T(2,128)}, u32[]{:S(2)}) copy-start(s32[24,2]{0,1:T(2,128)} %param.12) | copy-start | bytes 580
  10.0 6.9 %copy-start.2 = (f32[24,4,4]{0,2,1:T(4,128)S(1)}, f32[24,4,4]{0,2,1:T(4,128)}, u32[]{:S(2)}) copy-start(f32[24,4,4]{0,2,1:T(4,128)} %param.16) | copy-start | bytes 4612
  10.0 7.0 %copy-start.3 = (f32[24,4,4]{0,2,1:T(4,128)S(1)}, f32[24,4,4]{0,2,1:T(4,128)}, u32[]{:S(2)}) copy-start(f32[24,4,4]{0,2,1:T(4,128)} %param.17) | copy-start | bytes 4612
  11.1 24.3 %collective-permute-start = (f32[1,128,16,128]{3,1,2,0:T(8,128)}, f32[1,128,16,128]{3,1,2,0:T(8,128)}, u32[]{:S(2)}, u32[]{:S(2)}) collective-permute-start(f32[1,128,16,128]{3,1,2,0:T(8,128)} %get-tuple-element.262), channel_id=1, source_target_pairs={{0,4},{4,8},{8,12},{12,16},{16,20},{20,24},{24,28},{1,5},{5,9},{9,... | collective-permute-start | bytes 3145736 | tf_op jit(solution)/shard_map/ppermute | solution.py:15
  14.8 24.9 %collective-permute-start.1 = (f32[1,128,16,128]{3,1,2,0:T(8,128)S(1)}, f32[1,128,16,128]{3,1,2,0:T(8,128)}, u32[]{:S(2)}, u32[]{:S(2)}) collective-permute-start(f32[1,128,16,128]{3,1,2,0:T(8,128)S(1)} %get-tuple-element.263), channel_id=1, source_target_pairs={{4,0},{8,4},{12,8},{16,12},{20,16},{24,20},{28,24},{5,1},{9,5},{13... | collective-permute-start | bytes 3145736 | tf_op jit(solution)/shard_map/ppermute | solution.py:17
  17.1 26.5 %copy-start.5 = (s32[24]{0:T(128)S(1)}, s32[24]{0:T(128)}, u32[]{:S(2)}) copy-start(s32[24]{0:T(128)} %param.13) | copy-start | bytes 292
  53.6 1.9 copy-start
  59.9 1.3 copy-start.1
  71.3 1.9 copy-start
  77.6 1.3 copy-start.1
  89.0 1.9 copy-start
  95.3 1.3 copy-start.1
  106.6 1.9 copy-start
  113.0 1.3 copy-start.1
  124.3 1.9 copy-start
  130.6 1.3 copy-start.1
  142.0 1.9 copy-start
  148.3 1.3 copy-start.1
Sparse Core Ops, SparseCore 0:
  155.6 43.4 reduce-scatter.4
where the time goes:
time: 210 us; the launch traced here: 208 us
  waiting for transfers between devices  66.3 us (32%)
  matrix products  59.1 us (28%)
  local copies, waits for them, and re-layouts  51.9 us (25%)
  between operations  13.5 us (6%)
  other arithmetic  11 us (5%)
  starting transfers between devices  5.59 us (3%)
    unnamed x2, waiting for transfers between devices  43.6 us
    gather x12, local copies, waits for them, and re-layouts, per_sector(): source = lax.dynamic_index_in_dim(padded, index, 0, keepdims=False)  28.4 us
    dot_general x6, matrix products, apply_term(): return jnp.einsum('apd,bd->apb', mixed, right_block, precision=highest)  26.2 us
    dot_general x6, matrix products, apply_term(): jnp.dot(left_rows, source.reshape(source.shape[0], -1), precision=highest...  21.4 us
    ppermute x1, waiting for transfers between devices, extended(): lax.ppermute(tail, axis, [(i, (i + 1) % count) for i in range(ends)])  18.4 us
    dot_general x6, matrix products, apply_term(): mixed = jnp.einsum('pq,aqd->apd', site_pair, moved, precision=highest)  11.5 us
    while x30, local copies, waits for them, and re-layouts  10.3 us
    unnamed x14, local copies, waits for them, and re-layouts  7.26 us
  transfers between devices with their start and end apart: 3, of which 3 were waited for; matrix products, arithmetic and copies ran while one was open for 0% of the time, Pallas kernels for 0%

commit v1 on v0

v1 whole, which is shorter than its diff:
```python
import functools

import jax
import jax.numpy as jnp
from jax import lax
from jax.experimental import pallas as pl
from jax.experimental.pallas import tpu as pltpu
from jax.sharding import PartitionSpec as P

VMEM = pl.BlockSpec(memory_space=pltpu.VMEM)
SMEM = pl.BlockSpec(memory_space=pltpu.SMEM)
LIMIT = 40 * 1024 * 1024


def split(x):
    high = x.astype(jnp.bfloat16)
    low = (x - high.astype(jnp.float32)).astype(jnp.bfloat16)
    return high, low


def local_sector(blk, first):
    odd = lax.rem(blk, 2)
    return 1 - odd if first else odd


def partner_of(z):
    return z + 1 - 2 * lax.rem(z, 2)


def apply_kernel(
    own, first, groups, rows, states, bond, site, charge_ref, allowed_ref, one_ref, two_ref, theta_ref, halo_ref, *refs
):
    if own:
        left_ref, right_ref, out_ref, source, moved, mixed = refs
    else:
        env_ref, before_ref, mine_ref, rest_ref, source, moved, mixed, total = refs
    total = out_ref if own else total
    z = lax.axis_index("mpo")
    sector = local_sector(lax.axis_index("blk"), first)
    terms = (left_ref if own else env_ref).shape[0]
    height = groups * rows
    first_term = (z if own else partner_of(z)) * terms

    for slot in range(3):
        for q in range(states):
            if slot < 2:
                block = theta_ref[slot, pl.ds(q, bond, stride=states), :]
            else:
                block = halo_ref[pl.ds(q, bond, stride=states), :]
            high, low = split(block)
            source[slot, 0:bond, q * bond : (q + 1) * bond] = high
            source[slot, bond : 2 * bond, q * bond : (q + 1) * bond] = low

    total[...] = jnp.zeros_like(total) if own else before_ref[...]

    def pair(w, carry):
        term = first_term + w

        @pl.when(allowed_ref[term, sector] != 0)
        def _():
            shifted = sector - charge_ref[term]
            slot = jnp.where((shifted >= 0) & (shifted <= 1), shifted, 2)
            if own:
                parts = []
                for r in range(groups):
                    dest = lax.rem(lax.div(z, 2) + r, groups) * 2 + lax.rem(z, 2)
                    start = pl.multiple_of(dest * rows, rows)
                    parts.append(left_ref[w, sector, pl.ds(start, rows), :])
                left = jnp.concatenate(parts, axis=0) if groups > 1 else parts[0]
                right = right_ref[w, sector]
            else:
                left = env_ref[w, 0:height, :]
                right = env_ref[w, height : height + bond, :]
            stacked = jnp.concatenate(split(left), axis=0)
            rows_in = jnp.concatenate([stacked, stacked], axis=1)
            for s in range(site):
                cut = slice(s * site * bond, (s + 1) * site * bond)
                moved[:, cut] = jnp.dot(rows_in, source[slot, :, cut], preferred_element_type=jnp.float32)
            one = [[one_ref[term, i, j] for j in range(site)] for i in range(site)]
            two = [[two_ref[term, i, j] for j in range(site)] for i in range(site)]
            step = 16
            for start in range(0, height, step):
                half = []
                for s in range(site):
                    cols = []
                    for u in range(site):
                        cut = slice((s * site + u) * bond, (s * site + u + 1) * bond)
                        cols.append(moved[start : start + step, cut] + moved[height + start : height + start + step, cut])
                    half.append([sum(two[v][u] * cols[u] for u in range(site)) for v in range(site)])
                for v in range(site):
                    for t in range(site):
                        value = sum(one[t][s] * half[s][v] for s in range(site))
                        high, low = split(value)
                        at = (t * site + v) * height + start
                        mixed[at : at + step, 0:bond] = high
                        mixed[at : at + step, bond : 2 * bond] = low
            folded = jnp.concatenate(split(right), axis=0)
            weights = jnp.concatenate([folded, folded], axis=1)
            chunk = 256
            for at in range(0, states * height, chunk):
                got = lax.dot_general(
                    mixed[at : at + chunk, :], weights, (((1,), (1,)), ((), ())), preferred_element_type=jnp.float32
                )
                total[at : at + chunk, :] += got[:, :bond] + got[:, bond:]

        return carry

    lax.fori_loop(0, terms, pair, 0)
    if not own:
        for p in range(states):
            mine_ref[p] = total[p * height : p * height + rows, :]
            for r in range(1, groups):
                at = p * height + r * rows
                rest_ref[r - 1, p] = total[at : at + rows, :]


def apply_terms(own, first, groups, rows, scalars, theta, halo, operands):
    states = 16
    bond = theta.shape[-1]
    states = theta.shape[1] // bond
    site = scalars[2].shape[-1]
    height = groups * rows
    flat = jax.ShapeDtypeStruct((states * height, bond), jnp.float32)
    scratch = [
        pltpu.VMEM((3, 2 * bond, states * bond), jnp.bfloat16),
        pltpu.VMEM((2 * height, states * bond), jnp.float32),
        pltpu.VMEM((states * height, 2 * bond), jnp.bfloat16),
    ]
    if own:
        out = flat
    else:
        out = (
            jax.ShapeDtypeStruct((states, rows, bond), jnp.float32),
            jax.ShapeDtypeStruct((groups - 1, states, rows, bond), jnp.float32),
        )
        scratch.append(pltpu.VMEM(flat.shape, jnp.float32))
    pairs = operands[0].shape[0]
    return pl.pallas_call(
        functools.partial(apply_kernel, own, first, groups, rows, states, bond, site),
        out_shape=out,
        in_specs=[SMEM] * 4 + [VMEM] * (2 + len(operands)),
        out_specs=VMEM if own else (VMEM, VMEM),
        scratch_shapes=scratch,
        compiler_params=pltpu.CompilerParams(vmem_limit_bytes=LIMIT),
        cost_estimate=pl.CostEstimate(
            flops=pairs * 8 * states * height * bond * bond, bytes_accessed=4 * 1024 * 1024, transcendentals=0
        ),
        name=("own" if own else "partner") + ("_first" if first else "_second"),
    )(*scalars, theta, halo, *operands)


def finish_kernel(rows, states, bond, dims_ref, first_ref, first_got, second_ref, second_got, out_ref):
    z = lax.axis_index("mpo")
    blk = lax.axis_index("blk")
    for first, mine, got in ((True, first_ref, first_got), (False, second_ref, second_got)):
        sector = local_sector(blk, first)
        row = lax.broadcasted_iota(jnp.int32, (rows, bond), 0) + z * rows
        col = lax.broadcasted_iota(jnp.int32, (rows, bond), 1)
        keep = ((row < dims_ref[sector, 0]) & (col < dims_ref[sector, 1])).astype(jnp.float32)
        for p in range(states):
            value = mine[p]
            for r in range(got.shape[0]):
                value = value + got[r, p]
            out_ref[sector, pl.ds(p, rows, stride=states), :] = value * keep


def body(theta, block_dims, pair_mask, term_charge, left_env, right_env, site_one, site_two):
    sectors, bond, states, _ = theta.shape
    blk, z = lax.axis_index("blk"), lax.axis_index("mpo")
    blk_count, group_count = lax.axis_size("blk"), lax.axis_size("mpo")
    terms = left_env.shape[0]
    rows = bond // group_count
    groups = group_count // 2
    scalars = (term_charge, pair_mask, site_one, site_two)
    across = partner_of(z)
    swap = [(i, i ^ 1) for i in range(group_count)]

    def packed(first):
        sector = local_sector(blk, first)
        left = lax.dynamic_index_in_dim(left_env, sector, 1, keepdims=False)
        right = lax.dynamic_index_in_dim(right_env, sector, 1, keepdims=False)
        parts = []
        for r in range(groups):
            dest = lax.rem(lax.div(z, 2) + r, groups) * 2 + lax.rem(across, 2)
            parts.append(lax.dynamic_slice_in_dim(left, dest * rows, rows, 1))
        return jnp.concatenate(parts + [right], axis=1)

    env_first = lax.ppermute(packed(True), "mpo", swap)
    env_second = lax.ppermute(packed(False), "mpo", swap)

    places = jnp.arange(bond, dtype=jnp.int32)
    left_ok = places[None, :] < block_dims[:, 0:1]
    right_ok = places[None, :] < block_dims[:, 1:2]
    keep = (left_ok[:, :, None, None] & right_ok[:, None, None, :]).astype(jnp.float32)
    masked = theta * keep
    inner = lax.dynamic_index_in_dim(masked, local_sector(blk, True), 0, keepdims=False)
    outer = lax.dynamic_index_in_dim(masked, local_sector(blk, False), 0, keepdims=False)
    pairs = blk_count // 2
    halo_first = lax.ppermute(inner, "blk", [(i, i ^ 1) for i in range(2 * pairs)])
    crossing = [(2 * i + 1, 2 * i + 2) for i in range(pairs - 1)]
    halo_second = lax.ppermute(outer, "blk", crossing + [(b, a) for a, b in crossing])

    flat = masked.reshape(sectors, bond * states, bond)
    results = []
    for first, halo, env in ((True, halo_first, env_first), (False, halo_second, env_second)):
        halo = halo.reshape(bond * states, bond)
        own = apply_terms(True, first, groups, rows, scalars, flat, halo, (left_env, right_env))
        mine, rest = apply_terms(False, first, groups, rows, scalars, flat, halo, (env, own))
        got = []
        for r in range(1, groups):
            route = [(i, ((i // 2 + r) % groups) * 2 + i % 2) for i in range(group_count)]
            got.append(lax.ppermute(rest[r - 1], "mpo", route))
        got = got[0][None] if groups == 2 else jnp.stack(got)
        results += [mine, got]

    out = pl.pallas_call(
        functools.partial(finish_kernel, rows, states, bond),
        out_shape=jax.ShapeDtypeStruct((sectors, rows * states, bond), jnp.float32),
        in_specs=[SMEM] + [VMEM] * 4,
        out_specs=VMEM,
        compiler_params=pltpu.CompilerParams(vmem_limit_bytes=LIMIT),
        name="finish",
    )(block_dims, *results)
    return out.reshape(sectors, rows, states, bond)


def solution(mesh):
    placed = (
        P("blk", None, None, None),
        P("blk", None),
        P(None, "blk"),
        P(),
        P("mpo", "blk", None, None),
        P("mpo", "blk", None, None),
        P(),
        P(),
    )
    return jax.shard_map(
        body, mesh=mesh, in_specs=placed, out_specs=P("blk", "mpo", None, None), check_vma=False
    )
```

time: 210 us -> 65.4 us (0.31)
  matrix products: 59.1 us -> 0 us
  waiting for transfers between devices: 66.3 us -> 18.2 us
  local copies, waits for them, and re-layouts: 51.9 us -> 5.13 us
  Pallas kernels: 0 us -> 28.8 us
  between operations: 13.5 us -> 0.23 us
  other arithmetic: 11 us -> 3.72 us
  starting transfers between devices: 5.59 us -> 8.27 us
    dot_general x18 -> x0, matrix products: 59.1 us -> none  [the longest x6 26.2 us: apply_term(): return jnp.einsum('apd,bd->apb', mixed, right_block, precision=highest)]
    unnamed x2 -> x0, waiting for transfers between devices: 43.6 us -> none
    pallas_call x0 -> x5, Pallas kernels: none -> 28.8 us  [the longest x4 27.2 us: apply_terms(): pl.pallas_call(functools.partial(apply_kernel, own, first, groups, rows,...]
    gather x12 -> x0, local copies, waits for them, and re-layouts: 28.4 us -> none  [per_sector(): source = lax.dynamic_index_in_dim(padded, index, 0, keepdims=False)]
    while x30 -> x0, local copies, waits for them, and re-layouts: 10.3 us -> none
    unnamed x14 -> x19, local copies, waits for them, and re-layouts: 7.26 us -> 1.48 us
    concatenate x7 -> x2, other arithmetic: 7.19 us -> 1.73 us  [packed(): return jnp.concatenate(parts + [right], axis=1)]
    ppermute x2 -> x6, waiting for transfers between devices: 22.6 us -> 18.2 us  [the longest x2 12.7 us: body(): got.append(lax.ppermute(rest[r - 1], 'mpo', route))]
  transfers between devices with their start and end apart: 3 -> 6, of which waited for: 3 -> 2; matrix products, arithmetic and copies ran while one was open for 0% -> 5% of each run, Pallas kernels for 0% -> 42%
where the time goes in v1:
time: 65.4 us; the launch traced here: 64.3 us
  Pallas kernels  28.8 us (44%)
  waiting for transfers between devices  18.2 us (28%)
  starting transfers between devices  8.27 us (13%)
  local copies, waits for them, and re-layouts  5.13 us (8%)
  other arithmetic  3.72 us (6%)
    pallas_call x4, Pallas kernels, apply_terms(): pl.pallas_call(functools.partial(apply_kernel, own, first, groups, rows,...  27.2 us
    ppermute x2, waiting for transfers between devices, body(): got.append(lax.ppermute(rest[r - 1], 'mpo', route))  12.7 us
    ppermute x1, waiting for transfers between devices, body(): env_first = lax.ppermute(packed(True), 'mpo', swap)  5.45 us
    ppermute x2, starting transfers between devices, body(): got.append(lax.ppermute(rest[r - 1], 'mpo', route))  3.13 us
    ppermute x1, starting transfers between devices, body(): lax.ppermute(outer, 'blk', crossing + [(b, a) for a, b in crossing])  3 us
    mul x1, other arithmetic, body(): masked = theta * keep  1.8 us
    concatenate x2, other arithmetic, packed(): return jnp.concatenate(parts + [right], axis=1)  1.73 us
    pallas_call x1, Pallas kernels, body(): pl.pallas_call(functools.partial(finish_kernel, rows, states, bond), out_...  1.59 us
  transfers between devices with their start and end apart: 6, of which 2 were waited for; matrix products, arithmetic and copies ran while one was open for 5% of the time, Pallas kernels for 42%

profile of v1, /device:TPU:3, one launch (start us, length us, event | category | flops | bytes accessed | tf_op | source)
XLA Modules:
  0.0 64.3 jit_solution(12154474234309698171)
XLA Ops:
  0.0 1.0 %slice_reduce_fusion.1 = (s32[2]{0:T(128)S(1)}, s32[2]{0:T(128)S(1)}) fusion(s32[2,2]{1,0:T(2,128)} %dims_ref.1), kind=kLoop, calls=%fused_computation.14 | loop fusion | bytes 32 | tf_op jit(solution)/shard_map/slice | solution.py:192
  1.0 0.1 iota_compare_fusion
  1.0 0.1 and_convert_fusion
  1.2 1.8 %broadcast_multiply_fusion = f32[2,128,16,128]{3,2,1,0:T(8,128)S(1)} fusion(f32[2,128,16,128]{3,2,1,0:T(8,128)} %param.8, f32[2,128,128]{2,1,0:T(8,128)S(1)} %and_convert_fusion), kind=kLoop, calls=%fused_computation.2 | loop fusion | flops 524288 | bytes 4325376 | tf_op jit(solution)/shard_map/mul | solution.py:195
  3.0 0.0 copy-start
  3.0 1.5 %dynamic-slice_bitcast_fusion = (f32[128,16,128]{2,1,0:T(8,128)}, f32[128,16,128]{2,1,0:T(8,128)}) fusion(f32[2,128,16,128]{3,2,1,0:T(8,128)S(1)} %broadcast_multiply_fusion, s32[]{:T(128)S(6)} %select_n.34, s32[]{:T(128)S(6)} %select_n.28), kind=kLoop, calls=%fused_computation | loop fusion | bytes 4194312 | tf_op jit(solution)/shard_map/jit(dynamic_index_in_dim)/squeeze | solution.py:197
  4.5 0.7 %collective-permute-start = (f32[128,16,128]{2,1,0:T(8,128)}, f32[128,16,128]{2,1,0:T(8,128)}, u32[]{:S(2)}, u32[]{:S(2)}) collective-permute-start(f32[128,16,128]{2,1,0:T(8,128)} %get-tuple-element.16), channel_id=1, source_target_pairs={{0,4},{4,0},{8,12},{12,8},{16,20},{20,16},{24,28},{28,24},{1,5},{5... | collective-permute-start | bytes 3145736 | tf_op jit(solution)/shard_map/ppermute | solution.py:199
  5.2 3.0 %collective-permute-start.3 = (f32[128,16,128]{2,1,0:T(8,128)}, f32[128,16,128]{2,1,0:T(8,128)}, u32[]{:S(2)}, u32[]{:S(2)}) collective-permute-start(f32[128,16,128]{2,1,0:T(8,128)} %get-tuple-element.15), channel_id=1, source_target_pairs={{4,8},{12,16},{20,24},{8,4},{16,12},{24,20},{5,9},{13,17},{21,25},... | collective-permute-start | bytes 3145736 | tf_op jit(solution)/shard_map/ppermute | solution.py:201
  8.2 1.1 %dynamic-slice_bitcast_fusion.5 = (f32[6,32,128]{2,1,0:T(8,128)S(1)}, f32[6,32,128]{2,1,0:T(8,128)S(1)}, f32[6,32,128]{2,1,0:T(8,128)S(1)}, f32[6,32,128]{2,1,0:T(8,128)S(1)}) fusion(f32[6,2,128,128]{3,2,1,0:T(8,128)} %refs_0_.3, s32[]{:T(128)S(6)} %select_n.35, s32[]{:T(128)S(6)} %select_n.31, s32[]{:T(128)S(6)} %select_n.29, s32[]{:T(128)S(6)} %select_n.33), kind=kLoop, calls=%fused_computation.9 | loop fusion | bytes 786448 | tf_op jit(solution)/shard_map/dynamic_slice | solution.py:185
  9.4 0.0 copy-start.7
  9.4 0.0 copy-start.4
  9.4 0.1 dynamic-slice_bitcast_fusion.2
  9.5 0.9 %pad_maximum_fusion = f32[6,192,128]{2,1,0:T(8,128)} fusion(f32[6,128,128]{2,1,0:T(8,128)S(1)} %get-tuple-element.22, f32[6,32,128]{2,1,0:T(8,128)S(1)} %get-tuple-element.18, f32[6,32,128]{2,1,0:T(8,128)S(1)} %get-tuple-element.19), kind=kLoop, calls=%fused_computation.3 | loop fusion | flops 294912 | bytes 1179648 | tf_op jit(solution)/shard_map/concatenate | solution.py:186
  10.4 1.3 %collective-permute-start.1 = (f32[6,192,128]{2,1,0:T(8,128)}, f32[6,192,128]{2,1,0:T(8,128)}, u32[]{:S(2)}, u32[]{:S(2)}) collective-permute-start(f32[6,192,128]{2,1,0:T(8,128)} %pad_maximum_fusion), channel_id=1, source_target_pairs={{0,1},{1,0},{2,3},{3,2},{4,5},{5,4},{6,7},{7,6},{8,9},{9,8},{10,11... | collective-permute-start | bytes 1769480 | tf_op jit(solution)/shard_map/ppermute | solution.py:188
  11.7 0.9 %pad_maximum_fusion.1 = f32[6,192,128]{2,1,0:T(8,128)} fusion(f32[6,128,128]{2,1,0:T(8,128)S(1)} %get-tuple-element.21, f32[6,32,128]{2,1,0:T(8,128)S(1)} %get-tuple-element.20, f32[6,32,128]{2,1,0:T(8,128)S(1)} %get-tuple-element.17), kind=kLoop, calls=%fused_computation.4 | loop fusion | flops 294912 | bytes 1179648 | tf_op jit(solution)/shard_map/concatenate | solution.py:186
  12.5 0.1 collective-permute-start.4
  12.7 0.1 copy.12.allowed_ref
  12.8 0.1 copy.13.one_ref
  12.9 0.1 copy.14.two_ref
  13.0 0.0 copy-start.1
  13.0 1.1 %copy-done.1 = f32[6,2,128,128]{3,2,1,0:T(8,128)S(1)} copy-done((f32[6,2,128,128]{3,2,1,0:T(8,128)S(1)}, f32[6,2,128,128]{3,2,1,0:T(8,128)}, u32[]{:S(2)}) %copy-start.1) | copy-done | bytes 786456
  14.1 6.3 %own_first.1.refs_1_ = f32[1024,128]{1,0:T(8,128)S(1)} custom-call(s32[24]{0:T(128)S(1)} %copy-done.4, s32[24,2]{1,0:T(8,128)S(1)} %copy.12.allowed_ref, f32[24,4,4]{2,1,0:T(4,128)S(1)} %copy.13.one_ref, f32[24,4,4]{2,1,0:T(4,128)S(1)} %copy.14.two_ref, f32[2,2048,128]{2,1,0:T(8,128)S(1)} %bitcast.24, f32[2048,128]{1,0:T(8,128)} %bitcast.2.halo_ref, ...), custom_call_target="tpu_custom_call" | custom-call | flops 805306368 | bytes 4194304 | tf_op jit(solution)/shard_map/own_first/pallas_call | solution.py:138
  20.5 0.0 copy-start.2
  20.5 5.5 %collective-permute-done.1.refs_0_ = f32[6,192,128]{2,1,0:T(8,128)} collective-permute-done((f32[6,192,128]{2,1,0:T(8,128)}, f32[6,192,128]{2,1,0:T(8,128)}, u32[]{:S(2)}, u32[]{:S(2)}) %collective-permute-start.1) | collective-permute-done | bytes 589856 | tf_op jit(solution)/shard_map/ppermute | solution.py:188
  25.9 7.6 %partner_first.1 = (f32[16,32,128]{2,1,0:T(8,128)S(1)}, f32[1,16,32,128]{3,2,1,0:T(8,128)S(1)}) custom-call(s32[24]{0:T(128)S(1)} %copy-done.4, s32[24,2]{1,0:T(8,128)S(1)} %copy.12.allowed_ref, f32[24,4,4]{2,1,0:T(4,128)S(1)} %copy.13.one_ref, f32[24,4,4]{2,1,0:T(4,128)S(1)} %copy.14.two_ref, f32[2,2048,128]{2,1,0:T(8,128)S(1)} %bitcast.25, ...), custom_call_target="tpu_custom_call" | custom-call | flops 805306368 | bytes 4194304 | tf_op jit(solution)/shard_map/partner_first/pallas_call | solution.py:138
  33.6 1.8 %collective-permute-start.2 = (f32[16,32,128]{2,1,0:T(8,128)S(1)}, f32[16,32,128]{2,1,0:T(8,128)S(1)}, u32[]{:S(2)}, u32[]{:S(2)}) collective-permute-start(f32[16,32,128]{2,1,0:T(8,128)S(1)} %bitcast.30), channel_id=1, source_target_pairs={{0,2},{1,3},{2,0},{3,1},{4,6},{5,7},{6,4},{7,5},{8,10},{9,11},{10,... | collective-permute-start | bytes 786440 | tf_op jit(solution)/shard_map/ppermute | solution.py:212
  35.4 7.6 %own_second.1.refs_1_ = f32[1024,128]{1,0:T(8,128)S(1)} custom-call(s32[24]{0:T(128)S(1)} %copy-done.4, s32[24,2]{1,0:T(8,128)S(1)} %copy.12.allowed_ref, f32[24,4,4]{2,1,0:T(4,128)S(1)} %copy.13.one_ref, f32[24,4,4]{2,1,0:T(4,128)S(1)} %copy.14.two_ref, f32[2,2048,128]{2,1,0:T(8,128)S(1)} %bitcast.26, f32[2048,128]{1,0:T(8,128)} %bitcast.9.halo_ref, ...), custom_call_target="tpu_custom_call" | custom-call | flops 805306368 | bytes 4194304 | tf_op jit(solution)/shard_map/own_second/pallas_call | solution.py:138
  42.9 0.0 copy-start.3
  43.0 5.7 %partner_second.1 = (f32[16,32,128]{2,1,0:T(8,128)S(1)}, f32[1,16,32,128]{3,2,1,0:T(8,128)S(1)}) custom-call(s32[24]{0:T(128)S(1)} %copy-done.4, s32[24,2]{1,0:T(8,128)S(1)} %copy.12.allowed_ref, f32[24,4,4]{2,1,0:T(4,128)S(1)} %copy.13.one_ref, f32[24,4,4]{2,1,0:T(4,128)S(1)} %copy.14.two_ref, f32[2,2048,128]{2,1,0:T(8,128)S(1)} %bitcast.27, ...), custom_call_target="tpu_custom_call" | custom-call | flops 805306368 | bytes 4194304 | tf_op jit(solution)/shard_map/partner_second/pallas_call | solution.py:138
  48.7 1.3 %collective-permute-start.5 = (f32[16,32,128]{2,1,0:T(8,128)S(1)}, f32[16,32,128]{2,1,0:T(8,128)S(1)}, u32[]{:S(2)}, u32[]{:S(2)}) collective-permute-start(f32[16,32,128]{2,1,0:T(8,128)S(1)} %bitcast.31), channel_id=1, source_target_pairs={{0,2},{1,3},{2,0},{3,1},{4,6},{5,7},{6,4},{7,5},{8,10},{9,11},{10,... | collective-permute-start | bytes 786440 | tf_op jit(solution)/shard_map/ppermute | solution.py:212
  50.0 12.7 %collective-permute-done.5 = f32[16,32,128]{2,1,0:T(8,128)S(1)} collective-permute-done((f32[16,32,128]{2,1,0:T(8,128)S(1)}, f32[16,32,128]{2,1,0:T(8,128)S(1)}, u32[]{:S(2)}, u32[]{:S(2)}) %collective-permute-start.5) | collective-permute-done | bytes 262176 | tf_op jit(solution)/shard_map/ppermute | solution.py:212
  62.7 1.6 %finish.1 = f32[2,512,128]{2,1,0:T(8,128)} custom-call(s32[2,2]{1,0:T(2,128)S(1)} %copy-done.3, f32[16,32,128]{2,1,0:T(8,128)S(1)} %get-tuple-element.9.first_ref, f32[1,16,32,128]{3,2,1,0:T(8,128)S(1)} %bitcast.28, f32[16,32,128]{2,1,0:T(8,128)S(1)} %get-tuple-element.11.second_ref, f32[1,16,32,128]{3,2,1,0:T(8,128)S(1)} %bitcast.29), custom_call_target="tpu_custom_call" | custom-call | tf_op jit(solution)/shard_map/finish/pallas_call | solution.py:216
  (13 shorter events, 0.0 us)
Async XLA Ops:
  3.0 6.4 %copy-start = (f32[6,2,128,128]{3,2,1,0:T(8,128)S(1)}, f32[6,2,128,128]{3,2,1,0:T(8,128)}, u32[]{:S(2)}) copy-start(f32[6,2,128,128]{3,2,1,0:T(8,128)} %refs_1_.3) | copy-start | bytes 2359300
  4.5 8.5 %collective-permute-start = (f32[128,16,128]{2,1,0:T(8,128)}, f32[128,16,128]{2,1,0:T(8,128)}, u32[]{:S(2)}, u32[]{:S(2)}) collective-permute-start(f32[128,16,128]{2,1,0:T(8,128)} %get-tuple-element.16), channel_id=1, source_target_pairs={{0,4},{4,0},{8,12},{12,8},{16,20},{20,16},{24,28},{28,24},{1,5},{5... | collective-permute-start | bytes 3145736 | tf_op jit(solution)/shard_map/ppermute | solution.py:199
  5.2 30.2 %collective-permute-start.3 = (f32[128,16,128]{2,1,0:T(8,128)}, f32[128,16,128]{2,1,0:T(8,128)}, u32[]{:S(2)}, u32[]{:S(2)}) collective-permute-start(f32[128,16,128]{2,1,0:T(8,128)} %get-tuple-element.15), channel_id=1, source_target_pairs={{4,8},{12,16},{20,24},{8,4},{16,12},{24,20},{5,9},{13,17},{21,25},... | collective-permute-start | bytes 3145736 | tf_op jit(solution)/shard_map/ppermute | solution.py:201
  9.4 3.3 %copy-start.7 = (s32[24,2]{0,1:T(2,128)S(1)}, s32[24,2]{0,1:T(2,128)}, u32[]{:S(2)}) copy-start(s32[24,2]{0,1:T(2,128)} %param.10) | copy-start | bytes 580
  9.4 3.4 %copy-start.5 = (f32[24,4,4]{0,2,1:T(4,128)S(1)}, f32[24,4,4]{0,2,1:T(4,128)}, u32[]{:S(2)}) copy-start(f32[24,4,4]{0,2,1:T(4,128)} %param.14) | copy-start | bytes 4612
  9.4 3.5 %copy-start.6 = (f32[24,4,4]{0,2,1:T(4,128)S(1)}, f32[24,4,4]{0,2,1:T(4,128)}, u32[]{:S(2)}) copy-start(f32[24,4,4]{0,2,1:T(4,128)} %param.15) | copy-start | bytes 4612
  9.4 3.6 %copy-start.4 = (s32[24]{0:T(128)S(1)}, s32[24]{0:T(128)}, u32[]{:S(2)}) copy-start(s32[24]{0:T(128)} %charge_ref.7) | copy-start | bytes 292
  10.4 15.6 %collective-permute-start.1 = (f32[6,192,128]{2,1,0:T(8,128)}, f32[6,192,128]{2,1,0:T(8,128)}, u32[]{:S(2)}, u32[]{:S(2)}) collective-permute-start(f32[6,192,128]{2,1,0:T(8,128)} %pad_maximum_fusion), channel_id=1, source_target_pairs={{0,1},{1,0},{2,3},{3,2},{4,5},{5,4},{6,7},{7,6},{8,9},{9,8},{10,11... | collective-permute-start | bytes 1769480 | tf_op jit(solution)/shard_map/ppermute | solution.py:188
  12.5 30.4 %collective-permute-start.4 = (f32[6,192,128]{2,1,0:T(8,128)}, f32[6,192,128]{2,1,0:T(8,128)}, u32[]{:S(2)}, u32[]{:S(2)}) collective-permute-start(f32[6,192,128]{2,1,0:T(8,128)} %pad_maximum_fusion.1), channel_id=1, source_target_pairs={{0,1},{1,0},{2,3},{3,2},{4,5},{5,4},{6,7},{7,6},{8,9},{9,8},{10,11... | collective-permute-start | bytes 1769480 | tf_op jit(solution)/shard_map/ppermute | solution.py:189
  13.0 1.1 %copy-start.1 = (f32[6,2,128,128]{3,2,1,0:T(8,128)S(1)}, f32[6,2,128,128]{3,2,1,0:T(8,128)}, u32[]{:S(2)}) copy-start(f32[6,2,128,128]{3,2,1,0:T(8,128)} %refs_0_.3) | copy-start | bytes 2359300
  20.5 14.9 %copy-start.2 = (f32[6,2,128,128]{3,2,1,0:T(8,128)S(1)}, f32[6,2,128,128]{3,2,1,0:T(8,128)}, u32[]{:S(2)}) copy-start(f32[6,2,128,128]{3,2,1,0:T(8,128)} %refs_0_.3) | copy-start | bytes 2359300
  33.6 16.4 %collective-permute-start.2 = (f32[16,32,128]{2,1,0:T(8,128)S(1)}, f32[16,32,128]{2,1,0:T(8,128)S(1)}, u32[]{:S(2)}, u32[]{:S(2)}) collective-permute-start(f32[16,32,128]{2,1,0:T(8,128)S(1)} %bitcast.30), channel_id=1, source_target_pairs={{0,2},{1,3},{2,0},{3,1},{4,6},{5,7},{6,4},{7,5},{8,10},{9,11},{10,... | collective-permute-start | bytes 786440 | tf_op jit(solution)/shard_map/ppermute | solution.py:212
  42.9 19.8 %copy-start.3 = (s32[2,2]{1,0:T(2,128)S(1)}, s32[2,2]{1,0:T(2,128)}, u32[]{:S(2)}) copy-start(s32[2,2]{1,0:T(2,128)} %dims_ref.1) | copy-start | bytes 52
  48.7 14.0 %collective-permute-start.5 = (f32[16,32,128]{2,1,0:T(8,128)S(1)}, f32[16,32,128]{2,1,0:T(8,128)S(1)}, u32[]{:S(2)}, u32[]{:S(2)}) collective-permute-start(f32[16,32,128]{2,1,0:T(8,128)S(1)} %bitcast.31), channel_id=1, source_target_pairs={{0,2},{1,3},{2,0},{3,1},{4,6},{5,7},{6,4},{7,5},{8,10},{9,11},{10,... | collective-permute-start | bytes 786440 | tf_op jit(solution)/shard_map/ppermute | solution.py:212

commit v2 on v1

v2 whole, which is shorter than its diff:
```python
import functools

import jax
import jax.numpy as jnp
from jax import lax
from jax.experimental import pallas as pl
from jax.experimental.pallas import tpu as pltpu
from jax.sharding import PartitionSpec as P

VMEM = pl.BlockSpec(memory_space=pltpu.VMEM)
ANY = pl.BlockSpec(memory_space=pl.ANY)
LIGHT = pl.CostEstimate(flops=1, bytes_accessed=1, transcendentals=0)
PARAMS = pltpu.CompilerParams(vmem_limit_bytes=24 * 1024 * 1024)


def split(x):
    high = x.astype(jnp.bfloat16)
    low = (x - high.astype(jnp.float32)).astype(jnp.bfloat16)
    return high, low


def weighted(scales, values):
    total = scales[0] * values[0]
    for scale, value in zip(scales[1:], values[1:]):
        total = total + scale * value
    return total


def local_sector(blk, first):
    odd = lax.rem(blk, 2)
    return 1 - odd if first else odd


def partner_of(z):
    return z + 1 - 2 * lax.rem(z, 2)


def row_start(z, parity, r, groups, rows):
    dest = lax.rem(lax.div(z, 2) + r, groups) * 2 + parity
    return pl.multiple_of(dest * rows, rows)


def env_copies(first, own, groups, rows, left_ref, right_ref, env_ref, sem):
    z = lax.axis_index("mpo")
    sector = local_sector(lax.axis_index("blk"), first)
    height, bond = groups * rows, right_ref.shape[-1]
    copies = []
    for r in range(groups):
        start = row_start(z, lax.rem(z if own else partner_of(z), 2), r, groups, rows)
        source = left_ref.at[:, sector, pl.ds(start, rows), :]
        copies.append(pltpu.make_async_copy(source, env_ref.at[:, r * rows : (r + 1) * rows, :], sem.at[r]))
    source = right_ref.at[:, sector]
    copies.append(pltpu.make_async_copy(source, env_ref.at[:, height : height + bond, :], sem.at[groups]))
    return copies


def pack_kernel(first, groups, rows, left_ref, right_ref, env_ref, sem):
    copies = env_copies(first, False, groups, rows, left_ref, right_ref, env_ref, sem)
    for copy in copies:
        copy.start()
    for copy in copies:
        copy.wait()


def mask_kernel(first, states, dims_ref, theta_ref, out_ref, dims, held, sem):
    sector = local_sector(lax.axis_index("blk"), first)
    copies = [
        pltpu.make_async_copy(dims_ref, dims, sem.at[0]),
        pltpu.make_async_copy(theta_ref.at[sector], held, sem.at[1]),
    ]
    for copy in copies:
        copy.start()
    for copy in copies:
        copy.wait()
    step = 256

    def part(i, carry):
        start = pl.multiple_of(i * step, step)
        row = lax.broadcasted_iota(jnp.int32, (step, held.shape[1]), 0) + start
        col = lax.broadcasted_iota(jnp.int32, (step, held.shape[1]), 1)
        keep = (row < dims[sector, 0] * states) & (col < dims[sector, 1])
        out_ref[pl.ds(start, step), :] = jnp.where(keep, held[pl.ds(start, step), :], 0.0)
        return carry

    lax.fori_loop(0, held.shape[0] // step, part, 0)


def apply_kernel(own, first, groups, rows, bond, site, *refs):
    inputs, refs = refs[:4], refs[4:]
    if own:
        inner_ref, outer_ref, halo_ref, left_ref, right_ref, total, source, *refs = refs
        moved, mixed, charge_ref, allowed_ref, one_ref, two_ref, sem, env, env_sem, halo, halo_sem = refs
    else:
        source, env, before_ref, mine_ref, rest_ref, moved, mixed, charge_ref, allowed_ref, one_ref, two_ref, sem = refs
    scalars = (charge_ref, allowed_ref, one_ref, two_ref)
    states = site * site
    z = lax.axis_index("mpo")
    sector = local_sector(lax.axis_index("blk"), first)
    height = groups * rows
    terms = env.shape[0]
    first_term = (z if own else partner_of(z)) * terms
    block = min(rows, 16)
    joined = 16 // block

    small = [pltpu.make_async_copy(a, b, sem.at[i]) for i, (a, b) in enumerate(zip(inputs, scalars))]
    if own:
        fetch_halo = pltpu.make_async_copy(halo_ref, halo, halo_sem)
        large = env_copies(first, True, groups, rows, left_ref, right_ref, env, env_sem)
        fetch_halo.start()
    else:
        large = []
    for copy in small + large:
        copy.start()

    if own:
        total[...] = jnp.zeros_like(total)
        for slot, ref in enumerate((inner_ref, outer_ref, halo)):
            if slot == 2:
                fetch_halo.wait()

            def convert(s, carry, slot=slot, ref=ref):
                for u in range(site):
                    high, low = split(ref[pl.ds(s * site + u, bond, stride=states), :])
                    cut = pl.ds(pl.multiple_of((s * site + u) * bond, bond), bond)
                    source[slot, 0:bond, cut] = high
                    source[slot, bond : 2 * bond, cut] = low
                return carry

            lax.fori_loop(0, site, convert, 0)
    else:
        cut = mine_ref.shape[0]
        mine_ref[...] = before_ref[0:cut, :]
        rest_ref[...] = before_ref[cut:, :]
    for copy in small + large:
        copy.wait()

    def pair(w, carry):
        term = first_term + w

        @pl.when(allowed_ref[sector, term] != 0)
        def _():
            charge = charge_ref[term]
            shifted = sector - charge
            inside = (shifted >= 0) & (shifted <= 1)
            slot = jnp.where(inside, jnp.where(charge == 0, 0 if first else 1, 1 if first else 0), 2)
            stacked = jnp.concatenate(split(env[w, 0:height, :]), axis=0)
            rows_in = jnp.concatenate([stacked, stacked], axis=1)
            for s in range(site):
                cut = slice(s * site * bond, (s + 1) * site * bond)
                moved[:, cut] = jnp.dot(rows_in, source[slot, :, cut], preferred_element_type=jnp.float32)
            one = [[one_ref[i, j, term] for j in range(site)] for i in range(site)]
            two = [[two_ref[i, j, term] for j in range(site)] for i in range(site)]
            folded = jnp.concatenate(split(jnp.transpose(env[w, height : height + bond, :])), axis=1)
            weights = jnp.concatenate([folded, folded], axis=0)
            for start in range(0, height, block):
                half = []
                for s in range(site):
                    cols = []
                    for u in range(site):
                        cut = slice((s * site + u) * bond, (s * site + u + 1) * bond)
                        cols.append(moved[start : start + block, cut] + moved[height + start : height + start + block, cut])
                    half.append([weighted(two[v], cols) for v in range(site)])
                values = [weighted(one[t], [half[s][v] for s in range(site)]) for t in range(site) for v in range(site)]
                base = start * states
                for p in range(0, states, joined):
                    high, low = split(jnp.concatenate(values[p : p + joined], axis=0) if joined > 1 else values[p])
                    at = base + p * block
                    mixed[at : at + joined * block, 0:bond] = high
                    mixed[at : at + joined * block, bond : 2 * bond] = low
                got = jnp.dot(mixed[base : base + block * states, :], weights, preferred_element_type=jnp.float32)
                got = got[:, :bond] + got[:, bond:]
                if own:
                    total[base : base + block * states, :] += got
                elif start < rows:
                    mine_ref[base : base + block * states, :] += got
                else:
                    at = base - rows * states
                    rest_ref[at : at + block * states, :] += got

        return carry

    lax.fori_loop(0, terms, pair, 0)


def apply_terms(own, first, groups, rows, bond, terms, scalars, operands):
    site = scalars[2].shape[0]
    states = site * site
    height = groups * rows
    flat = jax.ShapeDtypeStruct((states * height, bond), jnp.float32)
    scratch = [
        pltpu.VMEM((2 * height, states * bond), jnp.float32),
        pltpu.VMEM((states * height, 2 * bond), jnp.bfloat16),
    ]
    scratch += [pltpu.SMEM(x.shape, x.dtype) for x in scalars]
    scratch += [pltpu.SemaphoreType.DMA((len(scalars),))]
    if own:
        out = (flat, jax.ShapeDtypeStruct((3, 2 * bond, states * bond), jnp.bfloat16))
        scratch += [pltpu.VMEM((terms, height + bond, bond), jnp.float32), pltpu.SemaphoreType.DMA((groups + 1,))]
        scratch += [pltpu.VMEM((states * bond, bond), jnp.float32), pltpu.SemaphoreType.DMA]
        places = [VMEM, VMEM, ANY, ANY, ANY]
    else:
        out = (
            jax.ShapeDtypeStruct((rows * states, bond), jnp.float32),
            jax.ShapeDtypeStruct(((groups - 1) * rows * states, bond), jnp.float32),
        )
        places = [VMEM, VMEM, VMEM]
    return pl.pallas_call(
        functools.partial(apply_kernel, own, first, groups, rows, bond, site),
        out_shape=out,
        in_specs=[ANY] * 4 + places,
        out_specs=(VMEM, VMEM),
        scratch_shapes=scratch,
        compiler_params=PARAMS,
        cost_estimate=LIGHT,
        name=("own" if own else "partner") + ("_first" if first else "_second"),
    )(*scalars, *operands)


def finish_kernel(rows, states, bond, dims_ref, *refs):
    out_ref, dims, sem = refs[-3:]
    parts = refs[:-3]
    count = len(parts) // 2
    copy = pltpu.make_async_copy(dims_ref, dims, sem)
    copy.start()
    copy.wait()
    z = lax.axis_index("mpo")
    blk = lax.axis_index("blk")
    for first, (mine, *got) in ((True, parts[:count]), (False, parts[count:])):
        sector = local_sector(blk, first)
        block = min(rows, 16)
        for start in range(0, rows, block):
            row = lax.broadcasted_iota(jnp.int32, (block, bond), 0) + (z * rows + start)
            col = lax.broadcasted_iota(jnp.int32, (block, bond), 1)
            keep = ((row < dims[sector, 0]) & (col < dims[sector, 1])).astype(jnp.float32)
            for p in range(states):
                at = (start * states) + p * block
                value = mine[at : at + block, :]
                for other in got:
                    value = value + other[at : at + block, :]
                out_ref[sector, pl.ds(start * states + p, block, stride=states), :] = value * keep


def body(theta, block_dims, pair_mask, term_charge, left_env, right_env, site_one, site_two):
    sectors, bond, states, _ = theta.shape
    blk_count, group_count = lax.axis_size("blk"), lax.axis_size("mpo")
    terms = left_env.shape[0]
    rows = bond // group_count
    groups = group_count // 2
    height = groups * rows
    scalars = (term_charge, pair_mask.T, site_one.transpose(1, 2, 0), site_two.transpose(1, 2, 0))
    swap = [(i, i ^ 1) for i in range(group_count)]

    def packed(first, left, right):
        return pl.pallas_call(
            functools.partial(pack_kernel, first, groups, rows),
            out_shape=jax.ShapeDtypeStruct((terms, height + bond, bond), jnp.float32),
            in_specs=[ANY, ANY],
            out_specs=ANY,
            scratch_shapes=[pltpu.SemaphoreType.DMA((groups + 1,))],
            compiler_params=PARAMS,
            cost_estimate=LIGHT,
            name="pack_first" if first else "pack_second",
        )(left, right)

    def masked(first, values):
        return pl.pallas_call(
            functools.partial(mask_kernel, first, states),
            out_shape=jax.ShapeDtypeStruct((bond * states, bond), jnp.float32),
            in_specs=[ANY, ANY],
            out_specs=VMEM,
            scratch_shapes=[
                pltpu.SMEM(block_dims.shape, block_dims.dtype),
                pltpu.VMEM((bond * states, bond), jnp.float32),
                pltpu.SemaphoreType.DMA((2,)),
            ],
            compiler_params=PARAMS,
            cost_estimate=LIGHT,
            name="mask_first" if first else "mask_second",
        )(block_dims, values)

    flat = pltpu.with_memory_space_constraint(theta.reshape(sectors, bond * states, bond), pltpu.HBM)
    left_env = pltpu.with_memory_space_constraint(left_env, pltpu.HBM)
    right_env = pltpu.with_memory_space_constraint(right_env, pltpu.HBM)
    pairs = blk_count // 2
    crossing = [(2 * i + 1, 2 * i + 2) for i in range(pairs - 1)]
    first_packed = packed(True, left_env, right_env)
    first_packed, flat = lax.optimization_barrier((first_packed, flat))
    env_first = lax.ppermute(first_packed, "mpo", swap)
    outer = masked(False, flat)
    outer, flat = lax.optimization_barrier((outer, flat))
    halo_second = lax.ppermute(outer, "blk", crossing + [(b, a) for a, b in crossing])
    inner = masked(True, flat)
    inner, left_tied, right_tied = lax.optimization_barrier((inner, left_env, right_env))
    halo_first = lax.ppermute(inner, "blk", [(i, i ^ 1) for i in range(2 * pairs)])
    second_packed = packed(False, left_tied, right_tied)
    env_second = lax.ppermute(second_packed, "mpo", swap)

    results = []
    for first, halo, env in ((True, halo_first, env_first), (False, halo_second, env_second)):
        if not first:
            results[0], halo = lax.optimization_barrier((results[0], halo))
        before, source = apply_terms(
            True, first, groups, rows, bond, terms, scalars, (inner, outer, halo, left_env, right_env)
        )
        mine, rest = apply_terms(False, first, groups, rows, bond, terms, scalars, (source, env, before))
        results.append(mine)
        for r in range(1, groups):
            route = [(i, ((i // 2 + r) % groups) * 2 + i % 2) for i in range(group_count)]
            cut = rows * states
            part = rest[(r - 1) * cut : r * cut]
            if not first:
                results[r], part = lax.optimization_barrier((results[r], part))
            results.append(lax.ppermute(part, "mpo", route))

    out = pl.pallas_call(
        functools.partial(finish_kernel, rows, states, bond),
        out_shape=jax.ShapeDtypeStruct((sectors, rows * states, bond), jnp.float32),
        in_specs=[ANY] + [VMEM] * len(results),
        out_specs=VMEM,
        scratch_shapes=[pltpu.SMEM(block_dims.shape, block_dims.dtype), pltpu.SemaphoreType.DMA],
        compiler_params=PARAMS,
        name="finish",
    )(block_dims, *results)
    return out.reshape(sectors, rows, states, bond)


def solution(mesh):
    placed = (
        P("blk", None, None, None),
        P("blk", None),
        P(None, "blk"),
        P(),
        P("mpo", "blk", None, None),
        P("mpo", "blk", None, None),
        P(),
        P(),
    )
    return jax.shard_map(
        body, mesh=mesh, in_specs=placed, out_specs=P("blk", "mpo", None, None), check_vma=False
    )
```

time: 65.4 us -> 62.3 us (0.953); the launches traced: 64.3 us -> 62 us
  waiting for transfers between devices: 18.2 us -> 29 us
  Pallas kernels: 28.8 us -> 21.8 us
  local copies, waits for them, and re-layouts: 5.13 us -> 0.7 us
  other arithmetic: 3.72 us -> 0 us
  starting transfers between devices: 8.27 us -> 10.3 us
    pallas_call x4, Pallas kernels: 27.2 us -> 15.1 us  [apply_terms(): pl.pallas_call(functools.partial(apply_kernel, own, first, groups, rows,...]
    ppermute x4, waiting for transfers between devices: 18.2 us -> 25.4 us  [the longest x2 13.5 us: body(): results.append(lax.ppermute(part, 'mpo', route))]
    pallas_call x0 -> x4, Pallas kernels: none -> 5.16 us  [the longest x2 2.91 us: masked(): pl.pallas_call(functools.partial(mask_kernel, first, states), out_shape=j...]
    ppermute x1, waiting for transfers between devices: 0.01 us -> 3.61 us  [body(): lax.ppermute(outer, 'blk', crossing + [(b, a) for a, b in crossing])]
    ppermute x4, starting transfers between devices: 4.6 us -> 6.56 us  [the longest x2 4.96 us: body(): results.append(lax.ppermute(part, 'mpo', route))]
    mul x1 -> x0, other arithmetic: 1.8 us -> none  [body(): masked = theta * keep]
    concatenate x2 -> x0, other arithmetic: 1.73 us -> none  [packed(): return jnp.concatenate(parts + [right], axis=1)]
    squeeze x2 -> x0, local copies, waits for them, and re-layouts: 1.55 us -> none  [the longest x1 1.49 us: body(): lax.dynamic_index_in_dim(masked, local_sector(blk, False), 0, keepdims=Fa...]
  transfers between devices with their start and end apart: 6 -> 6, of which waited for: 2 -> 4; matrix products, arithmetic and copies ran while one was open for 5% -> 0% of each run, Pallas kernels for 42% -> 26%
where the time goes in v2:
time: 62.3 us; the launch traced here: 62 us
  waiting for transfers between devices  29 us (47%)
  Pallas kernels  21.8 us (35%)
  starting transfers between devices  10.3 us (17%)
  local copies, waits for them, and re-layouts  0.7 us (1%)
    pallas_call x4, Pallas kernels, apply_terms(): pl.pallas_call(functools.partial(apply_kernel, own, first, groups, rows,...  15.1 us
    ppermute x2, waiting for transfers between devices, body(): results.append(lax.ppermute(part, 'mpo', route))  13.5 us
    ppermute x1, waiting for transfers between devices, body(): env_first = lax.ppermute(first_packed, 'mpo', swap)  8.19 us
    ppermute x2, starting transfers between devices, body(): results.append(lax.ppermute(part, 'mpo', route))  4.96 us
    ppermute x1, waiting for transfers between devices, body(): env_second = lax.ppermute(second_packed, 'mpo', swap)  3.66 us
    ppermute x1, waiting for transfers between devices, body(): lax.ppermute(outer, 'blk', crossing + [(b, a) for a, b in crossing])  3.61 us
    ppermute x1, starting transfers between devices, body(): lax.ppermute(outer, 'blk', crossing + [(b, a) for a, b in crossing])  3.02 us
    pallas_call x2, Pallas kernels, masked(): pl.pallas_call(functools.partial(mask_kernel, first, states), out_shape=j...  2.91 us
  transfers between devices with their start and end apart: 6, of which 4 were waited for; matrix products, arithmetic and copies ran while one was open for 0% of the time, Pallas kernels for 26%

profile of v2, /device:TPU:3, one launch (start us, length us, event | category | flops | bytes accessed | tf_op | source)
XLA Modules:
  0.0 62.0 jit_solution(16980136790709503014)
XLA Ops:
  0.0 1.1 %pack_first.1 = f32[6,192,128]{2,1,0:T(8,128)S(1)} custom-call(f32[6,2,128,128]{3,2,1,0:T(8,128)} %left_ref.2, f32[6,2,128,128]{3,2,1,0:T(8,128)} %right_ref.2), custom_call_target="tpu_custom_call" | custom-call | flops 1 | bytes 1 | tf_op jit(solution)/shard_map/pack_first/pallas_call | solution.py:254
  1.1 0.0 copy-start.3
  1.1 0.7 %copy-done.3 = s32[2,2]{1,0:T(2,128)S(1)} copy-done((s32[2,2]{1,0:T(2,128)S(1)}, s32[2,2]{1,0:T(2,128)}, u32[]{:S(2)}) %copy-start.3) | copy-done | bytes 40
  1.8 1.4 %mask_second.1.refs_5_ = f32[2048,128]{1,0:T(8,128)S(1)} custom-call(s32[2,2]{1,0:T(2,128)S(1)} %copy-done.3, f32[2,2048,128]{2,1,0:T(8,128)} %bitcast.17), custom_call_target="tpu_custom_call" | custom-call | flops 1 | bytes 1 | tf_op jit(solution)/shard_map/mask_second/pallas_call | solution.py:266
  3.3 0.0 copy-start
  3.3 0.0 copy-start.1
  3.3 0.0 copy-start.2
  3.3 0.0 copy-start.4
  3.3 1.5 %mask_first.1.refs_4_ = f32[2048,128]{1,0:T(8,128)S(1)} custom-call(s32[2,2]{1,0:T(2,128)S(1)} %copy-done.3, f32[2,2048,128]{2,1,0:T(8,128)} %bitcast.18), custom_call_target="tpu_custom_call" | custom-call | flops 1 | bytes 1 | tf_op jit(solution)/shard_map/mask_first/pallas_call | solution.py:266
  4.8 0.7 %collective-permute-start = (f32[2048,128]{1,0:T(8,128)S(1)}, f32[2048,128]{1,0:T(8,128)S(1)}, u32[]{:S(2)}, u32[]{:S(2)}) collective-permute-start(f32[2048,128]{1,0:T(8,128)S(1)} %mask_first.1.refs_4_), channel_id=1, source_target_pairs={{0,4},{4,0},{8,12},{12,8},{16,20},{20,16},{24,28},{28,24},{1,5},{5... | collective-permute-start | bytes 3145736 | tf_op jit(solution)/shard_map/ppermute | solution.py:294
  5.5 3.0 %collective-permute-start.2 = (f32[2048,128]{1,0:T(8,128)S(1)}, f32[2048,128]{1,0:T(8,128)S(1)}, u32[]{:S(2)}, u32[]{:S(2)}) collective-permute-start(f32[2048,128]{1,0:T(8,128)S(1)} %mask_second.1.refs_5_), channel_id=1, source_target_pairs={{4,8},{12,16},{20,24},{8,4},{16,12},{24,20},{5,9},{13,17},{21,25},... | collective-permute-start | bytes 3145736 | tf_op jit(solution)/shard_map/ppermute | solution.py:291
  8.6 1.4 %collective-permute-start.1 = (f32[6,192,128]{2,1,0:T(8,128)S(1)}, f32[6,192,128]{2,1,0:T(8,128)S(1)}, u32[]{:S(2)}, u32[]{:S(2)}) collective-permute-start(f32[6,192,128]{2,1,0:T(8,128)S(1)} %pack_first.1), channel_id=1, source_target_pairs={{0,1},{1,0},{2,3},{3,2},{4,5},{5,4},{6,7},{7,6},{8,9},{9,8},{10,11... | collective-permute-start | bytes 1769480 | tf_op jit(solution)/shard_map/ppermute | solution.py:288
  9.9 1.1 %pack_second.1 = f32[6,192,128]{2,1,0:T(8,128)S(1)} custom-call(f32[6,2,128,128]{3,2,1,0:T(8,128)} %left_ref.2, f32[6,2,128,128]{3,2,1,0:T(8,128)} %right_ref.2), custom_call_target="tpu_custom_call" | custom-call | flops 1 | bytes 1 | tf_op jit(solution)/shard_map/pack_second/pallas_call | solution.py:254
  11.1 0.2 collective-permute-start.4
  11.3 0.0 collective-permute-done.refs_6_
  11.3 0.0 copy-done
  11.3 0.0 copy-done.1
  11.3 0.0 copy-done.2
  11.3 0.0 copy-done.4
  11.3 4.4 %own_first.1 = (f32[1024,128]{1,0:T(8,128)S(1)}, bf16[3,256,2048]{2,1,0:T(8,128)(2,1)S(1)}) custom-call(s32[24]{0:T(128)S(1)} %copy-done.4, s32[2,24]{1,0:T(2,128)S(1)} %bitcast.13, f32[4,4,24]{2,1,0:T(4,128)S(1)} %bitcast.5, f32[4,4,24]{2,1,0:T(4,128)S(1)} %bitcast.9, f32[2048,128]{1,0:T(8,128)S(1)} %mask_first.1.refs_4_, ...), custom_call_target="tpu_custom_call" | custom-call | flops 1 | bytes 1 | tf_op jit(solution)/shard_map/own_first/pallas_call | solution.py:207
  15.7 8.2 %collective-permute-done.1.refs_5_ = f32[6,192,128]{2,1,0:T(8,128)S(1)} collective-permute-done((f32[6,192,128]{2,1,0:T(8,128)S(1)}, f32[6,192,128]{2,1,0:T(8,128)S(1)}, u32[]{:S(2)}, u32[]{:S(2)}) %collective-permute-start.1) | collective-permute-done | bytes 589856 | tf_op jit(solution)/shard_map/ppermute | solution.py:288
  23.9 2.2 %partner_first.1 = (f32[512,128]{1,0:T(8,128)S(1)}, f32[512,128]{1,0:T(8,128)S(1)}) custom-call(s32[24]{0:T(128)S(1)} %copy-done.4, s32[2,24]{1,0:T(2,128)S(1)} %bitcast.14, f32[4,4,24]{2,1,0:T(4,128)S(1)} %bitcast.6, f32[4,4,24]{2,1,0:T(4,128)S(1)} %bitcast.10, bf16[3,256,2048]{2,1,0:T(8,128)(2,1)S(1)} %get-tuple-element.28.refs_4_, ...), custom_call_target="tpu_custom_call" | custom-call | flops 1 | bytes 1 | tf_op jit(solution)/shard_map/partner_first/pallas_call | solution.py:207
  26.1 3.7 %collective-permute-start.3 = (f32[512,128]{1,0:T(8,128)S(1)}, f32[512,128]{1,0:T(8,128)S(1)}, u32[]{:S(2)}, u32[]{:S(2)}) collective-permute-start(f32[512,128]{1,0:T(8,128)S(1)} %get-tuple-element.33), channel_id=1, source_target_pairs={{0,2},{1,3},{2,0},{3,1},{4,6},{5,7},{6,4},{7,5},{8,10},{9,11},{10,... | collective-permute-start | bytes 786440 | tf_op jit(solution)/shard_map/ppermute | solution.py:313
  29.9 3.6 %collective-permute-done.2.refs_6_ = f32[2048,128]{1,0:T(8,128)S(1)} collective-permute-done((f32[2048,128]{1,0:T(8,128)S(1)}, f32[2048,128]{1,0:T(8,128)S(1)}, u32[]{:S(2)}, u32[]{:S(2)}) %collective-permute-start.2) | collective-permute-done | bytes 1048608 | tf_op jit(solution)/shard_map/ppermute | solution.py:291
  33.5 4.3 %own_second.1 = (f32[1024,128]{1,0:T(8,128)S(1)}, bf16[3,256,2048]{2,1,0:T(8,128)(2,1)S(1)}) custom-call(s32[24]{0:T(128)S(1)} %copy-done.4, s32[2,24]{1,0:T(2,128)S(1)} %bitcast.15, f32[4,4,24]{2,1,0:T(4,128)S(1)} %bitcast.7, f32[4,4,24]{2,1,0:T(4,128)S(1)} %bitcast.11, f32[2048,128]{1,0:T(8,128)S(1)} %mask_first.1.refs_4_, ...), custom_call_target="tpu_custom_call" | custom-call | flops 1 | bytes 1 | tf_op jit(solution)/shard_map/own_second/pallas_call | solution.py:207
  37.8 3.7 %collective-permute-done.4.refs_5_ = f32[6,192,128]{2,1,0:T(8,128)S(1)} collective-permute-done((f32[6,192,128]{2,1,0:T(8,128)S(1)}, f32[6,192,128]{2,1,0:T(8,128)S(1)}, u32[]{:S(2)}, u32[]{:S(2)}) %collective-permute-start.4) | collective-permute-done | bytes 589856 | tf_op jit(solution)/shard_map/ppermute | solution.py:296
  41.5 4.2 %partner_second.1 = (f32[512,128]{1,0:T(8,128)S(1)}, f32[512,128]{1,0:T(8,128)S(1)}) custom-call(s32[24]{0:T(128)S(1)} %copy-done.4, s32[2,24]{1,0:T(2,128)S(1)} %bitcast.16, f32[4,4,24]{2,1,0:T(4,128)S(1)} %bitcast.8, f32[4,4,24]{2,1,0:T(4,128)S(1)} %bitcast.12, bf16[3,256,2048]{2,1,0:T(8,128)(2,1)S(1)} %get-tuple-element.35.refs_4_, ...), custom_call_target="tpu_custom_call" | custom-call | flops 1 | bytes 1 | tf_op jit(solution)/shard_map/partner_second/pallas_call | solution.py:207
  45.7 0.0 collective-permute-done.3.refs_1_
  45.7 1.2 %collective-permute-start.5 = (f32[512,128]{1,0:T(8,128)S(1)}, f32[512,128]{1,0:T(8,128)S(1)}, u32[]{:S(2)}, u32[]{:S(2)}) collective-permute-start(f32[512,128]{1,0:T(8,128)S(1)} %get-tuple-element.42), channel_id=1, source_target_pairs={{0,2},{1,3},{2,0},{3,1},{4,6},{5,7},{6,4},{7,5},{8,10},{9,11},{10,... | collective-permute-start | bytes 786440 | tf_op jit(solution)/shard_map/ppermute | solution.py:313
  46.9 13.5 %collective-permute-done.5.refs_3_ = f32[512,128]{1,0:T(8,128)S(1)} collective-permute-done((f32[512,128]{1,0:T(8,128)S(1)}, f32[512,128]{1,0:T(8,128)S(1)}, u32[]{:S(2)}, u32[]{:S(2)}) %collective-permute-start.5) | collective-permute-done | bytes 262176 | tf_op jit(solution)/shard_map/ppermute | solution.py:313
  60.5 1.5 %finish.1 = f32[2,512,128]{2,1,0:T(8,128)} custom-call(s32[2,2]{1,0:T(2,128)S(1)} %copy-done.3, f32[512,128]{1,0:T(8,128)S(1)} %get-tuple-element.32.refs_0_, f32[512,128]{1,0:T(8,128)S(1)} %collective-permute-done.3.refs_1_, f32[512,128]{1,0:T(8,128)S(1)} %get-tuple-element.41.refs_2_, f32[512,128]{1,0:T(8,128)S(1)} %collective-permute-done.5.refs_3_), custom_call_target="tpu_custom_call" | custom-call | tf_op jit(solution)/shard_map/finish/pallas_call | solution.py:315
Async XLA Ops:
  1.1 0.7 %copy-start.3 = (s32[2,2]{1,0:T(2,128)S(1)}, s32[2,2]{1,0:T(2,128)}, u32[]{:S(2)}) copy-start(s32[2,2]{1,0:T(2,128)} %dims_ref.5) | copy-start | bytes 52
  3.3 8.0 %copy-start = (f32[24,4,4]{0,2,1:T(4,128)S(1)}, f32[24,4,4]{0,2,1:T(4,128)}, u32[]{:S(2)}) copy-start(f32[24,4,4]{0,2,1:T(4,128)} %param.14) | copy-start | bytes 4612
  3.3 8.0 %copy-start.1 = (f32[24,4,4]{0,2,1:T(4,128)S(1)}, f32[24,4,4]{0,2,1:T(4,128)}, u32[]{:S(2)}) copy-start(f32[24,4,4]{0,2,1:T(4,128)} %param.15) | copy-start | bytes 4612
  3.3 8.0 %copy-start.2 = (s32[24,2]{0,1:T(2,128)S(1)}, s32[24,2]{0,1:T(2,128)}, u32[]{:S(2)}) copy-start(s32[24,2]{0,1:T(2,128)} %param.10) | copy-start | bytes 580
  3.3 8.0 %copy-start.4 = (s32[24]{0:T(128)S(1)}, s32[24]{0:T(128)}, u32[]{:S(2)}) copy-start(s32[24]{0:T(128)} %refs_0_.7) | copy-start | bytes 292
  4.8 6.5 %collective-permute-start = (f32[2048,128]{1,0:T(8,128)S(1)}, f32[2048,128]{1,0:T(8,128)S(1)}, u32[]{:S(2)}, u32[]{:S(2)}) collective-permute-start(f32[2048,128]{1,0:T(8,128)S(1)} %mask_first.1.refs_4_), channel_id=1, source_target_pairs={{0,4},{4,0},{8,12},{12,8},{16,20},{20,16},{24,28},{28,24},{1,5},{5... | collective-permute-start | bytes 3145736 | tf_op jit(solution)/shard_map/ppermute | solution.py:294
  5.5 27.9 %collective-permute-start.2 = (f32[2048,128]{1,0:T(8,128)S(1)}, f32[2048,128]{1,0:T(8,128)S(1)}, u32[]{:S(2)}, u32[]{:S(2)}) collective-permute-start(f32[2048,128]{1,0:T(8,128)S(1)} %mask_second.1.refs_5_), channel_id=1, source_target_pairs={{4,8},{12,16},{20,24},{8,4},{16,12},{24,20},{5,9},{13,17},{21,25},... | collective-permute-start | bytes 3145736 | tf_op jit(solution)/shard_map/ppermute | solution.py:291
  8.6 15.3 %collective-permute-start.1 = (f32[6,192,128]{2,1,0:T(8,128)S(1)}, f32[6,192,128]{2,1,0:T(8,128)S(1)}, u32[]{:S(2)}, u32[]{:S(2)}) collective-permute-start(f32[6,192,128]{2,1,0:T(8,128)S(1)} %pack_first.1), channel_id=1, source_target_pairs={{0,1},{1,0},{2,3},{3,2},{4,5},{5,4},{6,7},{7,6},{8,9},{9,8},{10,11... | collective-permute-start | bytes 1769480 | tf_op jit(solution)/shard_map/ppermute | solution.py:288
  11.1 30.4 %collective-permute-start.4 = (f32[6,192,128]{2,1,0:T(8,128)S(1)}, f32[6,192,128]{2,1,0:T(8,128)S(1)}, u32[]{:S(2)}, u32[]{:S(2)}) collective-permute-start(f32[6,192,128]{2,1,0:T(8,128)S(1)} %pack_second.1), channel_id=1, source_target_pairs={{0,1},{1,0},{2,3},{3,2},{4,5},{5,4},{6,7},{7,6},{8,9},{9,8},{10,11... | collective-permute-start | bytes 1769480 | tf_op jit(solution)/shard_map/ppermute | solution.py:296
  26.1 19.5 %collective-permute-start.3 = (f32[512,128]{1,0:T(8,128)S(1)}, f32[512,128]{1,0:T(8,128)S(1)}, u32[]{:S(2)}, u32[]{:S(2)}) collective-permute-start(f32[512,128]{1,0:T(8,128)S(1)} %get-tuple-element.33), channel_id=1, source_target_pairs={{0,2},{1,3},{2,0},{3,1},{4,6},{5,7},{6,4},{7,5},{8,10},{9,11},{10,... | collective-permute-start | bytes 786440 | tf_op jit(solution)/shard_map/ppermute | solution.py:313
  45.7 14.8 %collective-permute-start.5 = (f32[512,128]{1,0:T(8,128)S(1)}, f32[512,128]{1,0:T(8,128)S(1)}, u32[]{:S(2)}, u32[]{:S(2)}) collective-permute-start(f32[512,128]{1,0:T(8,128)S(1)} %get-tuple-element.42), channel_id=1, source_target_pairs={{0,2},{1,3},{2,0},{3,1},{4,6},{5,7},{6,4},{7,5},{8,10},{9,11},{10,... | collective-permute-start | bytes 786440 | tf_op jit(solution)/shard_map/ppermute | solution.py:313

commit v3 on v2

v3 whole, which is shorter than its diff:
```python
import functools

import jax
import jax.numpy as jnp
from jax import lax
from jax.experimental import pallas as pl
from jax.experimental.pallas import tpu as pltpu
from jax.sharding import PartitionSpec as P

VMEM = pl.BlockSpec(memory_space=pltpu.VMEM)
ANY = pl.BlockSpec(memory_space=pl.ANY)
PARAMS = pltpu.CompilerParams(vmem_limit_bytes=24 * 1024 * 1024)
LIGHT = pl.CostEstimate(flops=1, bytes_accessed=1, transcendentals=0)
HEAVY = pl.CostEstimate(flops=10**10, bytes_accessed=1, transcendentals=0)


def split(x):
    high = x.astype(jnp.bfloat16)
    low = (x - high.astype(jnp.float32)).astype(jnp.bfloat16)
    return high, low


def weighted(scales, values):
    total = scales[0] * values[0]
    for scale, value in zip(scales[1:], values[1:]):
        total = total + scale * value
    return total


def local_sector(blk, first):
    odd = lax.rem(blk, 2)
    return 1 - odd if first else odd


def partner_of(z):
    return z + 1 - 2 * lax.rem(z, 2)


def row_start(z, parity, r, groups, rows):
    dest = lax.rem(lax.div(z, 2) + r, groups) * 2 + parity
    return pl.multiple_of(dest * rows, rows)


def env_copies(first, own, groups, rows, left_ref, right_ref, env_ref, sem):
    z = lax.axis_index("mpo")
    sector = local_sector(lax.axis_index("blk"), first)
    height, bond = groups * rows, right_ref.shape[-1]
    copies = []
    for r in range(groups):
        start = row_start(z, lax.rem(z if own else partner_of(z), 2), r, groups, rows)
        source = left_ref.at[:, sector, pl.ds(start, rows), :]
        copies.append(pltpu.make_async_copy(source, env_ref.at[:, r * rows : (r + 1) * rows, :], sem.at[r]))
    source = right_ref.at[:, sector]
    copies.append(pltpu.make_async_copy(source, env_ref.at[:, height : height + bond, :], sem.at[groups]))
    return copies


def front_kernel(leading, groups, rows, states, dims_ref, theta_ref, left_ref, right_ref, env_ref, out_ref, *scratch):
    dims, held, sem, env_sem = scratch
    sector = local_sector(lax.axis_index("blk"), leading)
    fetches = [
        pltpu.make_async_copy(dims_ref, dims, sem.at[0]),
        pltpu.make_async_copy(theta_ref.at[sector], held, sem.at[1]),
    ]
    copies = env_copies(leading, False, groups, rows, left_ref, right_ref, env_ref, env_sem)
    for copy in fetches + copies:
        copy.start()
    for copy in fetches:
        copy.wait()
    step = 256

    def part(j, carry):
        start = pl.multiple_of(j * step, step)
        row = lax.broadcasted_iota(jnp.int32, (step, held.shape[1]), 0) + start
        col = lax.broadcasted_iota(jnp.int32, (step, held.shape[1]), 1)
        keep = (row < dims[sector, 0] * states) & (col < dims[sector, 1])
        out_ref[pl.ds(start, step), :] = jnp.where(keep, held[pl.ds(start, step), :], 0.0)
        return carry

    lax.fori_loop(0, held.shape[0] // step, part, 0)
    for copy in copies:
        copy.wait()


def apply_kernel(own, first, span, groups, rows, bond, site, *refs):
    inputs, refs = refs[:4], list(refs[4:])
    take = lambda count: [refs.pop(0) for _ in range(count)]
    late = not own and not first
    if own:
        blocks = take(3 if first else 2)
        left_ref, right_ref, total, source = take(4)
    else:
        source, env, before_ref = take(3)
        if late:
            blocks = take(1)
            left_ref, right_ref = take(2)
        outs = take(2 if first else 1)
    moved, mixed, charge_ref, allowed_ref, one_ref, two_ref, sem = take(7)
    if own or late:
        own_env, env_sem = take(2)
    if late:
        kept, source, kept_sem = source, *take(2)
    states = site * site
    z = lax.axis_index("mpo")
    sector = local_sector(lax.axis_index("blk"), first)
    height = groups * rows
    low, high = span
    block = min(rows, 16)
    joined = 16 // block

    copies = [
        pltpu.make_async_copy(a, b, sem.at[i]) for i, (a, b) in enumerate(zip(inputs, (charge_ref, allowed_ref, one_ref, two_ref)))
    ]
    envs = env_copies(first, True, groups, rows, left_ref, right_ref, own_env, env_sem) if own or late else []
    if late:
        copies.append(pltpu.make_async_copy(kept.at[0:2], source.at[0:2], kept_sem))
    for copy in copies + envs:
        copy.start()

    def convert(slot, ref):
        def part(s, carry):
            for u in range(site):
                high, low = split(ref[pl.ds(s * site + u, bond, stride=states), :])
                cut = pl.ds(pl.multiple_of((s * site + u) * bond, bond), bond)
                source[slot, 0:bond, cut] = high
                source[slot, bond : 2 * bond, cut] = low
            return carry

        lax.fori_loop(0, site, part, 0)

    if own:
        total[...] = jnp.zeros_like(total)
        for slot, ref in enumerate(blocks):
            convert(slot, ref)
    else:
        at = low * states
        for out in outs:
            out[...] = before_ref[at : at + out.shape[0], :]
            at += out.shape[0]
    if late:
        convert(2, blocks[0])
    for copy in copies:
        copy.wait()

    def add_term(env, w, term, slot):
        left = env[w, low:high, :]
        left_rest = left - left.astype(jnp.bfloat16).astype(jnp.float32)
        stacked = jnp.concatenate([left, left_rest], axis=0).astype(jnp.bfloat16)
        rows_in = jnp.concatenate([stacked, stacked], axis=1)
        for s in range(site):
            cut = slice(s * site * bond, (s + 1) * site * bond)
            moved[:, cut] = jnp.dot(rows_in, source[slot, :, cut], preferred_element_type=jnp.float32)
        one = [[one_ref[i, j, term] for j in range(site)] for i in range(site)]
        two = [[two_ref[i, j, term] for j in range(site)] for i in range(site)]
        folded = jnp.concatenate(split(jnp.transpose(env[w, height : height + bond, :])), axis=1)
        weights = jnp.concatenate([folded, folded], axis=0)
        tall = high - low
        for start in range(0, tall, block):
            half = []
            for s in range(site):
                cols = []
                for u in range(site):
                    cut = slice((s * site + u) * bond, (s * site + u + 1) * bond)
                    cols.append(moved[start : start + block, cut] + moved[tall + start : tall + start + block, cut])
                half.append([weighted(two[v], cols) for v in range(site)])
            values = [weighted(one[t], [half[s][v] for s in range(site)]) for t in range(site) for v in range(site)]
            base = start * states
            for p in range(0, states, joined):
                upper, lower = split(jnp.concatenate(values[p : p + joined], axis=0) if joined > 1 else values[p])
                at = base + p * block
                mixed[at : at + joined * block, 0:bond] = upper
                mixed[at : at + joined * block, bond : 2 * bond] = lower
            got = jnp.dot(mixed[base : base + block * states, :], weights, preferred_element_type=jnp.float32)
            got = got[:, :bond] + got[:, bond:]
            if own:
                total[base : base + block * states, :] += got
            elif base < outs[0].shape[0]:
                outs[0][base : base + block * states, :] += got
            else:
                at = base - outs[0].shape[0]
                outs[1][at : at + block * states, :] += got

    def add_terms(env, owner, wanted):
        first_term = owner * env.shape[0]

        def one_term(w, carry):
            term = first_term + w
            charge = charge_ref[term]
            shifted = sector - charge
            inside = (shifted >= 0) & (shifted <= 1)
            slot = jnp.where(inside, jnp.where(charge == 0, 0 if first else 1, 1 if first else 0), 2)

            @pl.when((allowed_ref[sector, term] != 0) & wanted(slot))
            def _():
                add_term(env, w, term, slot)

            return carry

        lax.fori_loop(0, env.shape[0], one_term, 0)

    if not own:
        add_terms(env, partner_of(z), lambda slot: slot >= 0)
    for copy in envs:
        copy.wait()
    if own or late:
        add_terms(own_env, z, lambda slot: slot == 2 if late else slot <= (2 if first else 1))


def apply_terms(own, first, span, groups, rows, bond, terms, scalars, operands):
    site = scalars[2].shape[0]
    states = site * site
    height = groups * rows
    late = not own and not first
    held = jax.ShapeDtypeStruct((3, 2 * bond, states * bond), jnp.bfloat16)
    scratch = [
        pltpu.VMEM((2 * (span[1] - span[0]), states * bond), jnp.float32),
        pltpu.VMEM((states * (span[1] - span[0]), 2 * bond), jnp.bfloat16),
    ]
    scratch += [pltpu.SMEM(x.shape, x.dtype) for x in scalars]
    scratch += [pltpu.SemaphoreType.DMA((len(scalars),))]
    if own or late:
        scratch += [pltpu.VMEM((terms, height + bond, bond), jnp.float32), pltpu.SemaphoreType.DMA((groups + 1,))]
    if late:
        scratch += [pltpu.VMEM(held.shape, held.dtype), pltpu.SemaphoreType.DMA]
    if own:
        out = (jax.ShapeDtypeStruct((states * height, bond), jnp.float32), held)
        places = [VMEM] * (len(operands) - 2) + [ANY, ANY]
    else:
        cuts = [(0, rows), (rows, height)] if first else [span]
        out = tuple(jax.ShapeDtypeStruct(((b - a) * states, bond), jnp.float32) for a, b in cuts)
        places = [ANY, VMEM, VMEM, VMEM, ANY, ANY] if late else [VMEM] * 3
    return pl.pallas_call(
        functools.partial(apply_kernel, own, first, span, groups, rows, bond, site),
        out_shape=out,
        in_specs=[ANY] * 4 + places,
        out_specs=(VMEM,) * len(out),
        scratch_shapes=scratch,
        compiler_params=PARAMS,
        cost_estimate=HEAVY if own and first else LIGHT,
        name=("own" if own else "partner") + ("_first" if first else "_second" if own else f"_second_{span[0]}"),
    )(*scalars, *operands)


def finish_kernel(first, rows, states, bond, *refs):
    if first:
        dims_ref, *parts, out_ref, keep_ref, held, sem, dims = refs
        copy = pltpu.make_async_copy(dims_ref, dims, sem.at[1])
        copy.start()
        copy.wait()
    else:
        _, keep_ref, *parts, out_ref, held, sem = refs
    blk = lax.axis_index("blk")
    sector = local_sector(blk, first)
    block = min(rows, 16)

    def mask(sector, start):
        row = lax.broadcasted_iota(jnp.int32, (block, bond), 0) + (lax.axis_index("mpo") * rows + start)
        col = lax.broadcasted_iota(jnp.int32, (block, bond), 1)
        return ((row < dims[sector, 0]) & (col < dims[sector, 1])).astype(jnp.float32)

    for start in range(0, rows, block):
        if first:
            keep = mask(sector, start)
            keep_ref[start : start + block, :] = mask(local_sector(blk, False), start)
        else:
            keep = keep_ref[start : start + block, :]
        for p in range(states):
            at = start * states + p * block
            value = parts[0][at : at + block, :]
            for other in parts[1:]:
                value = value + other[at : at + block, :]
            held[pl.ds(start * states + p, block, stride=states), :] = value * keep
    copy = pltpu.make_async_copy(held, out_ref.at[sector], sem.at[0])
    copy.start()
    copy.wait()


def body(theta, block_dims, pair_mask, term_charge, left_env, right_env, site_one, site_two):
    sectors, bond, states, _ = theta.shape
    blk_count, group_count = lax.axis_size("blk"), lax.axis_size("mpo")
    terms = left_env.shape[0]
    rows = bond // group_count
    groups = group_count // 2
    height = groups * rows
    scalars = (term_charge, pair_mask.T, site_one.transpose(1, 2, 0), site_two.transpose(1, 2, 0))
    swap = [(i, i ^ 1) for i in range(group_count)]
    flat = pltpu.with_memory_space_constraint(theta.reshape(sectors, bond * states, bond), pltpu.HBM)
    left_env = pltpu.with_memory_space_constraint(left_env, pltpu.HBM)
    right_env = pltpu.with_memory_space_constraint(right_env, pltpu.HBM)
    dims = pltpu.with_memory_space_constraint(block_dims, pltpu.HBM)

    packet = jax.ShapeDtypeStruct((terms, height + bond, bond), jnp.float32)
    sector_block = jax.ShapeDtypeStruct((bond * states, bond), jnp.float32)
    def stage(leading, *args):
        return pl.pallas_call(
            functools.partial(front_kernel, leading, groups, rows, states),
            out_shape=(packet, sector_block),
            in_specs=[ANY] * 4,
            out_specs=(VMEM, VMEM),
            scratch_shapes=[
                pltpu.SMEM(block_dims.shape, block_dims.dtype),
                pltpu.VMEM((bond * states, bond), jnp.float32),
                pltpu.SemaphoreType.DMA((2,)),
                pltpu.SemaphoreType.DMA((groups + 1,)),
            ],
            compiler_params=PARAMS,
            cost_estimate=LIGHT,
            name="front_first" if leading else "front_second",
        )(*args)

    first_packed, inner = stage(True, dims, flat, left_env, right_env)
    first_packed, inner, dims, flat, left_env, right_env = lax.optimization_barrier((first_packed, inner, dims, flat, left_env, right_env))
    second_packed, outer = stage(False, dims, flat, left_env, right_env)
    pairs = blk_count // 2
    crossing = [(2 * i + 1, 2 * i + 2) for i in range(pairs - 1)]
    env_first = lax.ppermute(first_packed, "mpo", swap)
    halo_second = lax.ppermute(outer, "blk", crossing + [(b, a) for a, b in crossing])
    halo_first = lax.ppermute(inner, "blk", [(i, i ^ 1) for i in range(2 * pairs)])
    env_second = lax.ppermute(second_packed, "mpo", swap)

    shared = (groups, rows, bond, terms, scalars)
    whole, mine, rest = (0, height), (0, rows), (rows, height)
    before, source = apply_terms(True, True, whole, *shared, (inner, outer, halo_first, left_env, right_env))
    first_mine, first_rest = apply_terms(False, True, whole, *shared, (source, env_first, before))
    first_mine, outer = lax.optimization_barrier((first_mine, outer))
    before, source = apply_terms(True, False, whole, *shared, (inner, outer, left_env, right_env))
    late = (source, env_second, before, halo_second, left_env, right_env)
    (second_rest,) = apply_terms(False, False, rest, *shared, late)

    first_parts, second_parts = [], []
    cut = rows * states
    for r in range(1, groups):
        route = [(i, ((i // 2 + r) % groups) * 2 + i % 2) for i in range(group_count)]
        arrived = lax.ppermute(first_rest[(r - 1) * cut : r * cut], "mpo", route)
        arrived, leaving = lax.optimization_barrier((arrived, second_rest[(r - 1) * cut : r * cut]))
        first_parts.append(arrived)
        second_parts.append(lax.ppermute(leaving, "mpo", route))
    late = lax.optimization_barrier((*late, second_rest))[:-1]
    (second_mine,) = apply_terms(False, False, mine, *shared, late)

    def finish(first, *operands):
        out = jax.ShapeDtypeStruct((sectors, rows * states, bond), jnp.float32)
        keep = jax.ShapeDtypeStruct((rows, bond), jnp.float32)
        scratch = [pltpu.VMEM((rows * states, bond), jnp.float32), pltpu.SemaphoreType.DMA((2,))]
        if first:
            scratch.append(pltpu.SMEM(block_dims.shape, block_dims.dtype))
        return pl.pallas_call(
            functools.partial(finish_kernel, first, rows, states, bond),
            out_shape=(out, keep) if first else out,
            in_specs=[ANY] + [VMEM] * (len(operands) - 1),
            out_specs=(ANY, VMEM) if first else ANY,
            scratch_shapes=scratch,
            input_output_aliases={} if first else {0: 0},
            compiler_params=PARAMS,
            cost_estimate=LIGHT,
            name="finish_first" if first else "finish_second",
        )(*operands)

    out, keep = finish(True, dims, first_mine, *first_parts)
    out = finish(False, out, keep, second_mine, *second_parts)
    return out.reshape(sectors, rows, states, bond)


def solution(mesh):
    placed = (
        P("blk", None, None, None),
        P("blk", None),
        P(None, "blk"),
        P(),
        P("mpo", "blk", None, None),
        P("mpo", "blk", None, None),
        P(),
        P(),
    )
    return jax.shard_map(
        body, mesh=mesh, in_specs=placed, out_specs=P("blk", "mpo", None, None), check_vma=False
    )
```

time: 62.3 us -> 55.9 us (0.90)
  the two profiles are of different devices: /device:TPU:3 before, /device:TPU:0 now
where the time goes in v3:
time: 55.9 us; the launch traced here: 55.6 us
  Pallas kernels  27.8 us (50%)
  waiting for transfers between devices  19.4 us (35%)
  starting transfers between devices  8.38 us (15%)
    pallas_call x5, Pallas kernels, apply_terms(): pl.pallas_call(functools.partial(apply_kernel, own, first, span, groups,...  22.4 us
    ppermute x1, waiting for transfers between devices, body(): env_second = lax.ppermute(second_packed, 'mpo', swap)  6.97 us
    ppermute x1, waiting for transfers between devices, body(): env_first = lax.ppermute(first_packed, 'mpo', swap)  6.92 us
    ppermute x1, waiting for transfers between devices, body(): second_parts.append(lax.ppermute(leaving, 'mpo', route))  5.47 us
    ppermute x1, starting transfers between devices, body(): arrived = lax.ppermute(first_rest[(r - 1) * cut:r * cut], 'mpo', route)  4.31 us
    pallas_call x2, Pallas kernels, stage(): pl.pallas_call(functools.partial(front_kernel, leading, groups, rows, sta...  3.01 us
    ppermute x1, starting transfers between devices, body(): env_first = lax.ppermute(first_packed, 'mpo', swap)  2.65 us
    pallas_call x2, Pallas kernels, finish(): pl.pallas_call(functools.partial(finish_kernel, first, rows, states, bond...  2.32 us
  transfers between devices with their start and end apart: 6, of which 3 were waited for; matrix products, arithmetic and copies ran while one was open for 0% of the time, Pallas kernels for 46%

profile of v3, /device:TPU:0, one launch (start us, length us, event | category | flops | bytes accessed | tf_op | source)
XLA Modules:
  0.0 55.6 jit_solution(8932231304103045508)
XLA Ops:
  0.0 0.0 copy-start
  0.0 0.0 copy-start.1
  0.0 0.0 copy-start.2
  0.0 0.0 copy-start.3
  0.0 1.5 %front_first.1 = (f32[6,192,128]{2,1,0:T(8,128)S(1)}, f32[2048,128]{1,0:T(8,128)S(1)}) custom-call(s32[2,2]{1,0:T(2,128)} %refs_0_.9, f32[2,2048,128]{2,1,0:T(8,128)} %bitcast.20, f32[6,2,128,128]{3,2,1,0:T(8,128)} %refs_8_.2, f32[6,2,128,128]{3,2,1,0:T(8,128)} %refs_9_.1), custom_call_target="tpu_custom_call" | custom-call | flops 1 | bytes 1 | tf_op jit(solution)/shard_map/front_first/pallas_call | solution.py:295
  1.5 0.5 collective-permute-start
  2.1 2.6 %collective-permute-start.1 = (f32[6,192,128]{2,1,0:T(8,128)S(1)}, f32[6,192,128]{2,1,0:T(8,128)S(1)}, u32[]{:S(2)}, u32[]{:S(2)}) collective-permute-start(f32[6,192,128]{2,1,0:T(8,128)S(1)} %get-tuple-element.42), channel_id=1, source_target_pairs={{0,1},{1,0},{2,3},{3,2},{4,5},{5,4},{6,7},{7,6},{8,9},{9,8},{10,11... | collective-permute-start | bytes 1769480 | tf_op jit(solution)/shard_map/ppermute | solution.py:316
  4.7 1.5 %front_second.1 = (f32[6,192,128]{2,1,0:T(8,128)S(1)}, f32[2048,128]{1,0:T(8,128)S(1)}) custom-call(s32[2,2]{1,0:T(2,128)} %refs_0_.9, f32[2,2048,128]{2,1,0:T(8,128)} %bitcast.21, f32[6,2,128,128]{3,2,1,0:T(8,128)} %refs_8_.2, f32[6,2,128,128]{3,2,1,0:T(8,128)} %refs_9_.1), custom_call_target="tpu_custom_call" | custom-call | flops 1 | bytes 1 | tf_op jit(solution)/shard_map/front_second/pallas_call | solution.py:295
  6.2 0.7 %collective-permute-start.4 = (f32[2048,128]{1,0:T(8,128)S(1)}, f32[2048,128]{1,0:T(8,128)S(1)}, u32[]{:S(2)}, u32[]{:S(2)}) collective-permute-start(f32[2048,128]{1,0:T(8,128)S(1)} %get-tuple-element.47.refs_5_), channel_id=1, source_target_pairs={{4,8},{12,16},{20,24},{8,4},{16,12},{24,20},{5,9},{13,17},{21,25},... | collective-permute-start | bytes 3145736 | tf_op jit(solution)/shard_map/ppermute | solution.py:317
  6.9 0.1 collective-permute-start.3
  7.0 0.0 collective-permute-done.refs_6_
  7.0 0.0 copy-done
  7.0 0.0 copy-done.1
  7.0 0.0 copy-done.2
  7.1 0.0 copy-done.3
  7.1 4.9 %own_first.1 = (f32[1024,128]{1,0:T(8,128)S(1)}, bf16[3,256,2048]{2,1,0:T(8,128)(2,1)S(1)}) custom-call(s32[24]{0:T(128)S(1)} %copy-done.3, s32[2,24]{1,0:T(2,128)S(1)} %bitcast.15, f32[4,4,24]{2,1,0:T(4,128)S(1)} %bitcast.5, f32[4,4,24]{2,1,0:T(4,128)S(1)} %bitcast.10, f32[2048,128]{1,0:T(8,128)S(1)} %get-tuple-element.36.refs_4_, ...), custom_call_target="tpu_custom_call" | custom-call | flops 10000000000 | bytes 1 | tf_op jit(solution)/shard_map/own_first/pallas_call | solution.py:232
  12.0 6.9 %collective-permute-done.1.refs_5_ = f32[6,192,128]{2,1,0:T(8,128)S(1)} collective-permute-done((f32[6,192,128]{2,1,0:T(8,128)S(1)}, f32[6,192,128]{2,1,0:T(8,128)S(1)}, u32[]{:S(2)}, u32[]{:S(2)}) %collective-permute-start.1) | collective-permute-done | bytes 589856 | tf_op jit(solution)/shard_map/ppermute | solution.py:316
  18.9 3.5 %partner_first.1 = (f32[512,128]{1,0:T(8,128)S(1)}, f32[512,128]{1,0:T(8,128)S(1)}) custom-call(s32[24]{0:T(128)S(1)} %copy-done.3, s32[2,24]{1,0:T(2,128)S(1)} %bitcast.16, f32[4,4,24]{2,1,0:T(4,128)S(1)} %bitcast.6, f32[4,4,24]{2,1,0:T(4,128)S(1)} %bitcast.11, bf16[3,256,2048]{2,1,0:T(8,128)(2,1)S(1)} %get-tuple-element.41.refs_4_, ...), custom_call_target="tpu_custom_call" | custom-call | flops 1 | bytes 1 | tf_op jit(solution)/shard_map/partner_first/pallas_call | solution.py:232
  22.4 4.3 %collective-permute-start.2 = (f32[512,128]{1,0:T(8,128)S(1)}, f32[512,128]{1,0:T(8,128)S(1)}, u32[]{:S(2)}, u32[]{:S(2)}) collective-permute-start(f32[512,128]{1,0:T(8,128)S(1)} %get-tuple-element.46), channel_id=1, source_target_pairs={{0,2},{1,3},{2,0},{3,1},{4,6},{5,7},{6,4},{7,5},{8,10},{9,11},{10,... | collective-permute-start | bytes 786440 | tf_op jit(solution)/shard_map/ppermute | solution.py:334
  26.7 3.2 %own_second.1 = (f32[1024,128]{1,0:T(8,128)S(1)}, bf16[3,256,2048]{2,1,0:T(8,128)(2,1)S(1)}) custom-call(s32[24]{0:T(128)S(1)} %copy-done.3, s32[2,24]{1,0:T(2,128)S(1)} %bitcast.17, f32[4,4,24]{2,1,0:T(4,128)S(1)} %bitcast.7, f32[4,4,24]{2,1,0:T(4,128)S(1)} %bitcast.12, f32[2048,128]{1,0:T(8,128)S(1)} %get-tuple-element.36.refs_4_, ...), custom_call_target="tpu_custom_call" | custom-call | flops 1 | bytes 1 | tf_op jit(solution)/shard_map/own_second/pallas_call | solution.py:232
  29.9 7.0 %collective-permute-done.3.refs_5_ = f32[6,192,128]{2,1,0:T(8,128)S(1)} collective-permute-done((f32[6,192,128]{2,1,0:T(8,128)S(1)}, f32[6,192,128]{2,1,0:T(8,128)S(1)}, u32[]{:S(2)}, u32[]{:S(2)}) %collective-permute-start.3) | collective-permute-done | bytes 589856 | tf_op jit(solution)/shard_map/ppermute | solution.py:319
  36.9 0.0 collective-permute-done.4.refs_7_
  36.9 5.4 %partner_second_32.1 = f32[512,128]{1,0:T(8,128)S(1)} custom-call(s32[24]{0:T(128)S(1)} %copy-done.3, s32[2,24]{1,0:T(2,128)S(1)} %bitcast.18, f32[4,4,24]{2,1,0:T(4,128)S(1)} %bitcast.8, f32[4,4,24]{2,1,0:T(4,128)S(1)} %bitcast.13, bf16[3,256,2048]{2,1,0:T(8,128)(2,1)S(1)} %get-tuple-element.54.refs_4_, f32[6,192,128]{2,1,0:T(8,128)S(1)} %collective-permute-done.3.refs_5_, ...), custom_call_target="tpu_custom_call" | custom-call | flops 1 | bytes 1 | tf_op jit(solution)/shard_map/partner_second_32/pallas_call | solution.py:232
  42.3 0.0 collective-permute-done.2.refs_2_
  42.3 0.1 collective-permute-start.5
  42.4 5.4 %partner_second_0.1.refs_2_ = f32[512,128]{1,0:T(8,128)S(1)} custom-call(s32[24]{0:T(128)S(1)} %copy-done.3, s32[2,24]{1,0:T(2,128)S(1)} %bitcast.19, f32[4,4,24]{2,1,0:T(4,128)S(1)} %bitcast.9, f32[4,4,24]{2,1,0:T(4,128)S(1)} %bitcast.14, bf16[3,256,2048]{2,1,0:T(8,128)(2,1)S(1)} %get-tuple-element.54.refs_4_, ...), custom_call_target="tpu_custom_call" | custom-call | flops 1 | bytes 1 | tf_op jit(solution)/shard_map/partner_second_0/pallas_call | solution.py:232
  47.8 1.5 %finish_first.1 = (f32[2,512,128]{2,1,0:T(8,128)}, f32[32,128]{1,0:T(8,128)S(1)}) custom-call(s32[2,2]{1,0:T(2,128)} %refs_0_.9, f32[512,128]{1,0:T(8,128)S(1)} %get-tuple-element.45.refs_1_, f32[512,128]{1,0:T(8,128)S(1)} %collective-permute-done.2.refs_2_), custom_call_target="tpu_custom_call" | custom-call | flops 1 | bytes 1 | tf_op jit(solution)/shard_map/finish_first/pallas_call | solution.py:347
  49.3 5.5 %collective-permute-done.5.refs_3_ = f32[512,128]{1,0:T(8,128)S(1)} collective-permute-done((f32[512,128]{1,0:T(8,128)S(1)}, f32[512,128]{1,0:T(8,128)S(1)}, u32[]{:S(2)}, u32[]{:S(2)}) %collective-permute-start.5) | collective-permute-done | bytes 262176 | tf_op jit(solution)/shard_map/ppermute | solution.py:337
  54.8 0.8 %finish_second.1 = f32[2,512,128]{2,1,0:T(8,128)} custom-call(f32[2,512,128]{2,1,0:T(8,128)} %get-tuple-element.52.refs_0_, f32[32,128]{1,0:T(8,128)S(1)} %get-tuple-element.53.refs_1_, f32[512,128]{1,0:T(8,128)S(1)} %partner_second_0.1.refs_2_, f32[512,128]{1,0:T(8,128)S(1)} %collective-permute-done.5.refs_3_), custom_call_target="tpu_custom_call", output_to_operand_aliasing={{}: (0, {})} | custom-call | flops 1 | bytes 1 | tf_op jit(solution)/shard_map/finish_second/pallas_call | solution.py:347
Async XLA Ops:
  0.0 7.0 %copy-start = (f32[24,4,4]{0,2,1:T(4,128)S(1)}, f32[24,4,4]{0,2,1:T(4,128)}, u32[]{:S(2)}) copy-start(f32[24,4,4]{0,2,1:T(4,128)} %param.14) | copy-start | bytes 4612
  0.0 7.0 %copy-start.1 = (f32[24,4,4]{0,2,1:T(4,128)S(1)}, f32[24,4,4]{0,2,1:T(4,128)}, u32[]{:S(2)}) copy-start(f32[24,4,4]{0,2,1:T(4,128)} %param.15) | copy-start | bytes 4612
  0.0 7.0 %copy-start.2 = (s32[24,2]{0,1:T(2,128)S(1)}, s32[24,2]{0,1:T(2,128)}, u32[]{:S(2)}) copy-start(s32[24,2]{0,1:T(2,128)} %param.10) | copy-start | bytes 580
  0.0 7.0 %copy-start.3 = (s32[24]{0:T(128)S(1)}, s32[24]{0:T(128)}, u32[]{:S(2)}) copy-start(s32[24]{0:T(128)} %refs_0_.10) | copy-start | bytes 292
  1.5 5.5 %collective-permute-start = (f32[2048,128]{1,0:T(8,128)S(1)}, f32[2048,128]{1,0:T(8,128)S(1)}, u32[]{:S(2)}, u32[]{:S(2)}) collective-permute-start(f32[2048,128]{1,0:T(8,128)S(1)} %get-tuple-element.36.refs_4_), channel_id=1, source_target_pairs={{0,4},{4,0},{8,12},{12,8},{16,20},{20,16},{24,28},{28,24},{1,5},{5... | collective-permute-start | bytes 3145736 | tf_op jit(solution)/shard_map/ppermute | solution.py:318
  2.1 16.8 %collective-permute-start.1 = (f32[6,192,128]{2,1,0:T(8,128)S(1)}, f32[6,192,128]{2,1,0:T(8,128)S(1)}, u32[]{:S(2)}, u32[]{:S(2)}) collective-permute-start(f32[6,192,128]{2,1,0:T(8,128)S(1)} %get-tuple-element.42), channel_id=1, source_target_pairs={{0,1},{1,0},{2,3},{3,2},{4,5},{5,4},{6,7},{7,6},{8,9},{9,8},{10,11... | collective-permute-start | bytes 1769480 | tf_op jit(solution)/shard_map/ppermute | solution.py:316
  6.2 30.7 %collective-permute-start.4 = (f32[2048,128]{1,0:T(8,128)S(1)}, f32[2048,128]{1,0:T(8,128)S(1)}, u32[]{:S(2)}, u32[]{:S(2)}) collective-permute-start(f32[2048,128]{1,0:T(8,128)S(1)} %get-tuple-element.47.refs_5_), channel_id=1, source_target_pairs={{4,8},{12,16},{20,24},{8,4},{16,12},{24,20},{5,9},{13,17},{21,25},... | collective-permute-start | bytes 3145736 | tf_op jit(solution)/shard_map/ppermute | solution.py:317
  6.9 30.0 %collective-permute-start.3 = (f32[6,192,128]{2,1,0:T(8,128)S(1)}, f32[6,192,128]{2,1,0:T(8,128)S(1)}, u32[]{:S(2)}, u32[]{:S(2)}) collective-permute-start(f32[6,192,128]{2,1,0:T(8,128)S(1)} %get-tuple-element.49), channel_id=1, source_target_pairs={{0,1},{1,0},{2,3},{3,2},{4,5},{5,4},{6,7},{7,6},{8,9},{9,8},{10,11... | collective-permute-start | bytes 1769480 | tf_op jit(solution)/shard_map/ppermute | solution.py:319
  22.4 19.9 %collective-permute-start.2 = (f32[512,128]{1,0:T(8,128)S(1)}, f32[512,128]{1,0:T(8,128)S(1)}, u32[]{:S(2)}, u32[]{:S(2)}) collective-permute-start(f32[512,128]{1,0:T(8,128)S(1)} %get-tuple-element.46), channel_id=1, source_target_pairs={{0,2},{1,3},{2,0},{3,1},{4,6},{5,7},{6,4},{7,5},{8,10},{9,11},{10,... | collective-permute-start | bytes 786440 | tf_op jit(solution)/shard_map/ppermute | solution.py:334
  42.3 12.5 %collective-permute-start.5 = (f32[512,128]{1,0:T(8,128)S(1)}, f32[512,128]{1,0:T(8,128)S(1)}, u32[]{:S(2)}, u32[]{:S(2)}) collective-permute-start(f32[512,128]{1,0:T(8,128)S(1)} %partner_second_32.1), channel_id=1, source_target_pairs={{0,2},{1,3},{2,0},{3,1},{4,6},{5,7},{6,4},{7,5},{8,10},{9,11},{10,... | collective-permute-start | bytes 786440 | tf_op jit(solution)/shard_map/ppermute | solution.py:337

commit v4 on v3

v4 whole, which is shorter than its diff:
```python
import functools

import jax
import jax.numpy as jnp
from jax import lax
from jax.experimental import pallas as pl
from jax.experimental.pallas import tpu as pltpu
from jax.sharding import PartitionSpec as P

VMEM = pl.BlockSpec(memory_space=pltpu.VMEM)
ANY = pl.BlockSpec(memory_space=pl.ANY)
PARAMS = pltpu.CompilerParams(vmem_limit_bytes=24 * 1024 * 1024)
LIGHT = pl.CostEstimate(flops=1, bytes_accessed=1, transcendentals=0)


def split(x):
    high = x.astype(jnp.bfloat16)
    low = (x - high.astype(jnp.float32)).astype(jnp.bfloat16)
    return high, low


def weighted(scales, values):
    total = scales[0] * values[0]
    for scale, value in zip(scales[1:], values[1:]):
        total = total + scale * value
    return total


def local_sector(blk, first):
    odd = lax.rem(blk, 2)
    return 1 - odd if first else odd


def partner_of(z):
    return z + 1 - 2 * lax.rem(z, 2)


def row_start(z, parity, r, groups, rows):
    dest = lax.rem(lax.div(z, 2) + r, groups) * 2 + parity
    return pl.multiple_of(dest * rows, rows)


def env_copies(first, sides, groups, rows, left_ref, right_ref, env_ref, sem, skip=0):
    z = lax.axis_index("mpo")
    some = slice(skip, skip + env_ref.shape[0])
    sector = local_sector(lax.axis_index("blk"), first)
    bond = right_ref.shape[-1]
    copies, at = [], 0
    for own in sides:
        for r in range(groups):
            start = row_start(z, lax.rem(z if own else partner_of(z), 2), r, groups, rows)
            source = left_ref.at[some, sector, pl.ds(start, rows), :]
            copies.append(pltpu.make_async_copy(source, env_ref.at[:, at : at + rows, :], sem.at[len(copies)]))
            at += rows
    source = right_ref.at[some, sector]
    copies.append(pltpu.make_async_copy(source, env_ref.at[:, at : at + bond, :], sem.at[len(copies)]))
    return copies


def front_kernel(groups, rows, states, dims_ref, theta_ref, left_ref, right_ref, *refs):
    outer_ref, inner_ref, early_ref, last_ref, dims, held, sem, early_sem, last_sem = refs
    blk = lax.axis_index("blk")
    fetches = [pltpu.make_async_copy(dims_ref, dims, sem.at[2])]
    for i, first in enumerate((False, True)):
        fetches.append(pltpu.make_async_copy(theta_ref.at[local_sector(blk, first)], held.at[i], sem.at[i]))
    copies = env_copies(False, (False,), groups, rows, left_ref, right_ref, early_ref, early_sem)
    copies += env_copies(False, (False,), groups, rows, left_ref, right_ref, last_ref, last_sem, early_ref.shape[0])
    for copy in fetches + copies:
        copy.start()
    step = 256
    fetches[0].wait()
    for i, (first, out_ref) in enumerate(((False, outer_ref), (True, inner_ref))):
        sector = local_sector(blk, first)
        fetches[i + 1].wait()

        def part(j, carry, i=i, out_ref=out_ref, sector=sector):
            start = pl.multiple_of(j * step, step)
            row = lax.broadcasted_iota(jnp.int32, (step, held.shape[2]), 0) + start
            col = lax.broadcasted_iota(jnp.int32, (step, held.shape[2]), 1)
            keep = (row < dims[sector, 0] * states) & (col < dims[sector, 1])
            out_ref[pl.ds(start, step), :] = jnp.where(keep, held[i, pl.ds(start, step), :], 0.0)
            return carry

        lax.fori_loop(0, held.shape[1] // step, part, 0)
    for copy in copies:
        copy.wait()


class Call:
    def __init__(self, name, first, cuts, slots=(), own=(), packets=(), added=False, near=None):
        self.name, self.first, self.cuts, self.slots = name, first, cuts, slots
        self.own, self.packets, self.added, self.near = own, packets, added, near
        self.leads = 0 in slots
        self.far = slots == (2,)
        self.kept = not slots


def apply_kernel(call, groups, rows, bond, site, terms, *refs):
    refs = list(refs)
    take = lambda count: [refs.pop(0) for _ in range(count)]
    table_refs = take(4)
    blocks = take(len(call.slots))
    source = take(1)[0] if call.kept else None
    left_ref, right_ref = take(2) if call.own else (None, None)
    packets = take(len(call.packets))
    before_ref = take(1)[0] if call.added else None
    outs = take(len(call.cuts))
    if call.slots:
        source = take(1)[0]
    moved, mixed, charge_ref, allowed_ref, one_ref, two_ref, sem = take(7)
    states = site * site
    z = lax.axis_index("mpo")
    sector = local_sector(lax.axis_index("blk"), call.first)
    low, high = call.cuts[0][0], call.cuts[-1][1]
    tall = high - low
    block = min(rows, 16)
    joined = 16 // block

    tables = (charge_ref, allowed_ref, one_ref, two_ref)
    copies = [pltpu.make_async_copy(a, b, sem.at[i]) for i, (a, b) in enumerate(zip(table_refs, tables))]
    sides = [(packet, partner_of(z) * terms + skip) for packet, skip in zip(packets, call.packets)]
    if call.own:
        env, env_sem = take(2)
        copies += env_copies(call.first, call.own, groups, rows, left_ref, right_ref, env, env_sem)
        sides.append((env, z * terms))
    for copy in copies:
        copy.start()

    for i, ref in enumerate(blocks):

        def part(s, carry, i=i, ref=ref):
            for u in range(site):
                upper, lower = split(ref[pl.ds(s * site + u, bond, stride=states), :])
                cut = pl.ds(pl.multiple_of((s * site + u) * bond, bond), bond)
                source[i, 0:bond, cut] = upper
                source[i, bond : 2 * bond, cut] = lower
            return carry

        lax.fori_loop(0, site, part, 0)

    at = low * states
    for out in outs:
        out[...] = before_ref[at : at + out.shape[0], :] if call.added else jnp.zeros_like(out)
        at += out.shape[0]
    for copy in copies:
        copy.wait()

    def add_term(env, w, term, slot):
        left = env[w, low:high, :]
        left_rest = left - left.astype(jnp.bfloat16).astype(jnp.float32)
        stacked = jnp.concatenate([left, left_rest], axis=0).astype(jnp.bfloat16)
        rows_in = jnp.concatenate([stacked, stacked], axis=1)
        for s in range(site):
            cut = slice(s * site * bond, (s + 1) * site * bond)
            moved[:, cut] = jnp.dot(rows_in, source[slot, :, cut], preferred_element_type=jnp.float32)
        one = [[one_ref[i, j, term] for j in range(site)] for i in range(site)]
        two = [[two_ref[i, j, term] for j in range(site)] for i in range(site)]
        right = env[w, env.shape[1] - bond :, :]
        folded = jnp.concatenate(split(jnp.transpose(right)), axis=1)
        weights = jnp.concatenate([folded, folded], axis=0)
        for start in range(0, tall, block):
            half = []
            for s in range(site):
                cols = []
                for u in range(site):
                    cut = slice((s * site + u) * bond, (s * site + u + 1) * bond)
                    cols.append(moved[start : start + block, cut] + moved[tall + start : tall + start + block, cut])
                half.append([weighted(two[v], cols) for v in range(site)])
            values = [weighted(one[t], [half[s][v] for s in range(site)]) for t in range(site) for v in range(site)]
            base, size = start * states, block * states
            for p in range(0, states, joined):
                upper, lower = split(jnp.concatenate(values[p : p + joined], axis=0) if joined > 1 else values[p])
                here = base + p * block
                mixed[here : here + joined * block, 0:bond] = upper
                mixed[here : here + joined * block, bond : 2 * bond] = lower
            got = jnp.dot(mixed[base : base + size, :], weights, preferred_element_type=jnp.float32)
            got = got[:, :bond] + got[:, bond:]
            for (first_row, last_row), out in zip(call.cuts, outs):
                if first_row <= low + start < last_row:
                    at = (low + start - first_row) * states
                    out[at : at + size, :] += got

    for env, first_term in sides:

        def one_term(w, carry, env=env, first_term=first_term):
            term = first_term + w
            charge = charge_ref[term]
            shifted = sector - charge
            inside = (shifted >= 0) & (shifted <= 1)
            wanted = allowed_ref[sector, term] != 0
            if call.near is not None:
                wanted = wanted & (inside if call.near else jnp.logical_not(inside))
            if call.far:
                slot = 0
            else:
                slot = jnp.where(inside, jnp.where(charge == 0, 0 if call.first else 1, 1 if call.first else 0), 2)

            @pl.when(wanted)
            def _():
                add_term(env, w, term, slot)

            return carry

        lax.fori_loop(0, env.shape[0], one_term, 0)


def apply_terms(call, sizes, tables, operands):
    groups, rows, bond, site, terms = sizes
    states = site * site
    height = groups * rows
    tall = call.cuts[-1][1] - call.cuts[0][0]
    scratch = [
        pltpu.VMEM((2 * tall, states * bond), jnp.float32),
        pltpu.VMEM((states * tall, 2 * bond), jnp.bfloat16),
    ]
    scratch += [pltpu.SMEM(x.shape, x.dtype) for x in tables]
    scratch.append(pltpu.SemaphoreType.DMA((len(tables),)))
    places = [ANY] * 4 + [VMEM] * (len(call.slots) + call.kept)
    if call.own:
        places += [ANY, ANY]
        count = len(call.own)
        scratch.append(pltpu.VMEM((terms, count * height + bond, bond), jnp.float32))
        scratch.append(pltpu.SemaphoreType.DMA((count * groups + 1,)))
    places += [VMEM] * (len(call.packets) + call.added)
    out = [jax.ShapeDtypeStruct(((b - a) * states, bond), jnp.float32) for a, b in call.cuts]
    shape = (len(call.slots), 2 * bond, states * bond)
    if call.leads:
        out.append(jax.ShapeDtypeStruct(shape, jnp.bfloat16))
    elif call.slots:
        scratch.insert(0, pltpu.VMEM(shape, jnp.bfloat16))
    return pl.pallas_call(
        functools.partial(apply_kernel, call, *sizes),
        out_shape=tuple(out),
        in_specs=places,
        out_specs=(VMEM,) * len(out),
        scratch_shapes=scratch,
        compiler_params=PARAMS,
        cost_estimate=LIGHT,
        name=call.name,
    )(*tables, *operands)


def join_kernel(mine_ref, got_ref, out_ref):
    out_ref[...] = mine_ref[...] + got_ref[...]


def finish_kernel(first, rows, states, bond, *refs):
    if first:
        dims_ref, *parts, out_ref, keep_ref, held, sem, dims = refs
        copy = pltpu.make_async_copy(dims_ref, dims, sem.at[1])
        copy.start()
        copy.wait()
    else:
        _, keep_ref, *parts, out_ref, held, sem = refs
    blk = lax.axis_index("blk")
    sector = local_sector(blk, first)
    block = min(rows, 16)

    def mask(sector, start):
        row = lax.broadcasted_iota(jnp.int32, (block, bond), 0) + (lax.axis_index("mpo") * rows + start)
        col = lax.broadcasted_iota(jnp.int32, (block, bond), 1)
        return ((row < dims[sector, 0]) & (col < dims[sector, 1])).astype(jnp.float32)

    for start in range(0, rows, block):
        if first:
            keep = mask(sector, start)
            keep_ref[start : start + block, :] = mask(local_sector(blk, False), start)
        else:
            keep = keep_ref[start : start + block, :]
        for p in range(states):
            at = start * states + p * block
            value = parts[0][at : at + block, :]
            for other in parts[1:]:
                value = value + other[at : at + block, :]
            held[pl.ds(start * states + p, block, stride=states), :] = value * keep
    copy = pltpu.make_async_copy(held, out_ref.at[sector], sem.at[0])
    copy.start()
    copy.wait()


def body(theta, block_dims, pair_mask, term_charge, left_env, right_env, site_one, site_two):
    sectors, bond, states, _ = theta.shape
    blk_count, group_count = lax.axis_size("blk"), lax.axis_size("mpo")
    terms = left_env.shape[0]
    rows = bond // group_count
    groups = group_count // 2
    height = groups * rows
    swap = [(i, i ^ 1) for i in range(group_count)]
    flat = pltpu.with_memory_space_constraint(theta.reshape(sectors, bond * states, bond), pltpu.HBM)
    left_env = pltpu.with_memory_space_constraint(left_env, pltpu.HBM)
    right_env = pltpu.with_memory_space_constraint(right_env, pltpu.HBM)
    dims = pltpu.with_memory_space_constraint(block_dims, pltpu.HBM)

    sector_block = jax.ShapeDtypeStruct((bond * states, bond), jnp.float32)
    last = max(terms // 3, 1)
    early = terms - last
    packets = [jax.ShapeDtypeStruct((count, height + bond, bond), jnp.float32) for count in (early, last)]

    outer, inner, early_packed, last_packed = pl.pallas_call(
        functools.partial(front_kernel, groups, rows, states),
        out_shape=(sector_block, sector_block, *packets),
        in_specs=[ANY] * 4,
        out_specs=(VMEM,) * 4,
        scratch_shapes=[
            pltpu.SMEM(block_dims.shape, block_dims.dtype),
            pltpu.VMEM((2, bond * states, bond), jnp.float32),
            pltpu.SemaphoreType.DMA((3,)),
            pltpu.SemaphoreType.DMA((groups + 1,)),
            pltpu.SemaphoreType.DMA((groups + 1,)),
        ],
        compiler_params=PARAMS,
        cost_estimate=LIGHT,
        name="front",
    )(dims, flat, left_env, right_env)
    tables = (term_charge, pair_mask.T, site_one.transpose(1, 2, 0), site_two.transpose(1, 2, 0))
    pairs = blk_count // 2
    crossing = [(2 * i + 1, 2 * i + 2) for i in range(pairs - 1)]
    halo_second = lax.ppermute(outer, "blk", crossing + [(b, a) for a, b in crossing])
    halo_first = lax.ppermute(inner, "blk", [(i, i ^ 1) for i in range(2 * pairs)])
    early_env = lax.ppermute(early_packed, "mpo", swap)

    sizes = (groups, rows, bond, site_one.shape[-1], terms)
    every, mine, rest = [(0, height)], [(0, rows)], [(rows, height)]
    theirs = [(height, height + rows), (height + rows, 2 * height)]
    envs = (left_env, right_env)

    call = Call("first_own", True, mine + rest + theirs, slots=(0, 1, 2), own=(True, False))
    operands = (inner, outer, halo_first, *envs)
    first_mine, first_rest, mine_away, rest_away, source = apply_terms(call, sizes, tables, operands)
    rest_away, last_packed = lax.optimization_barrier((rest_away, last_packed))
    rest_got = lax.ppermute(rest_away, "mpo", swap)
    last_env = lax.ppermute(last_packed, "mpo", swap)
    call = Call("second_near", False, every, own=(True,), packets=(0,), near=True)
    (before,) = apply_terms(call, sizes, tables, (source, *envs, early_env))
    rest_got, before = lax.optimization_barrier((rest_got, before))
    first_rest = pl.pallas_call(
        join_kernel,
        out_shape=jax.ShapeDtypeStruct(first_rest.shape, first_rest.dtype),
        in_specs=[VMEM] * 2,
        out_specs=VMEM,
        compiler_params=PARAMS,
        cost_estimate=LIGHT,
        name="join",
    )(first_rest, rest_got)
    first_rest, before = lax.optimization_barrier((first_rest, before))
    call = Call("second_last", False, every, packets=(early,), added=True, near=True)
    (before,) = apply_terms(call, sizes, tables, (source, last_env, before))
    before, mine_away = lax.optimization_barrier((before, mine_away))
    mine_got = lax.ppermute(mine_away, "mpo", swap)
    operands = (halo_second, *envs, early_env, last_env, before)
    far = dict(slots=(2,), own=(True,), packets=(0, early), added=True, near=False)
    call = Call("second_rest", False, rest, **far)
    (second_rest,) = apply_terms(call, sizes, tables, operands)

    first_parts, second_parts = [mine_got], []
    cut = rows * states
    for r in range(1, groups):
        route = [(i, ((i // 2 + r) % groups) * 2 + i % 2) for i in range(group_count)]
        first_parts.append(lax.ppermute(first_rest[(r - 1) * cut : r * cut], "mpo", route))
        second_parts.append(lax.ppermute(second_rest[(r - 1) * cut : r * cut], "mpo", route))

    def finish(first, *operands):
        out = jax.ShapeDtypeStruct((sectors, rows * states, bond), jnp.float32)
        keep = jax.ShapeDtypeStruct((rows, bond), jnp.float32)
        scratch = [pltpu.VMEM((rows * states, bond), jnp.float32), pltpu.SemaphoreType.DMA((2,))]
        if first:
            scratch.append(pltpu.SMEM(block_dims.shape, block_dims.dtype))
        return pl.pallas_call(
            functools.partial(finish_kernel, first, rows, states, bond),
            out_shape=(out, keep) if first else out,
            in_specs=[ANY] + [VMEM] * (len(operands) - 1),
            out_specs=(ANY, VMEM) if first else ANY,
            scratch_shapes=scratch,
            input_output_aliases={} if first else {0: 0},
            compiler_params=PARAMS,
            cost_estimate=LIGHT,
            name="finish_first" if first else "finish_second",
        )(*operands)

    first_parts[1], *operands = lax.optimization_barrier((first_parts[1], *operands))
    call = Call("second_mine", False, mine, **far)
    (second_mine,) = apply_terms(call, sizes, tables, operands)
    second_mine, first_mine = lax.optimization_barrier((second_mine, first_mine))
    out, keep = finish(True, dims, first_mine, *first_parts)
    out = finish(False, out, keep, second_mine, *second_parts)
    return out.reshape(sectors, rows, states, bond)


def solution(mesh):
    placed = (
        P("blk", None, None, None),
        P("blk", None),
        P(None, "blk"),
        P(),
        P("mpo", "blk", None, None),
        P("mpo", "blk", None, None),
        P(),
        P(),
    )
    return jax.shard_map(
        body, mesh=mesh, in_specs=placed, out_specs=P("blk", "mpo", None, None), check_vma=False
    )
```

time: 55.9 us -> 50.7 us (0.907)
  the two profiles are of different devices: /device:TPU:0 before, /device:TPU:4 now
where the time goes in v4:
time: 50.7 us; the launch traced here: 50.2 us
  Pallas kernels  22.8 us (45%)
  starting transfers between devices  13.7 us (27%)
  waiting for transfers between devices  13.6 us (27%)
    pallas_call x5, Pallas kernels, apply_terms(): pl.pallas_call(functools.partial(apply_kernel, call, *sizes), out_shape=t...  18.6 us
    ppermute x1, waiting for transfers between devices, body(): lax.ppermute(second_rest[(r - 1) * cut:r * cut], 'mpo', route)  6.33 us
    ppermute x1, waiting for transfers between devices, body(): lax.ppermute(first_rest[(r - 1) * cut:r * cut], 'mpo', route)  4.55 us
    ppermute x1, starting transfers between devices, body(): lax.ppermute(outer, 'blk', crossing + [(b, a) for a, b in crossing])  3.43 us
    ppermute x1, starting transfers between devices, body(): mine_got = lax.ppermute(mine_away, 'mpo', swap)  2.54 us
    pallas_call x2, Pallas kernels, finish(): pl.pallas_call(functools.partial(finish_kernel, first, rows, states, bond...  2.32 us
    ppermute x1, starting transfers between devices, body(): lax.ppermute(second_rest[(r - 1) * cut:r * cut], 'mpo', route)  2.27 us
    ppermute x1, starting transfers between devices, body(): last_env = lax.ppermute(last_packed, 'mpo', swap)  2.01 us
  transfers between devices with their start and end apart: 8, of which 5 were waited for; matrix products, arithmetic and copies ran while one was open for 0% of the time, Pallas kernels for 40%

profile of v4, /device:TPU:4, one launch (start us, length us, event | category | flops | bytes accessed | tf_op | source)
XLA Modules:
  0.0 50.2 jit_solution(6261028694304588658)
XLA Ops:
  0.0 0.0 copy-start.2
  0.0 0.0 copy-start
  0.0 0.0 copy-start.1
  0.0 0.0 copy-start.3
  0.0 1.9 %front.1 = (f32[2048,128]{1,0:T(8,128)S(1)}, f32[2048,128]{1,0:T(8,128)S(1)}, f32[4,192,128]{2,1,0:T(8,128)S(1)}, f32[2,192,128]{2,1,0:T(8,128)S(1)}) custom-call(s32[2,2]{1,0:T(2,128)} %refs_0_.10, f32[2,2048,128]{2,1,0:T(8,128)} %bitcast.20, f32[6,2,128,128]{3,2,1,0:T(8,128)} %refs_5_.4, f32[6,2,128,128]{3,2,1,0:T(8,128)} %refs_6_.4), custom_call_target="tpu_custom_call" | custom-call | flops 1 | bytes 1 | tf_op jit(solution)/shard_map/front/pallas_call | solution.py:299
  1.9 0.1 collective-permute-start
  2.0 3.4 %collective-permute-start.4 = (f32[2048,128]{1,0:T(8,128)S(1)}, f32[2048,128]{1,0:T(8,128)S(1)}, u32[]{:S(2)}, u32[]{:S(2)}) collective-permute-start(f32[2048,128]{1,0:T(8,128)S(1)} %get-tuple-element.34.refs_5_), channel_id=1, source_target_pairs={{4,8},{12,16},{20,24},{8,4},{16,12},{24,20},{5,9},{13,17},{21,25},... | collective-permute-start | bytes 3145736 | tf_op jit(solution)/shard_map/ppermute | solution.py:318
  5.5 1.6 %collective-permute-start.2 = (f32[4,192,128]{2,1,0:T(8,128)S(1)}, f32[4,192,128]{2,1,0:T(8,128)S(1)}, u32[]{:S(2)}, u32[]{:S(2)}) collective-permute-start(f32[4,192,128]{2,1,0:T(8,128)S(1)} %get-tuple-element.40), channel_id=1, source_target_pairs={{0,1},{1,0},{2,3},{3,2},{4,5},{5,4},{6,7},{7,6},{8,9},{9,8},{10,11... | collective-permute-start | bytes 1179656 | tf_op jit(solution)/shard_map/ppermute | solution.py:320
  7.1 0.0 collective-permute-done.refs_6_
  7.1 0.0 copy-done.2
  7.1 0.0 copy-done
  7.1 0.0 copy-done.1
  7.1 0.0 copy-done.3
  7.1 5.9 %first_own.1 = (f32[512,128]{1,0:T(8,128)S(1)}, f32[512,128]{1,0:T(8,128)S(1)}, f32[512,128]{1,0:T(8,128)S(1)}, f32[512,128]{1,0:T(8,128)S(1)}, bf16[3,256,2048]{2,1,0:T(8,128)(2,1)S(1)}) custom-call(s32[24]{0:T(128)S(1)} %copy-done.3, s32[2,24]{1,0:T(2,128)S(1)} %bitcast.15, f32[4,4,24]{2,1,0:T(4,128)S(1)} %bitcast.5, f32[4,4,24]{2,1,0:T(4,128)S(1)} %bitcast.10, ...), custom_call_target="tpu_custom_call" | custom-call | flops 1 | bytes 1 | tf_op jit(solution)/shard_map/first_own/pallas_call | solution.py:231
  13.1 0.1 collective-permute-start.1
  13.2 2.0 %collective-permute-start.5 = (f32[2,192,128]{2,1,0:T(8,128)S(1)}, f32[2,192,128]{2,1,0:T(8,128)S(1)}, u32[]{:S(2)}, u32[]{:S(2)}) collective-permute-start(f32[2,192,128]{2,1,0:T(8,128)S(1)} %get-tuple-element.44), channel_id=1, source_target_pairs={{0,1},{1,0},{2,3},{3,2},{4,5},{5,4},{6,7},{7,6},{8,9},{9,8},{10,11... | collective-permute-start | bytes 589832 | tf_op jit(solution)/shard_map/ppermute | solution.py:332
  15.2 1.5 %collective-permute-done.2.refs_7_ = f32[4,192,128]{2,1,0:T(8,128)S(1)} collective-permute-done((f32[4,192,128]{2,1,0:T(8,128)S(1)}, f32[4,192,128]{2,1,0:T(8,128)S(1)}, u32[]{:S(2)}, u32[]{:S(2)}) %collective-permute-start.2) | collective-permute-done | bytes 393248 | tf_op jit(solution)/shard_map/ppermute | solution.py:320
  16.6 6.7 %second_near.1.refs_6_ = f32[1024,128]{1,0:T(8,128)S(1)} custom-call(s32[24]{0:T(128)S(1)} %copy-done.3, s32[2,24]{1,0:T(2,128)S(1)} %bitcast.16, f32[4,4,24]{2,1,0:T(4,128)S(1)} %bitcast.6, f32[4,4,24]{2,1,0:T(4,128)S(1)} %bitcast.11, bf16[3,256,2048]{2,1,0:T(8,128)(2,1)S(1)} %get-tuple-element.39.refs_4_, f32[6,2,128,128]{3,2,1,0:T(8,128)} %refs_5_.4, ...), custom_call_target="tpu_custom_call" | custom-call | flops 1 | bytes 1 | tf_op jit(solution)/shard_map/second_near/pallas_call | solution.py:231
  23.3 0.0 collective-permute-done.1.got_ref
  23.4 1.6 %collective-permute-start.3 = (f32[512,128]{1,0:T(8,128)S(1)}, f32[512,128]{1,0:T(8,128)S(1)}, u32[]{:S(2)}, u32[]{:S(2)}) collective-permute-start(f32[512,128]{1,0:T(8,128)S(1)} %join.1), channel_id=1, source_target_pairs={{0,2},{1,3},{2,0},{3,1},{4,6},{5,7},{6,4},{7,5},{8,10},{9,11},{10,... | collective-permute-start | bytes 786440 | tf_op jit(solution)/shard_map/ppermute | solution.py:359
  25.0 0.8 %collective-permute-done.5.refs_5_.refs_8_ = f32[2,192,128]{2,1,0:T(8,128)S(1)} collective-permute-done((f32[2,192,128]{2,1,0:T(8,128)S(1)}, f32[2,192,128]{2,1,0:T(8,128)S(1)}, u32[]{:S(2)}, u32[]{:S(2)}) %collective-permute-start.5) | collective-permute-done | bytes 196640 | tf_op jit(solution)/shard_map/ppermute | solution.py:332
  25.8 2.2 %second_last.1.refs_9_ = f32[1024,128]{1,0:T(8,128)S(1)} custom-call(s32[24]{0:T(128)S(1)} %copy-done.3, s32[2,24]{1,0:T(2,128)S(1)} %bitcast.17, f32[4,4,24]{2,1,0:T(4,128)S(1)} %bitcast.7, f32[4,4,24]{2,1,0:T(4,128)S(1)} %bitcast.12, bf16[3,256,2048]{2,1,0:T(8,128)(2,1)S(1)} %get-tuple-element.39.refs_4_, ...), custom_call_target="tpu_custom_call" | custom-call | flops 1 | bytes 1 | tf_op jit(solution)/shard_map/second_last/pallas_call | solution.py:231
  28.0 2.5 %collective-permute-start.6 = (f32[512,128]{1,0:T(8,128)S(1)}, f32[512,128]{1,0:T(8,128)S(1)}, u32[]{:S(2)}, u32[]{:S(2)}) collective-permute-start(f32[512,128]{1,0:T(8,128)S(1)} %get-tuple-element.56), channel_id=1, source_target_pairs={{0,1},{1,0},{2,3},{3,2},{4,5},{5,4},{6,7},{7,6},{8,9},{9,8},{10,11... | collective-permute-start | bytes 786440 | tf_op jit(solution)/shard_map/ppermute | solution.py:349
  30.5 0.0 collective-permute-done.4.refs_4_
  30.5 1.9 %second_rest.1 = f32[512,128]{1,0:T(8,128)S(1)} custom-call(s32[24]{0:T(128)S(1)} %copy-done.3, s32[2,24]{1,0:T(2,128)S(1)} %bitcast.18, f32[4,4,24]{2,1,0:T(4,128)S(1)} %bitcast.8, f32[4,4,24]{2,1,0:T(4,128)S(1)} %bitcast.13, f32[2048,128]{1,0:T(8,128)S(1)} %collective-permute-done.4.refs_4_, f32[6,2,128,128]{3,2,1,0:T(8,128)} %refs_5_.4, ...), custom_call_target="tpu_custom_call" | custom-call | flops 1 | bytes 1 | tf_op jit(solution)/shard_map/second_rest/pallas_call | solution.py:231
  32.4 2.3 %collective-permute-start.7 = (f32[512,128]{1,0:T(8,128)S(1)}, f32[512,128]{1,0:T(8,128)S(1)}, u32[]{:S(2)}, u32[]{:S(2)}) collective-permute-start(f32[512,128]{1,0:T(8,128)S(1)} %second_rest.1), channel_id=1, source_target_pairs={{0,2},{1,3},{2,0},{3,1},{4,6},{5,7},{6,4},{7,5},{8,10},{9,11},{10,... | collective-permute-start | bytes 786440 | tf_op jit(solution)/shard_map/ppermute | solution.py:360
  34.7 4.5 %collective-permute-done.3.refs_3_ = f32[512,128]{1,0:T(8,128)S(1)} collective-permute-done((f32[512,128]{1,0:T(8,128)S(1)}, f32[512,128]{1,0:T(8,128)S(1)}, u32[]{:S(2)}, u32[]{:S(2)}) %collective-permute-start.3) | collective-permute-done | bytes 262176 | tf_op jit(solution)/shard_map/ppermute | solution.py:359
  39.2 1.9 %second_mine.1.refs_2_ = f32[512,128]{1,0:T(8,128)S(1)} custom-call(s32[24]{0:T(128)S(1)} %copy-done.3, s32[2,24]{1,0:T(2,128)S(1)} %bitcast.19, f32[4,4,24]{2,1,0:T(4,128)S(1)} %bitcast.9, f32[4,4,24]{2,1,0:T(4,128)S(1)} %bitcast.14, f32[2048,128]{1,0:T(8,128)S(1)} %collective-permute-done.4.refs_4_, f32[6,2,128,128]{3,2,1,0:T(8,128)} %refs_5_.4, ...), custom_call_target="tpu_custom_call" | custom-call | flops 1 | bytes 1 | tf_op jit(solution)/shard_map/second_mine/pallas_call | solution.py:231
  41.1 0.5 collective-permute-done.6.refs_2_
  41.6 1.5 %finish_first.1 = (f32[2,512,128]{2,1,0:T(8,128)}, f32[32,128]{1,0:T(8,128)S(1)}) custom-call(s32[2,2]{1,0:T(2,128)} %refs_0_.10, f32[512,128]{1,0:T(8,128)S(1)} %get-tuple-element.55.refs_1_, f32[512,128]{1,0:T(8,128)S(1)} %collective-permute-done.6.refs_2_, f32[512,128]{1,0:T(8,128)S(1)} %collective-permute-done.3.refs_3_), custom_call_target="tpu_custom_call" | custom-call | flops 1 | bytes 1 | tf_op jit(solution)/shard_map/finish_first/pallas_call | solution.py:368
  43.1 6.3 %collective-permute-done.7.refs_3_ = f32[512,128]{1,0:T(8,128)S(1)} collective-permute-done((f32[512,128]{1,0:T(8,128)S(1)}, f32[512,128]{1,0:T(8,128)S(1)}, u32[]{:S(2)}, u32[]{:S(2)}) %collective-permute-start.7) | collective-permute-done | bytes 262176 | tf_op jit(solution)/shard_map/ppermute | solution.py:360
  49.4 0.8 %finish_second.1 = f32[2,512,128]{2,1,0:T(8,128)} custom-call(f32[2,512,128]{2,1,0:T(8,128)} %get-tuple-element.58.refs_0_, f32[32,128]{1,0:T(8,128)S(1)} %get-tuple-element.59.refs_1_, f32[512,128]{1,0:T(8,128)S(1)} %second_mine.1.refs_2_, f32[512,128]{1,0:T(8,128)S(1)} %collective-permute-done.7.refs_3_), custom_call_target="tpu_custom_call", output_to_operand_aliasing={{}: (0, {})} | custom-call | flops 1 | bytes 1 | tf_op jit(solution)/shard_map/finish_second/pallas_call | solution.py:368
  (1 shorter events, 0.0 us)
Async XLA Ops:
  0.0 7.1 %copy-start.2 = (s32[24,2]{0,1:T(2,128)S(1)}, s32[24,2]{0,1:T(2,128)}, u32[]{:S(2)}) copy-start(s32[24,2]{0,1:T(2,128)} %param.10) | copy-start | bytes 580
  0.0 7.1 %copy-start = (f32[24,4,4]{0,2,1:T(4,128)S(1)}, f32[24,4,4]{0,2,1:T(4,128)}, u32[]{:S(2)}) copy-start(f32[24,4,4]{0,2,1:T(4,128)} %param.14) | copy-start | bytes 4612
  0.0 7.1 %copy-start.1 = (f32[24,4,4]{0,2,1:T(4,128)S(1)}, f32[24,4,4]{0,2,1:T(4,128)}, u32[]{:S(2)}) copy-start(f32[24,4,4]{0,2,1:T(4,128)} %param.15) | copy-start | bytes 4612
  0.0 7.1 %copy-start.3 = (s32[24]{0:T(128)S(1)}, s32[24]{0:T(128)}, u32[]{:S(2)}) copy-start(s32[24]{0:T(128)} %refs_0_.11) | copy-start | bytes 292
  1.9 5.2 %collective-permute-start = (f32[2048,128]{1,0:T(8,128)S(1)}, f32[2048,128]{1,0:T(8,128)S(1)}, u32[]{:S(2)}, u32[]{:S(2)}) collective-permute-start(f32[2048,128]{1,0:T(8,128)S(1)} %get-tuple-element.33.refs_4_), channel_id=1, source_target_pairs={{0,4},{4,0},{8,12},{12,8},{16,20},{20,16},{24,28},{28,24},{1,5},{5... | collective-permute-start | bytes 3145736 | tf_op jit(solution)/shard_map/ppermute | solution.py:319
  2.0 28.5 %collective-permute-start.4 = (f32[2048,128]{1,0:T(8,128)S(1)}, f32[2048,128]{1,0:T(8,128)S(1)}, u32[]{:S(2)}, u32[]{:S(2)}) collective-permute-start(f32[2048,128]{1,0:T(8,128)S(1)} %get-tuple-element.34.refs_5_), channel_id=1, source_target_pairs={{4,8},{12,16},{20,24},{8,4},{16,12},{24,20},{5,9},{13,17},{21,25},... | collective-permute-start | bytes 3145736 | tf_op jit(solution)/shard_map/ppermute | solution.py:318
  5.5 11.2 %collective-permute-start.2 = (f32[4,192,128]{2,1,0:T(8,128)S(1)}, f32[4,192,128]{2,1,0:T(8,128)S(1)}, u32[]{:S(2)}, u32[]{:S(2)}) collective-permute-start(f32[4,192,128]{2,1,0:T(8,128)S(1)} %get-tuple-element.40), channel_id=1, source_target_pairs={{0,1},{1,0},{2,3},{3,2},{4,5},{5,4},{6,7},{7,6},{8,9},{9,8},{10,11... | collective-permute-start | bytes 1179656 | tf_op jit(solution)/shard_map/ppermute | solution.py:320
  13.1 10.2 %collective-permute-start.1 = (f32[512,128]{1,0:T(8,128)S(1)}, f32[512,128]{1,0:T(8,128)S(1)}, u32[]{:S(2)}, u32[]{:S(2)}) collective-permute-start(f32[512,128]{1,0:T(8,128)S(1)} %get-tuple-element.38), channel_id=1, source_target_pairs={{0,1},{1,0},{2,3},{3,2},{4,5},{5,4},{6,7},{7,6},{8,9},{9,8},{10,11... | collective-permute-start | bytes 786440 | tf_op jit(solution)/shard_map/ppermute | solution.py:331
  13.2 12.6 %collective-permute-start.5 = (f32[2,192,128]{2,1,0:T(8,128)S(1)}, f32[2,192,128]{2,1,0:T(8,128)S(1)}, u32[]{:S(2)}, u32[]{:S(2)}) collective-permute-start(f32[2,192,128]{2,1,0:T(8,128)S(1)} %get-tuple-element.44), channel_id=1, source_target_pairs={{0,1},{1,0},{2,3},{3,2},{4,5},{5,4},{6,7},{7,6},{8,9},{9,8},{10,11... | collective-permute-start | bytes 589832 | tf_op jit(solution)/shard_map/ppermute | solution.py:332
  23.4 15.9 %collective-permute-start.3 = (f32[512,128]{1,0:T(8,128)S(1)}, f32[512,128]{1,0:T(8,128)S(1)}, u32[]{:S(2)}, u32[]{:S(2)}) collective-permute-start(f32[512,128]{1,0:T(8,128)S(1)} %join.1), channel_id=1, source_target_pairs={{0,2},{1,3},{2,0},{3,1},{4,6},{5,7},{6,4},{7,5},{8,10},{9,11},{10,... | collective-permute-start | bytes 786440 | tf_op jit(solution)/shard_map/ppermute | solution.py:359
  28.0 13.6 %collective-permute-start.6 = (f32[512,128]{1,0:T(8,128)S(1)}, f32[512,128]{1,0:T(8,128)S(1)}, u32[]{:S(2)}, u32[]{:S(2)}) collective-permute-start(f32[512,128]{1,0:T(8,128)S(1)} %get-tuple-element.56), channel_id=1, source_target_pairs={{0,1},{1,0},{2,3},{3,2},{4,5},{5,4},{6,7},{7,6},{8,9},{9,8},{10,11... | collective-permute-start | bytes 786440 | tf_op jit(solution)/shard_map/ppermute | solution.py:349
  32.4 17.0 %collective-permute-start.7 = (f32[512,128]{1,0:T(8,128)S(1)}, f32[512,128]{1,0:T(8,128)S(1)}, u32[]{:S(2)}, u32[]{:S(2)}) collective-permute-start(f32[512,128]{1,0:T(8,128)S(1)} %second_rest.1), channel_id=1, source_target_pairs={{0,2},{1,3},{2,0},{3,1},{4,6},{5,7},{6,4},{7,5},{8,10},{9,11},{10,... | collective-permute-start | bytes 786440 | tf_op jit(solution)/shard_map/ppermute | solution.py:360

commit v5 on v4

--- a/solution.py
+++ b/solution.py
@@ -129,14 +129,14 @@
     for i, ref in enumerate(blocks):
 
         def part(s, carry, i=i, ref=ref):
-            for u in range(site):
-                upper, lower = split(ref[pl.ds(s * site + u, bond, stride=states), :])
-                cut = pl.ds(pl.multiple_of((s * site + u) * bond, bond), bond)
-                source[i, 0:bond, cut] = upper
-                source[i, bond : 2 * bond, cut] = lower
+            for u in range(0, site, 2):
+                pieces = [split(ref[pl.ds(s * site + u + k, bond, stride=states), :]) for k in range(2)]
+                cut = pl.ds(pl.multiple_of((s * site + u) * bond, bond), 2 * bond)
+                source[i, 0:bond, cut] = jnp.concatenate([pieces[0][0], pieces[1][0]], axis=1)
+                source[i, bond : 2 * bond, cut] = jnp.concatenate([pieces[0][1], pieces[1][1]], axis=1)
             return carry
 
-        lax.fori_loop(0, site, part, 0)
+        lax.fori_loop(0, site, part, 0, unroll=2)
 
     at = low * states
     for out in outs:

time: 50.7 us -> 50.1 us (0.988)
  the two profiles are of different devices: /device:TPU:4 before, /device:TPU:3 now
where the time goes in v5:
time: 50.1 us; the launch traced here: 49.3 us
  Pallas kernels  23.5 us (47%)
  starting transfers between devices  14.2 us (28%)
  waiting for transfers between devices  11.5 us (23%)
    pallas_call x5, Pallas kernels, apply_terms(): pl.pallas_call(functools.partial(apply_kernel, call, *sizes), out_shape=t...  19.2 us
    ppermute x1, waiting for transfers between devices, body(): lax.ppermute(second_rest[(r - 1) * cut:r * cut], 'mpo', route)  4.42 us
    ppermute x1, starting transfers between devices, body(): mine_got = lax.ppermute(mine_away, 'mpo', swap)  3.35 us
    ppermute x1, starting transfers between devices, body(): lax.ppermute(outer, 'blk', crossing + [(b, a) for a, b in crossing])  3.02 us
    ppermute x1, starting transfers between devices, body(): lax.ppermute(first_rest[(r - 1) * cut:r * cut], 'mpo', route)  2.45 us
    pallas_call x2, Pallas kernels, finish(): pl.pallas_call(functools.partial(finish_kernel, first, rows, states, bond...  2.32 us
    ppermute x1, waiting for transfers between devices, body(): mine_got = lax.ppermute(mine_away, 'mpo', swap)  1.95 us
    pallas_call x1, Pallas kernels, body(): pl.pallas_call(functools.partial(front_kernel, groups, rows, states), out...  1.91 us
  transfers between devices with their start and end apart: 8, of which 7 were waited for; matrix products, arithmetic and copies ran while one was open for 0% of the time, Pallas kernels for 42%

profile of v5, /device:TPU:3, one launch (start us, length us, event | category | flops | bytes accessed | tf_op | source)
XLA Modules:
  0.0 49.3 jit_solution(2599666444991792135)
XLA Ops:
  0.0 0.0 copy-start.2
  0.0 0.0 copy-start
  0.0 0.0 copy-start.1
  0.0 0.0 copy-start.3
  0.0 1.9 %front.1 = (f32[2048,128]{1,0:T(8,128)S(1)}, f32[2048,128]{1,0:T(8,128)S(1)}, f32[4,192,128]{2,1,0:T(8,128)S(1)}, f32[2,192,128]{2,1,0:T(8,128)S(1)}) custom-call(s32[2,2]{1,0:T(2,128)} %refs_0_.10, f32[2,2048,128]{2,1,0:T(8,128)} %bitcast.20, f32[6,2,128,128]{3,2,1,0:T(8,128)} %refs_5_.4, f32[6,2,128,128]{3,2,1,0:T(8,128)} %refs_6_.4), custom_call_target="tpu_custom_call" | custom-call | flops 1 | bytes 1 | tf_op jit(solution)/shard_map/front/pallas_call | solution.py:299
  1.9 0.7 %collective-permute-start = (f32[2048,128]{1,0:T(8,128)S(1)}, f32[2048,128]{1,0:T(8,128)S(1)}, u32[]{:S(2)}, u32[]{:S(2)}) collective-permute-start(f32[2048,128]{1,0:T(8,128)S(1)} %get-tuple-element.33.refs_4_), channel_id=1, source_target_pairs={{0,4},{4,0},{8,12},{12,8},{16,20},{20,16},{24,28},{28,24},{1,5},{5... | collective-permute-start | bytes 3145736 | tf_op jit(solution)/shard_map/ppermute | solution.py:319
  2.7 3.0 %collective-permute-start.4 = (f32[2048,128]{1,0:T(8,128)S(1)}, f32[2048,128]{1,0:T(8,128)S(1)}, u32[]{:S(2)}, u32[]{:S(2)}) collective-permute-start(f32[2048,128]{1,0:T(8,128)S(1)} %get-tuple-element.34.refs_5_), channel_id=1, source_target_pairs={{4,8},{12,16},{20,24},{8,4},{16,12},{24,20},{5,9},{13,17},{21,25},... | collective-permute-start | bytes 3145736 | tf_op jit(solution)/shard_map/ppermute | solution.py:318
  5.7 1.4 %collective-permute-start.2 = (f32[4,192,128]{2,1,0:T(8,128)S(1)}, f32[4,192,128]{2,1,0:T(8,128)S(1)}, u32[]{:S(2)}, u32[]{:S(2)}) collective-permute-start(f32[4,192,128]{2,1,0:T(8,128)S(1)} %get-tuple-element.40), channel_id=1, source_target_pairs={{0,1},{1,0},{2,3},{3,2},{4,5},{5,4},{6,7},{7,6},{8,9},{9,8},{10,11... | collective-permute-start | bytes 1179656 | tf_op jit(solution)/shard_map/ppermute | solution.py:320
  7.1 0.0 collective-permute-done.refs_6_
  7.1 0.0 copy-done.2
  7.1 0.0 copy-done
  7.1 0.0 copy-done.1
  7.1 0.0 copy-done.3
  7.1 6.6 %first_own.1 = (f32[512,128]{1,0:T(8,128)S(1)}, f32[512,128]{1,0:T(8,128)S(1)}, f32[512,128]{1,0:T(8,128)S(1)}, f32[512,128]{1,0:T(8,128)S(1)}, bf16[3,256,2048]{2,1,0:T(8,128)(2,1)S(1)}) custom-call(s32[24]{0:T(128)S(1)} %copy-done.3, s32[2,24]{1,0:T(2,128)S(1)} %bitcast.15, f32[4,4,24]{2,1,0:T(4,128)S(1)} %bitcast.5, f32[4,4,24]{2,1,0:T(4,128)S(1)} %bitcast.10, ...), custom_call_target="tpu_custom_call" | custom-call | flops 1 | bytes 1 | tf_op jit(solution)/shard_map/first_own/pallas_call | solution.py:231
  13.7 1.3 %collective-permute-start.1 = (f32[512,128]{1,0:T(8,128)S(1)}, f32[512,128]{1,0:T(8,128)S(1)}, u32[]{:S(2)}, u32[]{:S(2)}) collective-permute-start(f32[512,128]{1,0:T(8,128)S(1)} %get-tuple-element.38), channel_id=1, source_target_pairs={{0,1},{1,0},{2,3},{3,2},{4,5},{5,4},{6,7},{7,6},{8,9},{9,8},{10,11... | collective-permute-start | bytes 786440 | tf_op jit(solution)/shard_map/ppermute | solution.py:331
  14.9 0.3 collective-permute-start.5
  15.2 1.6 %collective-permute-done.2.refs_7_ = f32[4,192,128]{2,1,0:T(8,128)S(1)} collective-permute-done((f32[4,192,128]{2,1,0:T(8,128)S(1)}, f32[4,192,128]{2,1,0:T(8,128)S(1)}, u32[]{:S(2)}, u32[]{:S(2)}) %collective-permute-start.2) | collective-permute-done | bytes 393248 | tf_op jit(solution)/shard_map/ppermute | solution.py:320
  16.8 4.7 %second_near.1.refs_6_ = f32[1024,128]{1,0:T(8,128)S(1)} custom-call(s32[24]{0:T(128)S(1)} %copy-done.3, s32[2,24]{1,0:T(2,128)S(1)} %bitcast.16, f32[4,4,24]{2,1,0:T(4,128)S(1)} %bitcast.6, f32[4,4,24]{2,1,0:T(4,128)S(1)} %bitcast.11, bf16[3,256,2048]{2,1,0:T(8,128)(2,1)S(1)} %get-tuple-element.39.refs_4_, f32[6,2,128,128]{3,2,1,0:T(8,128)} %refs_5_.4, ...), custom_call_target="tpu_custom_call" | custom-call | flops 1 | bytes 1 | tf_op jit(solution)/shard_map/second_near/pallas_call | solution.py:231
  21.5 0.9 %collective-permute-done.1.got_ref = f32[512,128]{1,0:T(8,128)S(1)} collective-permute-done((f32[512,128]{1,0:T(8,128)S(1)}, f32[512,128]{1,0:T(8,128)S(1)}, u32[]{:S(2)}, u32[]{:S(2)}) %collective-permute-start.1) | collective-permute-done | bytes 262176 | tf_op jit(solution)/shard_map/ppermute | solution.py:331
  22.5 2.5 %collective-permute-start.3 = (f32[512,128]{1,0:T(8,128)S(1)}, f32[512,128]{1,0:T(8,128)S(1)}, u32[]{:S(2)}, u32[]{:S(2)}) collective-permute-start(f32[512,128]{1,0:T(8,128)S(1)} %join.1), channel_id=1, source_target_pairs={{0,2},{1,3},{2,0},{3,1},{4,6},{5,7},{6,4},{7,5},{8,10},{9,11},{10,... | collective-permute-start | bytes 786440 | tf_op jit(solution)/shard_map/ppermute | solution.py:359
  24.9 1.1 %collective-permute-done.5.refs_5_.refs_8_ = f32[2,192,128]{2,1,0:T(8,128)S(1)} collective-permute-done((f32[2,192,128]{2,1,0:T(8,128)S(1)}, f32[2,192,128]{2,1,0:T(8,128)S(1)}, u32[]{:S(2)}, u32[]{:S(2)}) %collective-permute-start.5) | collective-permute-done | bytes 196640 | tf_op jit(solution)/shard_map/ppermute | solution.py:332
  26.0 0.9 %second_last.1.refs_9_ = f32[1024,128]{1,0:T(8,128)S(1)} custom-call(s32[24]{0:T(128)S(1)} %copy-done.3, s32[2,24]{1,0:T(2,128)S(1)} %bitcast.17, f32[4,4,24]{2,1,0:T(4,128)S(1)} %bitcast.7, f32[4,4,24]{2,1,0:T(4,128)S(1)} %bitcast.12, bf16[3,256,2048]{2,1,0:T(8,128)(2,1)S(1)} %get-tuple-element.39.refs_4_, ...), custom_call_target="tpu_custom_call" | custom-call | flops 1 | bytes 1 | tf_op jit(solution)/shard_map/second_last/pallas_call | solution.py:231
  26.9 3.4 %collective-permute-start.6 = (f32[512,128]{1,0:T(8,128)S(1)}, f32[512,128]{1,0:T(8,128)S(1)}, u32[]{:S(2)}, u32[]{:S(2)}) collective-permute-start(f32[512,128]{1,0:T(8,128)S(1)} %get-tuple-element.56), channel_id=1, source_target_pairs={{0,1},{1,0},{2,3},{3,2},{4,5},{5,4},{6,7},{7,6},{8,9},{9,8},{10,11... | collective-permute-start | bytes 786440 | tf_op jit(solution)/shard_map/ppermute | solution.py:349
  30.2 0.4 collective-permute-done.4.refs_4_
  30.6 3.5 %second_rest.1 = f32[512,128]{1,0:T(8,128)S(1)} custom-call(s32[24]{0:T(128)S(1)} %copy-done.3, s32[2,24]{1,0:T(2,128)S(1)} %bitcast.18, f32[4,4,24]{2,1,0:T(4,128)S(1)} %bitcast.8, f32[4,4,24]{2,1,0:T(4,128)S(1)} %bitcast.13, f32[2048,128]{1,0:T(8,128)S(1)} %collective-permute-done.4.refs_4_, f32[6,2,128,128]{3,2,1,0:T(8,128)} %refs_5_.4, ...), custom_call_target="tpu_custom_call" | custom-call | flops 1 | bytes 1 | tf_op jit(solution)/shard_map/second_rest/pallas_call | solution.py:231
  34.1 1.7 %collective-permute-start.7 = (f32[512,128]{1,0:T(8,128)S(1)}, f32[512,128]{1,0:T(8,128)S(1)}, u32[]{:S(2)}, u32[]{:S(2)}) collective-permute-start(f32[512,128]{1,0:T(8,128)S(1)} %second_rest.1), channel_id=1, source_target_pairs={{0,2},{1,3},{2,0},{3,1},{4,6},{5,7},{6,4},{7,5},{8,10},{9,11},{10,... | collective-permute-start | bytes 786440 | tf_op jit(solution)/shard_map/ppermute | solution.py:360
  35.9 1.1 %collective-permute-done.3.refs_3_ = f32[512,128]{1,0:T(8,128)S(1)} collective-permute-done((f32[512,128]{1,0:T(8,128)S(1)}, f32[512,128]{1,0:T(8,128)S(1)}, u32[]{:S(2)}, u32[]{:S(2)}) %collective-permute-start.3) | collective-permute-done | bytes 262176 | tf_op jit(solution)/shard_map/ppermute | solution.py:359
  37.0 3.5 %second_mine.1.refs_2_ = f32[512,128]{1,0:T(8,128)S(1)} custom-call(s32[24]{0:T(128)S(1)} %copy-done.3, s32[2,24]{1,0:T(2,128)S(1)} %bitcast.19, f32[4,4,24]{2,1,0:T(4,128)S(1)} %bitcast.9, f32[4,4,24]{2,1,0:T(4,128)S(1)} %bitcast.14, f32[2048,128]{1,0:T(8,128)S(1)} %collective-permute-done.4.refs_4_, f32[6,2,128,128]{3,2,1,0:T(8,128)} %refs_5_.4, ...), custom_call_target="tpu_custom_call" | custom-call | flops 1 | bytes 1 | tf_op jit(solution)/shard_map/second_mine/pallas_call | solution.py:231
  40.6 2.0 %collective-permute-done.6.refs_2_ = f32[512,128]{1,0:T(8,128)S(1)} collective-permute-done((f32[512,128]{1,0:T(8,128)S(1)}, f32[512,128]{1,0:T(8,128)S(1)}, u32[]{:S(2)}, u32[]{:S(2)}) %collective-permute-start.6) | collective-permute-done | bytes 262176 | tf_op jit(solution)/shard_map/ppermute | solution.py:349
  42.5 1.5 %finish_first.1 = (f32[2,512,128]{2,1,0:T(8,128)}, f32[32,128]{1,0:T(8,128)S(1)}) custom-call(s32[2,2]{1,0:T(2,128)} %refs_0_.10, f32[512,128]{1,0:T(8,128)S(1)} %get-tuple-element.55.refs_1_, f32[512,128]{1,0:T(8,128)S(1)} %collective-permute-done.6.refs_2_, f32[512,128]{1,0:T(8,128)S(1)} %collective-permute-done.3.refs_3_), custom_call_target="tpu_custom_call" | custom-call | flops 1 | bytes 1 | tf_op jit(solution)/shard_map/finish_first/pallas_call | solution.py:368
  44.0 4.4 %collective-permute-done.7.refs_3_ = f32[512,128]{1,0:T(8,128)S(1)} collective-permute-done((f32[512,128]{1,0:T(8,128)S(1)}, f32[512,128]{1,0:T(8,128)S(1)}, u32[]{:S(2)}, u32[]{:S(2)}) %collective-permute-start.7) | collective-permute-done | bytes 262176 | tf_op jit(solution)/shard_map/ppermute | solution.py:360
  48.4 0.8 %finish_second.1 = f32[2,512,128]{2,1,0:T(8,128)} custom-call(f32[2,512,128]{2,1,0:T(8,128)} %get-tuple-element.58.refs_0_, f32[32,128]{1,0:T(8,128)S(1)} %get-tuple-element.59.refs_1_, f32[512,128]{1,0:T(8,128)S(1)} %second_mine.1.refs_2_, f32[512,128]{1,0:T(8,128)S(1)} %collective-permute-done.7.refs_3_), custom_call_target="tpu_custom_call", output_to_operand_aliasing={{}: (0, {})} | custom-call | flops 1 | bytes 1 | tf_op jit(solution)/shard_map/finish_second/pallas_call | solution.py:368
  (1 shorter events, 0.0 us)
Async XLA Ops:
  0.0 7.1 %copy-start.2 = (s32[24,2]{0,1:T(2,128)S(1)}, s32[24,2]{0,1:T(2,128)}, u32[]{:S(2)}) copy-start(s32[24,2]{0,1:T(2,128)} %param.10) | copy-start | bytes 580
  0.0 7.1 %copy-start = (f32[24,4,4]{0,2,1:T(4,128)S(1)}, f32[24,4,4]{0,2,1:T(4,128)}, u32[]{:S(2)}) copy-start(f32[24,4,4]{0,2,1:T(4,128)} %param.14) | copy-start | bytes 4612
  0.0 7.1 %copy-start.1 = (f32[24,4,4]{0,2,1:T(4,128)S(1)}, f32[24,4,4]{0,2,1:T(4,128)}, u32[]{:S(2)}) copy-start(f32[24,4,4]{0,2,1:T(4,128)} %param.15) | copy-start | bytes 4612
  0.0 7.1 %copy-start.3 = (s32[24]{0:T(128)S(1)}, s32[24]{0:T(128)}, u32[]{:S(2)}) copy-start(s32[24]{0:T(128)} %refs_0_.11) | copy-start | bytes 292
  1.9 5.1 %collective-permute-start = (f32[2048,128]{1,0:T(8,128)S(1)}, f32[2048,128]{1,0:T(8,128)S(1)}, u32[]{:S(2)}, u32[]{:S(2)}) collective-permute-start(f32[2048,128]{1,0:T(8,128)S(1)} %get-tuple-element.33.refs_4_), channel_id=1, source_target_pairs={{0,4},{4,0},{8,12},{12,8},{16,20},{20,16},{24,28},{28,24},{1,5},{5... | collective-permute-start | bytes 3145736 | tf_op jit(solution)/shard_map/ppermute | solution.py:319
  2.7 27.9 %collective-permute-start.4 = (f32[2048,128]{1,0:T(8,128)S(1)}, f32[2048,128]{1,0:T(8,128)S(1)}, u32[]{:S(2)}, u32[]{:S(2)}) collective-permute-start(f32[2048,128]{1,0:T(8,128)S(1)} %get-tuple-element.34.refs_5_), channel_id=1, source_target_pairs={{4,8},{12,16},{20,24},{8,4},{16,12},{24,20},{5,9},{13,17},{21,25},... | collective-permute-start | bytes 3145736 | tf_op jit(solution)/shard_map/ppermute | solution.py:318
  5.7 11.1 %collective-permute-start.2 = (f32[4,192,128]{2,1,0:T(8,128)S(1)}, f32[4,192,128]{2,1,0:T(8,128)S(1)}, u32[]{:S(2)}, u32[]{:S(2)}) collective-permute-start(f32[4,192,128]{2,1,0:T(8,128)S(1)} %get-tuple-element.40), channel_id=1, source_target_pairs={{0,1},{1,0},{2,3},{3,2},{4,5},{5,4},{6,7},{7,6},{8,9},{9,8},{10,11... | collective-permute-start | bytes 1179656 | tf_op jit(solution)/shard_map/ppermute | solution.py:320
  13.7 8.8 %collective-permute-start.1 = (f32[512,128]{1,0:T(8,128)S(1)}, f32[512,128]{1,0:T(8,128)S(1)}, u32[]{:S(2)}, u32[]{:S(2)}) collective-permute-start(f32[512,128]{1,0:T(8,128)S(1)} %get-tuple-element.38), channel_id=1, source_target_pairs={{0,1},{1,0},{2,3},{3,2},{4,5},{5,4},{6,7},{7,6},{8,9},{9,8},{10,11... | collective-permute-start | bytes 786440 | tf_op jit(solution)/shard_map/ppermute | solution.py:331
  14.9 11.1 %collective-permute-start.5 = (f32[2,192,128]{2,1,0:T(8,128)S(1)}, f32[2,192,128]{2,1,0:T(8,128)S(1)}, u32[]{:S(2)}, u32[]{:S(2)}) collective-permute-start(f32[2,192,128]{2,1,0:T(8,128)S(1)} %get-tuple-element.44), channel_id=1, source_target_pairs={{0,1},{1,0},{2,3},{3,2},{4,5},{5,4},{6,7},{7,6},{8,9},{9,8},{10,11... | collective-permute-start | bytes 589832 | tf_op jit(solution)/shard_map/ppermute | solution.py:332
  22.5 14.5 %collective-permute-start.3 = (f32[512,128]{1,0:T(8,128)S(1)}, f32[512,128]{1,0:T(8,128)S(1)}, u32[]{:S(2)}, u32[]{:S(2)}) collective-permute-start(f32[512,128]{1,0:T(8,128)S(1)} %join.1), channel_id=1, source_target_pairs={{0,2},{1,3},{2,0},{3,1},{4,6},{5,7},{6,4},{7,5},{8,10},{9,11},{10,... | collective-permute-start | bytes 786440 | tf_op jit(solution)/shard_map/ppermute | solution.py:359
  26.9 15.6 %collective-permute-start.6 = (f32[512,128]{1,0:T(8,128)S(1)}, f32[512,128]{1,0:T(8,128)S(1)}, u32[]{:S(2)}, u32[]{:S(2)}) collective-permute-start(f32[512,128]{1,0:T(8,128)S(1)} %get-tuple-element.56), channel_id=1, source_target_pairs={{0,1},{1,0},{2,3},{3,2},{4,5},{5,4},{6,7},{7,6},{8,9},{9,8},{10,11... | collective-permute-start | bytes 786440 | tf_op jit(solution)/shard_map/ppermute | solution.py:349
  34.1 14.3 %collective-permute-start.7 = (f32[512,128]{1,0:T(8,128)S(1)}, f32[512,128]{1,0:T(8,128)S(1)}, u32[]{:S(2)}, u32[]{:S(2)}) collective-permute-start(f32[512,128]{1,0:T(8,128)S(1)} %second_rest.1), channel_id=1, source_target_pairs={{0,2},{1,3},{2,0},{3,1},{4,6},{5,7},{6,4},{7,5},{8,10},{9,11},{10,... | collective-permute-start | bytes 786440 | tf_op jit(solution)/shard_map/ppermute | solution.py:360

commit v6 on v5

--- a/solution.py
+++ b/solution.py
@@ -87,12 +87,13 @@
 
 
 class Call:
-    def __init__(self, name, first, cuts, slots=(), own=(), packets=(), added=False, near=None):
+    def __init__(self, name, first, cuts, slots=(), own=(), packets=(), added=False, near=None, whole=()):
         self.name, self.first, self.cuts, self.slots = name, first, cuts, slots
         self.own, self.packets, self.added, self.near = own, packets, added, near
         self.leads = 0 in slots
         self.far = slots == (2,)
-        self.kept = not slots
+        self.whole = whole
+        self.kept = not slots or bool(whole)
 
 
 def apply_kernel(call, groups, rows, bond, site, terms, *refs):
@@ -100,7 +101,7 @@
     take = lambda count: [refs.pop(0) for _ in range(count)]
     table_refs = take(4)
     blocks = take(len(call.slots))
-    source = take(1)[0] if call.kept else None
+    kept = source = take(1)[0] if call.kept else None
     left_ref, right_ref = take(2) if call.own else (None, None)
     packets = take(len(call.packets))
     before_ref = take(1)[0] if call.added else None
@@ -118,11 +119,12 @@
 
     tables = (charge_ref, allowed_ref, one_ref, two_ref)
     copies = [pltpu.make_async_copy(a, b, sem.at[i]) for i, (a, b) in enumerate(zip(table_refs, tables))]
-    sides = [(packet, partner_of(z) * terms + skip) for packet, skip in zip(packets, call.packets)]
+    sides = [(packet, partner_of(z) * terms + skip, call.near) for packet, skip in zip(packets, call.packets)]
+    sides += [(packets[i], partner_of(z) * terms + call.packets[i], True) for i in call.whole]
     if call.own:
         env, env_sem = take(2)
         copies += env_copies(call.first, call.own, groups, rows, left_ref, right_ref, env, env_sem)
-        sides.append((env, z * terms))
+        sides.append((env, z * terms, call.near))
     for copy in copies:
         copy.start()
 
@@ -145,7 +147,7 @@
     for copy in copies:
         copy.wait()
 
-    def add_term(env, w, term, slot):
+    def add_term(env, w, term, source, slot):
         left = env[w, low:high, :]
         left_rest = left - left.astype(jnp.bfloat16).astype(jnp.float32)
         stacked = jnp.concatenate([left, left_rest], axis=0).astype(jnp.bfloat16)
@@ -180,24 +182,26 @@
                     at = (low + start - first_row) * states
                     out[at : at + size, :] += got
 
-    for env, first_term in sides:
-
-        def one_term(w, carry, env=env, first_term=first_term):
+    for env, first_term, near in sides:
+
+        def one_term(w, carry, env=env, first_term=first_term, near=near):
             term = first_term + w
             charge = charge_ref[term]
             shifted = sector - charge
             inside = (shifted >= 0) & (shifted <= 1)
             wanted = allowed_ref[sector, term] != 0
-            if call.near is not None:
-                wanted = wanted & (inside if call.near else jnp.logical_not(inside))
-            if call.far:
+            if near is not None:
+                wanted = wanted & (inside if near else jnp.logical_not(inside))
+            chosen = source
+            if call.far and not near:
                 slot = 0
             else:
+                chosen = kept if call.kept else source
                 slot = jnp.where(inside, jnp.where(charge == 0, 0 if call.first else 1, 1 if call.first else 0), 2)
 
             @pl.when(wanted)
             def _():
-                add_term(env, w, term, slot)
+                add_term(env, w, term, chosen, slot)
 
             return carry
 
@@ -343,12 +347,10 @@
         name="join",
     )(first_rest, rest_got)
     first_rest, before = lax.optimization_barrier((first_rest, before))
-    call = Call("second_last", False, every, packets=(early,), added=True, near=True)
-    (before,) = apply_terms(call, sizes, tables, (source, last_env, before))
-    before, mine_away = lax.optimization_barrier((before, mine_away))
+    last_env, mine_away = lax.optimization_barrier((last_env, mine_away))
     mine_got = lax.ppermute(mine_away, "mpo", swap)
-    operands = (halo_second, *envs, early_env, last_env, before)
-    far = dict(slots=(2,), own=(True,), packets=(0, early), added=True, near=False)
+    operands = (halo_second, source, *envs, early_env, last_env, before)
+    far = dict(slots=(2,), own=(True,), packets=(0, early), added=True, near=False, whole=(1,))
     call = Call("second_rest", False, rest, **far)
     (second_rest,) = apply_terms(call, sizes, tables, operands)
 

time: 50.1 us -> 50.7 us (1.012)
  Pallas kernels: 23.5 us -> 20.9 us
  waiting for transfers between devices: 11.5 us -> 13.4 us
  starting transfers between devices: 14.2 us -> 15.3 us
    ppermute x1, waiting for transfers between devices: 4.42 us -> 7.27 us  [body(): lax.ppermute(second_rest[(r - 1) * cut:r * cut], 'mpo', route)]
    pallas_call x5 -> x4, Pallas kernels: 19.2 us -> 16.6 us  [apply_terms(): pl.pallas_call(functools.partial(apply_kernel, call, *sizes), out_shape=t...]
    ppermute x1, waiting for transfers between devices: 0.36 us -> 2.6 us  [body(): lax.ppermute(outer, 'blk', crossing + [(b, a) for a, b in crossing])]
    ppermute x1, waiting for transfers between devices: 1.95 us -> 0.01 us  [body(): mine_got = lax.ppermute(mine_away, 'mpo', swap)]
    ppermute x1, starting transfers between devices: 1.74 us -> 3.4 us  [body(): lax.ppermute(second_rest[(r - 1) * cut:r * cut], 'mpo', route)]
    ppermute x1, starting transfers between devices: 3.35 us -> 2.06 us  [body(): mine_got = lax.ppermute(mine_away, 'mpo', swap)]
    ppermute x1, waiting for transfers between devices: 1.13 us -> 0.01 us  [body(): lax.ppermute(first_rest[(r - 1) * cut:r * cut], 'mpo', route)]
    ppermute x1, starting transfers between devices: 0.27 us -> 1.31 us  [body(): last_env = lax.ppermute(last_packed, 'mpo', swap)]
  transfers between devices with their start and end apart: 8 -> 8, of which waited for: 7 -> 5; matrix products, arithmetic and copies ran while one was open for 0% -> 0% of each run, Pallas kernels for 42% -> 37%
where the time goes in v6:
time: 50.7 us; the launch traced here: 49.7 us
  Pallas kernels  20.9 us (41%)
  starting transfers between devices  15.3 us (30%)
  waiting for transfers between devices  13.4 us (26%)
    pallas_call x4, Pallas kernels, apply_terms(): pl.pallas_call(functools.partial(apply_kernel, call, *sizes), out_shape=t...  16.6 us
    ppermute x1, waiting for transfers between devices, body(): lax.ppermute(second_rest[(r - 1) * cut:r * cut], 'mpo', route)  7.27 us
    ppermute x1, starting transfers between devices, body(): lax.ppermute(second_rest[(r - 1) * cut:r * cut], 'mpo', route)  3.4 us
    ppermute x1, starting transfers between devices, body(): lax.ppermute(first_rest[(r - 1) * cut:r * cut], 'mpo', route)  3.16 us
    ppermute x1, starting transfers between devices, body(): lax.ppermute(outer, 'blk', crossing + [(b, a) for a, b in crossing])  3.02 us
    ppermute x1, waiting for transfers between devices, body(): lax.ppermute(outer, 'blk', crossing + [(b, a) for a, b in crossing])  2.6 us
    pallas_call x2, Pallas kernels, finish(): pl.pallas_call(functools.partial(finish_kernel, first, rows, states, bond...  2.34 us
    ppermute x1, starting transfers between devices, body(): mine_got = lax.ppermute(mine_away, 'mpo', swap)  2.06 us
  transfers between devices with their start and end apart: 8, of which 5 were waited for; matrix products, arithmetic and copies ran while one was open for 0% of the time, Pallas kernels for 37%

profile of v6, /device:TPU:3, one launch (start us, length us, event | category | flops | bytes accessed | tf_op | source)
XLA Modules:
  0.0 49.7 jit_solution(11749618964400353331)
XLA Ops:
  0.0 0.0 copy-start.2
  0.0 0.0 copy-start
  0.0 0.0 copy-start.1
  0.0 0.0 copy-start.3
  0.0 1.9 %front.1 = (f32[2048,128]{1,0:T(8,128)S(1)}, f32[2048,128]{1,0:T(8,128)S(1)}, f32[4,192,128]{2,1,0:T(8,128)S(1)}, f32[2,192,128]{2,1,0:T(8,128)S(1)}) custom-call(s32[2,2]{1,0:T(2,128)} %refs_0_.8, f32[2,2048,128]{2,1,0:T(8,128)} %bitcast.17, f32[6,2,128,128]{3,2,1,0:T(8,128)} %refs_6_.4, f32[6,2,128,128]{3,2,1,0:T(8,128)} %refs_7_.4), custom_call_target="tpu_custom_call" | custom-call | flops 1 | bytes 1 | tf_op jit(solution)/shard_map/front/pallas_call | solution.py:303
  1.9 0.7 %collective-permute-start = (f32[2048,128]{1,0:T(8,128)S(1)}, f32[2048,128]{1,0:T(8,128)S(1)}, u32[]{:S(2)}, u32[]{:S(2)}) collective-permute-start(f32[2048,128]{1,0:T(8,128)S(1)} %get-tuple-element.34.refs_4_), channel_id=1, source_target_pairs={{0,4},{4,0},{8,12},{12,8},{16,20},{20,16},{24,28},{28,24},{1,5},{5... | collective-permute-start | bytes 3145736 | tf_op jit(solution)/shard_map/ppermute | solution.py:323
  2.7 3.0 %collective-permute-start.4 = (f32[2048,128]{1,0:T(8,128)S(1)}, f32[2048,128]{1,0:T(8,128)S(1)}, u32[]{:S(2)}, u32[]{:S(2)}) collective-permute-start(f32[2048,128]{1,0:T(8,128)S(1)} %get-tuple-element.35.refs_5_), channel_id=1, source_target_pairs={{4,8},{12,16},{20,24},{8,4},{16,12},{24,20},{5,9},{13,17},{21,25},... | collective-permute-start | bytes 3145736 | tf_op jit(solution)/shard_map/ppermute | solution.py:322
  5.7 1.4 %collective-permute-start.2 = (f32[4,192,128]{2,1,0:T(8,128)S(1)}, f32[4,192,128]{2,1,0:T(8,128)S(1)}, u32[]{:S(2)}, u32[]{:S(2)}) collective-permute-start(f32[4,192,128]{2,1,0:T(8,128)S(1)} %get-tuple-element.41), channel_id=1, source_target_pairs={{0,1},{1,0},{2,3},{3,2},{4,5},{5,4},{6,7},{7,6},{8,9},{9,8},{10,11... | collective-permute-start | bytes 1179656 | tf_op jit(solution)/shard_map/ppermute | solution.py:324
  7.1 0.0 collective-permute-done.refs_6_
  7.1 0.0 copy-done.2
  7.1 0.0 copy-done
  7.1 0.0 copy-done.1
  7.1 0.0 copy-done.3
  7.1 6.6 %first_own.1 = (f32[512,128]{1,0:T(8,128)S(1)}, f32[512,128]{1,0:T(8,128)S(1)}, f32[512,128]{1,0:T(8,128)S(1)}, f32[512,128]{1,0:T(8,128)S(1)}, bf16[3,256,2048]{2,1,0:T(8,128)(2,1)S(1)}) custom-call(s32[24]{0:T(128)S(1)} %copy-done.3, s32[2,24]{1,0:T(2,128)S(1)} %bitcast.13, f32[4,4,24]{2,1,0:T(4,128)S(1)} %bitcast.5, f32[4,4,24]{2,1,0:T(4,128)S(1)} %bitcast.9, ...), custom_call_target="tpu_custom_call" | custom-call | flops 1 | bytes 1 | tf_op jit(solution)/shard_map/first_own/pallas_call | solution.py:235
  13.7 0.2 collective-permute-start.1
  13.9 1.3 %collective-permute-start.5 = (f32[2,192,128]{2,1,0:T(8,128)S(1)}, f32[2,192,128]{2,1,0:T(8,128)S(1)}, u32[]{:S(2)}, u32[]{:S(2)}) collective-permute-start(f32[2,192,128]{2,1,0:T(8,128)S(1)} %get-tuple-element.45), channel_id=1, source_target_pairs={{0,1},{1,0},{2,3},{3,2},{4,5},{5,4},{6,7},{7,6},{8,9},{9,8},{10,11... | collective-permute-start | bytes 589832 | tf_op jit(solution)/shard_map/ppermute | solution.py:336
  15.2 1.2 %collective-permute-done.2.refs_7_.refs_8_ = f32[4,192,128]{2,1,0:T(8,128)S(1)} collective-permute-done((f32[4,192,128]{2,1,0:T(8,128)S(1)}, f32[4,192,128]{2,1,0:T(8,128)S(1)}, u32[]{:S(2)}, u32[]{:S(2)}) %collective-permute-start.2) | collective-permute-done | bytes 393248 | tf_op jit(solution)/shard_map/ppermute | solution.py:324
  16.4 4.0 %second_near.1.refs_10_ = f32[1024,128]{1,0:T(8,128)S(1)} custom-call(s32[24]{0:T(128)S(1)} %copy-done.3, s32[2,24]{1,0:T(2,128)S(1)} %bitcast.14, f32[4,4,24]{2,1,0:T(4,128)S(1)} %bitcast.6, f32[4,4,24]{2,1,0:T(4,128)S(1)} %bitcast.10, bf16[3,256,2048]{2,1,0:T(8,128)(2,1)S(1)} %get-tuple-element.50.refs_4_.refs_5_, f32[6,2,128,128]{3,2,1,0:T(8,128)} %refs_6_.4, ...), custom_call_target="tpu_custom_call" | custom-call | flops 1 | bytes 1 | tf_op jit(solution)/shard_map/second_near/pallas_call | solution.py:235
  20.4 1.3 %collective-permute-done.1.got_ref = f32[512,128]{1,0:T(8,128)S(1)} collective-permute-done((f32[512,128]{1,0:T(8,128)S(1)}, f32[512,128]{1,0:T(8,128)S(1)}, u32[]{:S(2)}, u32[]{:S(2)}) %collective-permute-start.1) | collective-permute-done | bytes 262176 | tf_op jit(solution)/shard_map/ppermute | solution.py:335
  21.8 3.2 %collective-permute-start.3 = (f32[512,128]{1,0:T(8,128)S(1)}, f32[512,128]{1,0:T(8,128)S(1)}, u32[]{:S(2)}, u32[]{:S(2)}) collective-permute-start(f32[512,128]{1,0:T(8,128)S(1)} %join.1), channel_id=1, source_target_pairs={{0,2},{1,3},{2,0},{3,1},{4,6},{5,7},{6,4},{7,5},{8,10},{9,11},{10,... | collective-permute-start | bytes 786440 | tf_op jit(solution)/shard_map/ppermute | solution.py:361
  24.9 1.0 %collective-permute-done.5.refs_9_ = f32[2,192,128]{2,1,0:T(8,128)S(1)} collective-permute-done((f32[2,192,128]{2,1,0:T(8,128)S(1)}, f32[2,192,128]{2,1,0:T(8,128)S(1)}, u32[]{:S(2)}, u32[]{:S(2)}) %collective-permute-start.5) | collective-permute-done | bytes 196640 | tf_op jit(solution)/shard_map/ppermute | solution.py:336
  25.9 2.1 %collective-permute-start.6 = (f32[512,128]{1,0:T(8,128)S(1)}, f32[512,128]{1,0:T(8,128)S(1)}, u32[]{:S(2)}, u32[]{:S(2)}) collective-permute-start(f32[512,128]{1,0:T(8,128)S(1)} %get-tuple-element.58), channel_id=1, source_target_pairs={{0,1},{1,0},{2,3},{3,2},{4,5},{5,4},{6,7},{7,6},{8,9},{9,8},{10,11... | collective-permute-start | bytes 786440 | tf_op jit(solution)/shard_map/ppermute | solution.py:351
  28.0 2.6 %collective-permute-done.4.refs_4_ = f32[2048,128]{1,0:T(8,128)S(1)} collective-permute-done((f32[2048,128]{1,0:T(8,128)S(1)}, f32[2048,128]{1,0:T(8,128)S(1)}, u32[]{:S(2)}, u32[]{:S(2)}) %collective-permute-start.4) | collective-permute-done | bytes 1048608 | tf_op jit(solution)/shard_map/ppermute | solution.py:322
  30.6 3.0 %second_rest.1 = f32[512,128]{1,0:T(8,128)S(1)} custom-call(s32[24]{0:T(128)S(1)} %copy-done.3, s32[2,24]{1,0:T(2,128)S(1)} %bitcast.15, f32[4,4,24]{2,1,0:T(4,128)S(1)} %bitcast.7, f32[4,4,24]{2,1,0:T(4,128)S(1)} %bitcast.11, f32[2048,128]{1,0:T(8,128)S(1)} %collective-permute-done.4.refs_4_, bf16[3,256,2048]{2,1,0:T(8,128)(2,1)S(1)} %get-tuple-element.50.refs_4_.refs_5_, ...), custom_call_target="tpu_custom_call" | custom-call | flops 1 | bytes 1 | tf_op jit(solution)/shard_map/second_rest/pallas_call | solution.py:235
  33.6 3.4 %collective-permute-start.7 = (f32[512,128]{1,0:T(8,128)S(1)}, f32[512,128]{1,0:T(8,128)S(1)}, u32[]{:S(2)}, u32[]{:S(2)}) collective-permute-start(f32[512,128]{1,0:T(8,128)S(1)} %second_rest.1), channel_id=1, source_target_pairs={{0,2},{1,3},{2,0},{3,1},{4,6},{5,7},{6,4},{7,5},{8,10},{9,11},{10,... | collective-permute-start | bytes 786440 | tf_op jit(solution)/shard_map/ppermute | solution.py:362
  37.0 0.0 collective-permute-done.3.refs_3_
  37.0 3.0 %second_mine.1.refs_2_ = f32[512,128]{1,0:T(8,128)S(1)} custom-call(s32[24]{0:T(128)S(1)} %copy-done.3, s32[2,24]{1,0:T(2,128)S(1)} %bitcast.16, f32[4,4,24]{2,1,0:T(4,128)S(1)} %bitcast.8, f32[4,4,24]{2,1,0:T(4,128)S(1)} %bitcast.12, f32[2048,128]{1,0:T(8,128)S(1)} %collective-permute-done.4.refs_4_, ...), custom_call_target="tpu_custom_call" | custom-call | flops 1 | bytes 1 | tf_op jit(solution)/shard_map/second_mine/pallas_call | solution.py:235
  40.1 0.0 collective-permute-done.6.refs_2_
  40.1 1.5 %finish_first.1 = (f32[2,512,128]{2,1,0:T(8,128)}, f32[32,128]{1,0:T(8,128)S(1)}) custom-call(s32[2,2]{1,0:T(2,128)} %refs_0_.8, f32[512,128]{1,0:T(8,128)S(1)} %get-tuple-element.57.refs_1_, f32[512,128]{1,0:T(8,128)S(1)} %collective-permute-done.6.refs_2_, f32[512,128]{1,0:T(8,128)S(1)} %collective-permute-done.3.refs_3_), custom_call_target="tpu_custom_call" | custom-call | flops 1 | bytes 1 | tf_op jit(solution)/shard_map/finish_first/pallas_call | solution.py:370
  41.6 7.3 %collective-permute-done.7.refs_3_ = f32[512,128]{1,0:T(8,128)S(1)} collective-permute-done((f32[512,128]{1,0:T(8,128)S(1)}, f32[512,128]{1,0:T(8,128)S(1)}, u32[]{:S(2)}, u32[]{:S(2)}) %collective-permute-start.7) | collective-permute-done | bytes 262176 | tf_op jit(solution)/shard_map/ppermute | solution.py:362
  48.9 0.8 %finish_second.1 = f32[2,512,128]{2,1,0:T(8,128)} custom-call(f32[2,512,128]{2,1,0:T(8,128)} %get-tuple-element.60.refs_0_, f32[32,128]{1,0:T(8,128)S(1)} %get-tuple-element.61.refs_1_, f32[512,128]{1,0:T(8,128)S(1)} %second_mine.1.refs_2_, f32[512,128]{1,0:T(8,128)S(1)} %collective-permute-done.7.refs_3_), custom_call_target="tpu_custom_call", output_to_operand_aliasing={{}: (0, {})} | custom-call | flops 1 | bytes 1 | tf_op jit(solution)/shard_map/finish_second/pallas_call | solution.py:370
  (1 shorter events, 0.0 us)
Async XLA Ops:
  0.0 7.1 %copy-start.2 = (s32[24,2]{0,1:T(2,128)S(1)}, s32[24,2]{0,1:T(2,128)}, u32[]{:S(2)}) copy-start(s32[24,2]{0,1:T(2,128)} %param.10) | copy-start | bytes 580
  0.0 7.1 %copy-start = (f32[24,4,4]{0,2,1:T(4,128)S(1)}, f32[24,4,4]{0,2,1:T(4,128)}, u32[]{:S(2)}) copy-start(f32[24,4,4]{0,2,1:T(4,128)} %param.14) | copy-start | bytes 4612
  0.0 7.1 %copy-start.1 = (f32[24,4,4]{0,2,1:T(4,128)S(1)}, f32[24,4,4]{0,2,1:T(4,128)}, u32[]{:S(2)}) copy-start(f32[24,4,4]{0,2,1:T(4,128)} %param.15) | copy-start | bytes 4612
  0.0 7.1 %copy-start.3 = (s32[24]{0:T(128)S(1)}, s32[24]{0:T(128)}, u32[]{:S(2)}) copy-start(s32[24]{0:T(128)} %refs_0_.9) | copy-start | bytes 292
  1.9 5.1 %collective-permute-start = (f32[2048,128]{1,0:T(8,128)S(1)}, f32[2048,128]{1,0:T(8,128)S(1)}, u32[]{:S(2)}, u32[]{:S(2)}) collective-permute-start(f32[2048,128]{1,0:T(8,128)S(1)} %get-tuple-element.34.refs_4_), channel_id=1, source_target_pairs={{0,4},{4,0},{8,12},{12,8},{16,20},{20,16},{24,28},{28,24},{1,5},{5... | collective-permute-start | bytes 3145736 | tf_op jit(solution)/shard_map/ppermute | solution.py:323
  2.7 27.9 %collective-permute-start.4 = (f32[2048,128]{1,0:T(8,128)S(1)}, f32[2048,128]{1,0:T(8,128)S(1)}, u32[]{:S(2)}, u32[]{:S(2)}) collective-permute-start(f32[2048,128]{1,0:T(8,128)S(1)} %get-tuple-element.35.refs_5_), channel_id=1, source_target_pairs={{4,8},{12,16},{20,24},{8,4},{16,12},{24,20},{5,9},{13,17},{21,25},... | collective-permute-start | bytes 3145736 | tf_op jit(solution)/shard_map/ppermute | solution.py:322
  5.7 10.7 %collective-permute-start.2 = (f32[4,192,128]{2,1,0:T(8,128)S(1)}, f32[4,192,128]{2,1,0:T(8,128)S(1)}, u32[]{:S(2)}, u32[]{:S(2)}) collective-permute-start(f32[4,192,128]{2,1,0:T(8,128)S(1)} %get-tuple-element.41), channel_id=1, source_target_pairs={{0,1},{1,0},{2,3},{3,2},{4,5},{5,4},{6,7},{7,6},{8,9},{9,8},{10,11... | collective-permute-start | bytes 1179656 | tf_op jit(solution)/shard_map/ppermute | solution.py:324
  13.7 8.1 %collective-permute-start.1 = (f32[512,128]{1,0:T(8,128)S(1)}, f32[512,128]{1,0:T(8,128)S(1)}, u32[]{:S(2)}, u32[]{:S(2)}) collective-permute-start(f32[512,128]{1,0:T(8,128)S(1)} %get-tuple-element.39), channel_id=1, source_target_pairs={{0,1},{1,0},{2,3},{3,2},{4,5},{5,4},{6,7},{7,6},{8,9},{9,8},{10,11... | collective-permute-start | bytes 786440 | tf_op jit(solution)/shard_map/ppermute | solution.py:335
  13.9 12.0 %collective-permute-start.5 = (f32[2,192,128]{2,1,0:T(8,128)S(1)}, f32[2,192,128]{2,1,0:T(8,128)S(1)}, u32[]{:S(2)}, u32[]{:S(2)}) collective-permute-start(f32[2,192,128]{2,1,0:T(8,128)S(1)} %get-tuple-element.45), channel_id=1, source_target_pairs={{0,1},{1,0},{2,3},{3,2},{4,5},{5,4},{6,7},{7,6},{8,9},{9,8},{10,11... | collective-permute-start | bytes 589832 | tf_op jit(solution)/shard_map/ppermute | solution.py:336
  21.8 15.3 %collective-permute-start.3 = (f32[512,128]{1,0:T(8,128)S(1)}, f32[512,128]{1,0:T(8,128)S(1)}, u32[]{:S(2)}, u32[]{:S(2)}) collective-permute-start(f32[512,128]{1,0:T(8,128)S(1)} %join.1), channel_id=1, source_target_pairs={{0,2},{1,3},{2,0},{3,1},{4,6},{5,7},{6,4},{7,5},{8,10},{9,11},{10,... | collective-permute-start | bytes 786440 | tf_op jit(solution)/shard_map/ppermute | solution.py:361
  25.9 14.1 %collective-permute-start.6 = (f32[512,128]{1,0:T(8,128)S(1)}, f32[512,128]{1,0:T(8,128)S(1)}, u32[]{:S(2)}, u32[]{:S(2)}) collective-permute-start(f32[512,128]{1,0:T(8,128)S(1)} %get-tuple-element.58), channel_id=1, source_target_pairs={{0,1},{1,0},{2,3},{3,2},{4,5},{5,4},{6,7},{7,6},{8,9},{9,8},{10,11... | collective-permute-start | bytes 786440 | tf_op jit(solution)/shard_map/ppermute | solution.py:351
  33.6 15.3 %collective-permute-start.7 = (f32[512,128]{1,0:T(8,128)S(1)}, f32[512,128]{1,0:T(8,128)S(1)}, u32[]{:S(2)}, u32[]{:S(2)}) collective-permute-start(f32[512,128]{1,0:T(8,128)S(1)} %second_rest.1), channel_id=1, source_target_pairs={{0,2},{1,3},{2,0},{3,1},{4,6},{5,7},{6,4},{7,5},{8,10},{9,11},{10,... | collective-permute-start | bytes 786440 | tf_op jit(solution)/shard_map/ppermute | solution.py:362

commit v7 on v6

--- a/solution.py
+++ b/solution.py
@@ -125,7 +125,9 @@
         env, env_sem = take(2)
         copies += env_copies(call.first, call.own, groups, rows, left_ref, right_ref, env, env_sem)
         sides.append((env, z * terms, call.near))
-    for copy in copies:
+    late = copies[len(tables) :]
+    copies = copies[: len(tables)]
+    for copy in copies + late:
         copy.start()
 
     for i, ref in enumerate(blocks):
@@ -182,7 +184,10 @@
                     at = (low + start - first_row) * states
                     out[at : at + size, :] += got
 
-    for env, first_term, near in sides:
+    for n, (env, first_term, near) in enumerate(sides):
+        if n == len(sides) - 1:
+            for copy in late:
+                copy.wait()
 
         def one_term(w, carry, env=env, first_term=first_term, near=near):
             term = first_term + w
@@ -265,6 +270,7 @@
         col = lax.broadcasted_iota(jnp.int32, (block, bond), 1)
         return ((row < dims[sector, 0]) & (col < dims[sector, 1])).astype(jnp.float32)
 
+    copies = []
     for start in range(0, rows, block):
         if first:
             keep = mask(sector, start)
@@ -277,9 +283,11 @@
             for other in parts[1:]:
                 value = value + other[at : at + block, :]
             held[pl.ds(start * states + p, block, stride=states), :] = value * keep
-    copy = pltpu.make_async_copy(held, out_ref.at[sector], sem.at[0])
-    copy.start()
-    copy.wait()
+        some = pl.ds(start * states, block * states)
+        copies.append(pltpu.make_async_copy(held.at[some, :], out_ref.at[sector, some, :], sem.at[2 + len(copies)]))
+        copies[-1].start()
+    for copy in copies:
+        copy.wait()
 
 
 def body(theta, block_dims, pair_mask, term_charge, left_env, right_env, site_one, site_two):
@@ -364,7 +372,7 @@
     def finish(first, *operands):
         out = jax.ShapeDtypeStruct((sectors, rows * states, bond), jnp.float32)
         keep = jax.ShapeDtypeStruct((rows, bond), jnp.float32)
-        scratch = [pltpu.VMEM((rows * states, bond), jnp.float32), pltpu.SemaphoreType.DMA((2,))]
+        scratch = [pltpu.VMEM((rows * states, bond), jnp.float32), pltpu.SemaphoreType.DMA((2 + rows // min(rows, 16),))]
         if first:
             scratch.append(pltpu.SMEM(block_dims.shape, block_dims.dtype))
         return pl.pallas_call(

time: 50.7 us -> 49.7 us (0.980); the launches traced: 49.7 us -> 49.6 us
  starting transfers between devices: 15.3 us -> 13.9 us
  Pallas kernels: 20.9 us -> 22 us
    ppermute x1, waiting for transfers between devices: 1.29 us -> 0.01 us  [body(): rest_got = lax.ppermute(rest_away, 'mpo', swap)]
    pallas_call x4, Pallas kernels: 16.6 us -> 17.8 us  [apply_terms(): pl.pallas_call(functools.partial(apply_kernel, call, *sizes), out_shape=t...]
    ppermute x1, waiting for transfers between devices: 0.01 us -> 0.92 us  [body(): lax.ppermute(first_rest[(r - 1) * cut:r * cut], 'mpo', route)]
    ppermute x1, starting transfers between devices: 3.16 us -> 2.32 us  [body(): lax.ppermute(first_rest[(r - 1) * cut:r * cut], 'mpo', route)]
  transfers between devices with their start and end apart: 8 -> 8, of which waited for: 5 -> 5; matrix products, arithmetic and copies ran while one was open for 0% -> 0% of each run, Pallas kernels for 37% -> 39%
where the time goes in v7:
time: 49.7 us; the launch traced here: 49.6 us
  Pallas kernels  22 us (44%)
  starting transfers between devices  13.9 us (28%)
  waiting for transfers between devices  13.5 us (27%)
    pallas_call x4, Pallas kernels, apply_terms(): pl.pallas_call(functools.partial(apply_kernel, call, *sizes), out_shape=t...  17.8 us
    ppermute x1, waiting for transfers between devices, body(): lax.ppermute(second_rest[(r - 1) * cut:r * cut], 'mpo', route)  7.28 us
    ppermute x1, starting transfers between devices, body(): lax.ppermute(outer, 'blk', crossing + [(b, a) for a, b in crossing])  3.02 us
    ppermute x1, starting transfers between devices, body(): lax.ppermute(second_rest[(r - 1) * cut:r * cut], 'mpo', route)  2.91 us
    ppermute x1, waiting for transfers between devices, body(): lax.ppermute(outer, 'blk', crossing + [(b, a) for a, b in crossing])  2.6 us
    ppermute x1, starting transfers between devices, body(): lax.ppermute(first_rest[(r - 1) * cut:r * cut], 'mpo', route)  2.32 us
    pallas_call x2, Pallas kernels, finish(): pl.pallas_call(functools.partial(finish_kernel, first, rows, states, bond...  2.28 us
    ppermute x1, starting transfers between devices, body(): mine_got = lax.ppermute(mine_away, 'mpo', swap)  2.02 us
  transfers between devices with their start and end apart: 8, of which 5 were waited for; matrix products, arithmetic and copies ran while one was open for 0% of the time, Pallas kernels for 39%

profile of v7, /device:TPU:3, one launch (start us, length us, event | category | flops | bytes accessed | tf_op | source)
XLA Modules:
  0.0 49.6 jit_solution(7472673019598448837)
XLA Ops:
  0.0 0.0 copy-start.2
  0.0 0.0 copy-start
  0.0 0.0 copy-start.1
  0.0 0.0 copy-start.3
  0.0 1.9 %front.1 = (f32[2048,128]{1,0:T(8,128)S(1)}, f32[2048,128]{1,0:T(8,128)S(1)}, f32[4,192,128]{2,1,0:T(8,128)S(1)}, f32[2,192,128]{2,1,0:T(8,128)S(1)}) custom-call(s32[2,2]{1,0:T(2,128)} %refs_0_.8, f32[2,2048,128]{2,1,0:T(8,128)} %bitcast.17, f32[6,2,128,128]{3,2,1,0:T(8,128)} %refs_6_.4, f32[6,2,128,128]{3,2,1,0:T(8,128)} %refs_7_.4), custom_call_target="tpu_custom_call" | custom-call | flops 1 | bytes 1 | tf_op jit(solution)/shard_map/front/pallas_call | solution.py:311
  1.9 0.7 %collective-permute-start = (f32[2048,128]{1,0:T(8,128)S(1)}, f32[2048,128]{1,0:T(8,128)S(1)}, u32[]{:S(2)}, u32[]{:S(2)}) collective-permute-start(f32[2048,128]{1,0:T(8,128)S(1)} %get-tuple-element.34.refs_4_), channel_id=1, source_target_pairs={{0,4},{4,0},{8,12},{12,8},{16,20},{20,16},{24,28},{28,24},{1,5},{5... | collective-permute-start | bytes 3145736 | tf_op jit(solution)/shard_map/ppermute | solution.py:331
  2.7 3.0 %collective-permute-start.4 = (f32[2048,128]{1,0:T(8,128)S(1)}, f32[2048,128]{1,0:T(8,128)S(1)}, u32[]{:S(2)}, u32[]{:S(2)}) collective-permute-start(f32[2048,128]{1,0:T(8,128)S(1)} %get-tuple-element.35.refs_5_), channel_id=1, source_target_pairs={{4,8},{12,16},{20,24},{8,4},{16,12},{24,20},{5,9},{13,17},{21,25},... | collective-permute-start | bytes 3145736 | tf_op jit(solution)/shard_map/ppermute | solution.py:330
  5.7 1.4 %collective-permute-start.2 = (f32[4,192,128]{2,1,0:T(8,128)S(1)}, f32[4,192,128]{2,1,0:T(8,128)S(1)}, u32[]{:S(2)}, u32[]{:S(2)}) collective-permute-start(f32[4,192,128]{2,1,0:T(8,128)S(1)} %get-tuple-element.41), channel_id=1, source_target_pairs={{0,1},{1,0},{2,3},{3,2},{4,5},{5,4},{6,7},{7,6},{8,9},{9,8},{10,11... | collective-permute-start | bytes 1179656 | tf_op jit(solution)/shard_map/ppermute | solution.py:332
  7.1 0.0 collective-permute-done.refs_6_
  7.1 0.0 copy-done.2
  7.1 0.0 copy-done
  7.1 0.0 copy-done.1
  7.1 0.0 copy-done.3
  7.1 6.6 %first_own.1 = (f32[512,128]{1,0:T(8,128)S(1)}, f32[512,128]{1,0:T(8,128)S(1)}, f32[512,128]{1,0:T(8,128)S(1)}, f32[512,128]{1,0:T(8,128)S(1)}, bf16[3,256,2048]{2,1,0:T(8,128)(2,1)S(1)}) custom-call(s32[24]{0:T(128)S(1)} %copy-done.3, s32[2,24]{1,0:T(2,128)S(1)} %bitcast.13, f32[4,4,24]{2,1,0:T(4,128)S(1)} %bitcast.5, f32[4,4,24]{2,1,0:T(4,128)S(1)} %bitcast.9, ...), custom_call_target="tpu_custom_call" | custom-call | flops 1 | bytes 1 | tf_op jit(solution)/shard_map/first_own/pallas_call | solution.py:240
  13.7 0.2 collective-permute-start.1
  13.9 1.3 %collective-permute-start.5 = (f32[2,192,128]{2,1,0:T(8,128)S(1)}, f32[2,192,128]{2,1,0:T(8,128)S(1)}, u32[]{:S(2)}, u32[]{:S(2)}) collective-permute-start(f32[2,192,128]{2,1,0:T(8,128)S(1)} %get-tuple-element.45), channel_id=1, source_target_pairs={{0,1},{1,0},{2,3},{3,2},{4,5},{5,4},{6,7},{7,6},{8,9},{9,8},{10,11... | collective-permute-start | bytes 589832 | tf_op jit(solution)/shard_map/ppermute | solution.py:344
  15.2 1.6 %collective-permute-done.2.refs_7_.refs_8_ = f32[4,192,128]{2,1,0:T(8,128)S(1)} collective-permute-done((f32[4,192,128]{2,1,0:T(8,128)S(1)}, f32[4,192,128]{2,1,0:T(8,128)S(1)}, u32[]{:S(2)}, u32[]{:S(2)}) %collective-permute-start.2) | collective-permute-done | bytes 393248 | tf_op jit(solution)/shard_map/ppermute | solution.py:332
  16.8 5.7 %second_near.1.refs_10_ = f32[1024,128]{1,0:T(8,128)S(1)} custom-call(s32[24]{0:T(128)S(1)} %copy-done.3, s32[2,24]{1,0:T(2,128)S(1)} %bitcast.14, f32[4,4,24]{2,1,0:T(4,128)S(1)} %bitcast.6, f32[4,4,24]{2,1,0:T(4,128)S(1)} %bitcast.10, bf16[3,256,2048]{2,1,0:T(8,128)(2,1)S(1)} %get-tuple-element.50.refs_4_.refs_5_, f32[6,2,128,128]{3,2,1,0:T(8,128)} %refs_6_.4, ...), custom_call_target="tpu_custom_call" | custom-call | flops 1 | bytes 1 | tf_op jit(solution)/shard_map/second_near/pallas_call | solution.py:240
  22.6 0.0 collective-permute-done.1.got_ref
  22.6 2.3 %collective-permute-start.3 = (f32[512,128]{1,0:T(8,128)S(1)}, f32[512,128]{1,0:T(8,128)S(1)}, u32[]{:S(2)}, u32[]{:S(2)}) collective-permute-start(f32[512,128]{1,0:T(8,128)S(1)} %join.1), channel_id=1, source_target_pairs={{0,2},{1,3},{2,0},{3,1},{4,6},{5,7},{6,4},{7,5},{8,10},{9,11},{10,... | collective-permute-start | bytes 786440 | tf_op jit(solution)/shard_map/ppermute | solution.py:369
  24.9 1.1 %collective-permute-done.5.refs_9_ = f32[2,192,128]{2,1,0:T(8,128)S(1)} collective-permute-done((f32[2,192,128]{2,1,0:T(8,128)S(1)}, f32[2,192,128]{2,1,0:T(8,128)S(1)}, u32[]{:S(2)}, u32[]{:S(2)}) %collective-permute-start.5) | collective-permute-done | bytes 196640 | tf_op jit(solution)/shard_map/ppermute | solution.py:344
  26.0 2.0 %collective-permute-start.6 = (f32[512,128]{1,0:T(8,128)S(1)}, f32[512,128]{1,0:T(8,128)S(1)}, u32[]{:S(2)}, u32[]{:S(2)}) collective-permute-start(f32[512,128]{1,0:T(8,128)S(1)} %get-tuple-element.58), channel_id=1, source_target_pairs={{0,1},{1,0},{2,3},{3,2},{4,5},{5,4},{6,7},{7,6},{8,9},{9,8},{10,11... | collective-permute-start | bytes 786440 | tf_op jit(solution)/shard_map/ppermute | solution.py:359
  28.0 2.6 %collective-permute-done.4.refs_4_ = f32[2048,128]{1,0:T(8,128)S(1)} collective-permute-done((f32[2048,128]{1,0:T(8,128)S(1)}, f32[2048,128]{1,0:T(8,128)S(1)}, u32[]{:S(2)}, u32[]{:S(2)}) %collective-permute-start.4) | collective-permute-done | bytes 1048608 | tf_op jit(solution)/shard_map/ppermute | solution.py:330
  30.6 2.8 %second_rest.1 = f32[512,128]{1,0:T(8,128)S(1)} custom-call(s32[24]{0:T(128)S(1)} %copy-done.3, s32[2,24]{1,0:T(2,128)S(1)} %bitcast.15, f32[4,4,24]{2,1,0:T(4,128)S(1)} %bitcast.7, f32[4,4,24]{2,1,0:T(4,128)S(1)} %bitcast.11, f32[2048,128]{1,0:T(8,128)S(1)} %collective-permute-done.4.refs_4_, bf16[3,256,2048]{2,1,0:T(8,128)(2,1)S(1)} %get-tuple-element.50.refs_4_.refs_5_, ...), custom_call_target="tpu_custom_call" | custom-call | flops 1 | bytes 1 | tf_op jit(solution)/shard_map/second_rest/pallas_call | solution.py:240
  33.4 2.9 %collective-permute-start.7 = (f32[512,128]{1,0:T(8,128)S(1)}, f32[512,128]{1,0:T(8,128)S(1)}, u32[]{:S(2)}, u32[]{:S(2)}) collective-permute-start(f32[512,128]{1,0:T(8,128)S(1)} %second_rest.1), channel_id=1, source_target_pairs={{0,2},{1,3},{2,0},{3,1},{4,6},{5,7},{6,4},{7,5},{8,10},{9,11},{10,... | collective-permute-start | bytes 786440 | tf_op jit(solution)/shard_map/ppermute | solution.py:370
  36.3 0.9 %collective-permute-done.3.refs_3_ = f32[512,128]{1,0:T(8,128)S(1)} collective-permute-done((f32[512,128]{1,0:T(8,128)S(1)}, f32[512,128]{1,0:T(8,128)S(1)}, u32[]{:S(2)}, u32[]{:S(2)}) %collective-permute-start.3) | collective-permute-done | bytes 262176 | tf_op jit(solution)/shard_map/ppermute | solution.py:369
  37.2 2.8 %second_mine.1.refs_2_ = f32[512,128]{1,0:T(8,128)S(1)} custom-call(s32[24]{0:T(128)S(1)} %copy-done.3, s32[2,24]{1,0:T(2,128)S(1)} %bitcast.16, f32[4,4,24]{2,1,0:T(4,128)S(1)} %bitcast.8, f32[4,4,24]{2,1,0:T(4,128)S(1)} %bitcast.12, f32[2048,128]{1,0:T(8,128)S(1)} %collective-permute-done.4.refs_4_, ...), custom_call_target="tpu_custom_call" | custom-call | flops 1 | bytes 1 | tf_op jit(solution)/shard_map/second_mine/pallas_call | solution.py:240
  40.0 0.0 collective-permute-done.6.refs_2_
  40.0 1.5 %finish_first.1 = (f32[2,512,128]{2,1,0:T(8,128)}, f32[32,128]{1,0:T(8,128)S(1)}) custom-call(s32[2,2]{1,0:T(2,128)} %refs_0_.8, f32[512,128]{1,0:T(8,128)S(1)} %get-tuple-element.57.refs_1_, f32[512,128]{1,0:T(8,128)S(1)} %collective-permute-done.6.refs_2_, f32[512,128]{1,0:T(8,128)S(1)} %collective-permute-done.3.refs_3_), custom_call_target="tpu_custom_call" | custom-call | flops 1 | bytes 1 | tf_op jit(solution)/shard_map/finish_first/pallas_call | solution.py:378
  41.5 7.3 %collective-permute-done.7.refs_3_ = f32[512,128]{1,0:T(8,128)S(1)} collective-permute-done((f32[512,128]{1,0:T(8,128)S(1)}, f32[512,128]{1,0:T(8,128)S(1)}, u32[]{:S(2)}, u32[]{:S(2)}) %collective-permute-start.7) | collective-permute-done | bytes 262176 | tf_op jit(solution)/shard_map/ppermute | solution.py:370
  48.8 0.8 %finish_second.1 = f32[2,512,128]{2,1,0:T(8,128)} custom-call(f32[2,512,128]{2,1,0:T(8,128)} %get-tuple-element.60.refs_0_, f32[32,128]{1,0:T(8,128)S(1)} %get-tuple-element.61.refs_1_, f32[512,128]{1,0:T(8,128)S(1)} %second_mine.1.refs_2_, f32[512,128]{1,0:T(8,128)S(1)} %collective-permute-done.7.refs_3_), custom_call_target="tpu_custom_call", output_to_operand_aliasing={{}: (0, {})} | custom-call | flops 1 | bytes 1 | tf_op jit(solution)/shard_map/finish_second/pallas_call | solution.py:378
  (1 shorter events, 0.0 us)
Async XLA Ops:
  0.0 7.1 %copy-start.2 = (s32[24,2]{0,1:T(2,128)S(1)}, s32[24,2]{0,1:T(2,128)}, u32[]{:S(2)}) copy-start(s32[24,2]{0,1:T(2,128)} %param.10) | copy-start | bytes 580
  0.0 7.1 %copy-start = (f32[24,4,4]{0,2,1:T(4,128)S(1)}, f32[24,4,4]{0,2,1:T(4,128)}, u32[]{:S(2)}) copy-start(f32[24,4,4]{0,2,1:T(4,128)} %param.14) | copy-start | bytes 4612
  0.0 7.1 %copy-start.1 = (f32[24,4,4]{0,2,1:T(4,128)S(1)}, f32[24,4,4]{0,2,1:T(4,128)}, u32[]{:S(2)}) copy-start(f32[24,4,4]{0,2,1:T(4,128)} %param.15) | copy-start | bytes 4612
  0.0 7.1 %copy-start.3 = (s32[24]{0:T(128)S(1)}, s32[24]{0:T(128)}, u32[]{:S(2)}) copy-start(s32[24]{0:T(128)} %refs_0_.9) | copy-start | bytes 292
  1.9 5.1 %collective-permute-start = (f32[2048,128]{1,0:T(8,128)S(1)}, f32[2048,128]{1,0:T(8,128)S(1)}, u32[]{:S(2)}, u32[]{:S(2)}) collective-permute-start(f32[2048,128]{1,0:T(8,128)S(1)} %get-tuple-element.34.refs_4_), channel_id=1, source_target_pairs={{0,4},{4,0},{8,12},{12,8},{16,20},{20,16},{24,28},{28,24},{1,5},{5... | collective-permute-start | bytes 3145736 | tf_op jit(solution)/shard_map/ppermute | solution.py:331
  2.7 27.9 %collective-permute-start.4 = (f32[2048,128]{1,0:T(8,128)S(1)}, f32[2048,128]{1,0:T(8,128)S(1)}, u32[]{:S(2)}, u32[]{:S(2)}) collective-permute-start(f32[2048,128]{1,0:T(8,128)S(1)} %get-tuple-element.35.refs_5_), channel_id=1, source_target_pairs={{4,8},{12,16},{20,24},{8,4},{16,12},{24,20},{5,9},{13,17},{21,25},... | collective-permute-start | bytes 3145736 | tf_op jit(solution)/shard_map/ppermute | solution.py:330
  5.7 11.1 %collective-permute-start.2 = (f32[4,192,128]{2,1,0:T(8,128)S(1)}, f32[4,192,128]{2,1,0:T(8,128)S(1)}, u32[]{:S(2)}, u32[]{:S(2)}) collective-permute-start(f32[4,192,128]{2,1,0:T(8,128)S(1)} %get-tuple-element.41), channel_id=1, source_target_pairs={{0,1},{1,0},{2,3},{3,2},{4,5},{5,4},{6,7},{7,6},{8,9},{9,8},{10,11... | collective-permute-start | bytes 1179656 | tf_op jit(solution)/shard_map/ppermute | solution.py:332
  13.7 8.9 %collective-permute-start.1 = (f32[512,128]{1,0:T(8,128)S(1)}, f32[512,128]{1,0:T(8,128)S(1)}, u32[]{:S(2)}, u32[]{:S(2)}) collective-permute-start(f32[512,128]{1,0:T(8,128)S(1)} %get-tuple-element.39), channel_id=1, source_target_pairs={{0,1},{1,0},{2,3},{3,2},{4,5},{5,4},{6,7},{7,6},{8,9},{9,8},{10,11... | collective-permute-start | bytes 786440 | tf_op jit(solution)/shard_map/ppermute | solution.py:343
  13.9 12.1 %collective-permute-start.5 = (f32[2,192,128]{2,1,0:T(8,128)S(1)}, f32[2,192,128]{2,1,0:T(8,128)S(1)}, u32[]{:S(2)}, u32[]{:S(2)}) collective-permute-start(f32[2,192,128]{2,1,0:T(8,128)S(1)} %get-tuple-element.45), channel_id=1, source_target_pairs={{0,1},{1,0},{2,3},{3,2},{4,5},{5,4},{6,7},{7,6},{8,9},{9,8},{10,11... | collective-permute-start | bytes 589832 | tf_op jit(solution)/shard_map/ppermute | solution.py:344
  22.6 14.6 %collective-permute-start.3 = (f32[512,128]{1,0:T(8,128)S(1)}, f32[512,128]{1,0:T(8,128)S(1)}, u32[]{:S(2)}, u32[]{:S(2)}) collective-permute-start(f32[512,128]{1,0:T(8,128)S(1)} %join.1), channel_id=1, source_target_pairs={{0,2},{1,3},{2,0},{3,1},{4,6},{5,7},{6,4},{7,5},{8,10},{9,11},{10,... | collective-permute-start | bytes 786440 | tf_op jit(solution)/shard_map/ppermute | solution.py:369
  26.0 14.0 %collective-permute-start.6 = (f32[512,128]{1,0:T(8,128)S(1)}, f32[512,128]{1,0:T(8,128)S(1)}, u32[]{:S(2)}, u32[]{:S(2)}) collective-permute-start(f32[512,128]{1,0:T(8,128)S(1)} %get-tuple-element.58), channel_id=1, source_target_pairs={{0,1},{1,0},{2,3},{3,2},{4,5},{5,4},{6,7},{7,6},{8,9},{9,8},{10,11... | collective-permute-start | bytes 786440 | tf_op jit(solution)/shard_map/ppermute | solution.py:359
  33.4 15.4 %collective-permute-start.7 = (f32[512,128]{1,0:T(8,128)S(1)}, f32[512,128]{1,0:T(8,128)S(1)}, u32[]{:S(2)}, u32[]{:S(2)}) collective-permute-start(f32[512,128]{1,0:T(8,128)S(1)} %second_rest.1), channel_id=1, source_target_pairs={{0,2},{1,3},{2,0},{3,1},{4,6},{5,7},{6,4},{7,5},{8,10},{9,11},{10,... | collective-permute-start | bytes 786440 | tf_op jit(solution)/shard_map/ppermute | solution.py:370

commit v8 on v7

--- a/solution.py
+++ b/solution.py
@@ -355,12 +355,12 @@
         name="join",
     )(first_rest, rest_got)
     first_rest, before = lax.optimization_barrier((first_rest, before))
-    last_env, mine_away = lax.optimization_barrier((last_env, mine_away))
-    mine_got = lax.ppermute(mine_away, "mpo", swap)
     operands = (halo_second, source, *envs, early_env, last_env, before)
     far = dict(slots=(2,), own=(True,), packets=(0, early), added=True, near=False, whole=(1,))
     call = Call("second_rest", False, rest, **far)
     (second_rest,) = apply_terms(call, sizes, tables, operands)
+    second_rest, mine_away = lax.optimization_barrier((second_rest, mine_away))
+    mine_got = lax.ppermute(mine_away, "mpo", swap)
 
     first_parts, second_parts = [mine_got], []
     cut = rows * states

time: 49.7 us -> 50.9 us (1.024)
  waiting for transfers between devices: 13.5 us -> 17.6 us
  Pallas kernels: 22 us -> 20.6 us
  starting transfers between devices: 13.9 us -> 12.6 us
    ppermute x1, waiting for transfers between devices: 0.01 us -> 8.8 us  [body(): mine_got = lax.ppermute(mine_away, 'mpo', swap)]
    ppermute x1, waiting for transfers between devices: 7.28 us -> 0.01 us  [body(): lax.ppermute(second_rest[(r - 1) * cut:r * cut], 'mpo', route)]
    ppermute x1, waiting for transfers between devices: 2.6 us -> 5.68 us  [body(): lax.ppermute(outer, 'blk', crossing + [(b, a) for a, b in crossing])]
    pallas_call x4, Pallas kernels: 17.8 us -> 16.4 us  [apply_terms(): pl.pallas_call(functools.partial(apply_kernel, call, *sizes), out_shape=t...]
    ppermute x1, waiting for transfers between devices: 1.06 us -> 0.01 us  [body(): last_env = lax.ppermute(last_packed, 'mpo', swap)]
    ppermute x1, starting transfers between devices: 2.91 us -> 2.01 us  [body(): lax.ppermute(second_rest[(r - 1) * cut:r * cut], 'mpo', route)]
    ppermute x1, waiting for transfers between devices: 1.63 us -> 2.29 us  [body(): early_env = lax.ppermute(early_packed, 'mpo', swap)]
  transfers between devices with their start and end apart: 8 -> 8, of which waited for: 5 -> 4; matrix products, arithmetic and copies ran while one was open for 0% -> 0% of each run, Pallas kernels for 39% -> 35%
where the time goes in v8:
time: 50.9 us
  Pallas kernels  20.6 us (40%)
  waiting for transfers between devices  17.6 us (35%)
  starting transfers between devices  12.6 us (25%)
    pallas_call x4, Pallas kernels, apply_terms(): pl.pallas_call(functools.partial(apply_kernel, call, *sizes), out_shape=t...  16.4 us
    ppermute x1, waiting for transfers between devices, body(): mine_got = lax.ppermute(mine_away, 'mpo', swap)  8.8 us
    ppermute x1, waiting for transfers between devices, body(): lax.ppermute(outer, 'blk', crossing + [(b, a) for a, b in crossing])  5.68 us
    ppermute x1, starting transfers between devices, body(): lax.ppermute(outer, 'blk', crossing + [(b, a) for a, b in crossing])  3.02 us
    ppermute x1, waiting for transfers between devices, body(): early_env = lax.ppermute(early_packed, 'mpo', swap)  2.29 us
    pallas_call x2, Pallas kernels, finish(): pl.pallas_call(functools.partial(finish_kernel, first, rows, states, bond...  2.28 us
    ppermute x1, starting transfers between devices, body(): lax.ppermute(first_rest[(r - 1) * cut:r * cut], 'mpo', route)  2.03 us
    ppermute x1, starting transfers between devices, body(): lax.ppermute(second_rest[(r - 1) * cut:r * cut], 'mpo', route)  2.01 us
  transfers between devices with their start and end apart: 8, of which 4 were waited for; matrix products, arithmetic and copies ran while one was open for 0% of the time, Pallas kernels for 35%

profile of v8, /device:TPU:3, one launch (start us, length us, event | category | flops | bytes accessed | tf_op | source)
XLA Modules:
  0.0 50.9 jit_solution(2458658515177063980)
XLA Ops:
  0.0 0.0 copy-start.2
  0.0 0.0 copy-start
  0.0 0.0 copy-start.1
  0.0 0.0 copy-start.3
  0.0 1.9 %front.1 = (f32[2048,128]{1,0:T(8,128)S(1)}, f32[2048,128]{1,0:T(8,128)S(1)}, f32[4,192,128]{2,1,0:T(8,128)S(1)}, f32[2,192,128]{2,1,0:T(8,128)S(1)}) custom-call(s32[2,2]{1,0:T(2,128)} %refs_0_.9, f32[2,2048,128]{2,1,0:T(8,128)} %bitcast.17, f32[6,2,128,128]{3,2,1,0:T(8,128)} %refs_6_.4, f32[6,2,128,128]{3,2,1,0:T(8,128)} %refs_7_.4), custom_call_target="tpu_custom_call" | custom-call | flops 1 | bytes 1 | tf_op jit(solution)/shard_map/front/pallas_call | solution.py:311
  1.9 0.7 %collective-permute-start = (f32[2048,128]{1,0:T(8,128)S(1)}, f32[2048,128]{1,0:T(8,128)S(1)}, u32[]{:S(2)}, u32[]{:S(2)}) collective-permute-start(f32[2048,128]{1,0:T(8,128)S(1)} %get-tuple-element.34.refs_4_), channel_id=1, source_target_pairs={{0,4},{4,0},{8,12},{12,8},{16,20},{20,16},{24,28},{28,24},{1,5},{5... | collective-permute-start | bytes 3145736 | tf_op jit(solution)/shard_map/ppermute | solution.py:331
  2.7 3.0 %collective-permute-start.4 = (f32[2048,128]{1,0:T(8,128)S(1)}, f32[2048,128]{1,0:T(8,128)S(1)}, u32[]{:S(2)}, u32[]{:S(2)}) collective-permute-start(f32[2048,128]{1,0:T(8,128)S(1)} %get-tuple-element.35.refs_5_), channel_id=1, source_target_pairs={{4,8},{12,16},{20,24},{8,4},{16,12},{24,20},{5,9},{13,17},{21,25},... | collective-permute-start | bytes 3145736 | tf_op jit(solution)/shard_map/ppermute | solution.py:330
  5.7 1.4 %collective-permute-start.2 = (f32[4,192,128]{2,1,0:T(8,128)S(1)}, f32[4,192,128]{2,1,0:T(8,128)S(1)}, u32[]{:S(2)}, u32[]{:S(2)}) collective-permute-start(f32[4,192,128]{2,1,0:T(8,128)S(1)} %get-tuple-element.41), channel_id=1, source_target_pairs={{0,1},{1,0},{2,3},{3,2},{4,5},{5,4},{6,7},{7,6},{8,9},{9,8},{10,11... | collective-permute-start | bytes 1179656 | tf_op jit(solution)/shard_map/ppermute | solution.py:332
  7.1 0.0 collective-permute-done.refs_6_
  7.1 0.0 copy-done.2
  7.1 0.0 copy-done
  7.1 0.0 copy-done.1
  7.1 0.0 copy-done.3
  7.1 5.5 %first_own.1 = (f32[512,128]{1,0:T(8,128)S(1)}, f32[512,128]{1,0:T(8,128)S(1)}, f32[512,128]{1,0:T(8,128)S(1)}, f32[512,128]{1,0:T(8,128)S(1)}, bf16[3,256,2048]{2,1,0:T(8,128)(2,1)S(1)}) custom-call(s32[24]{0:T(128)S(1)} %copy-done.3, s32[2,24]{1,0:T(2,128)S(1)} %bitcast.13, f32[4,4,24]{2,1,0:T(4,128)S(1)} %bitcast.5, f32[4,4,24]{2,1,0:T(4,128)S(1)} %bitcast.9, ...), custom_call_target="tpu_custom_call" | custom-call | flops 1 | bytes 1 | tf_op jit(solution)/shard_map/first_own/pallas_call | solution.py:240
  12.6 0.2 collective-permute-start.1
  12.9 1.3 %collective-permute-start.5 = (f32[2,192,128]{2,1,0:T(8,128)S(1)}, f32[2,192,128]{2,1,0:T(8,128)S(1)}, u32[]{:S(2)}, u32[]{:S(2)}) collective-permute-start(f32[2,192,128]{2,1,0:T(8,128)S(1)} %get-tuple-element.45), channel_id=1, source_target_pairs={{0,1},{1,0},{2,3},{3,2},{4,5},{5,4},{6,7},{7,6},{8,9},{9,8},{10,11... | collective-permute-start | bytes 589832 | tf_op jit(solution)/shard_map/ppermute | solution.py:344
  14.2 2.3 %collective-permute-done.2.refs_7_.refs_8_ = f32[4,192,128]{2,1,0:T(8,128)S(1)} collective-permute-done((f32[4,192,128]{2,1,0:T(8,128)S(1)}, f32[4,192,128]{2,1,0:T(8,128)S(1)}, u32[]{:S(2)}, u32[]{:S(2)}) %collective-permute-start.2) | collective-permute-done | bytes 393248 | tf_op jit(solution)/shard_map/ppermute | solution.py:332
  16.4 6.4 %second_near.1.refs_10_ = f32[1024,128]{1,0:T(8,128)S(1)} custom-call(s32[24]{0:T(128)S(1)} %copy-done.3, s32[2,24]{1,0:T(2,128)S(1)} %bitcast.14, f32[4,4,24]{2,1,0:T(4,128)S(1)} %bitcast.6, f32[4,4,24]{2,1,0:T(4,128)S(1)} %bitcast.10, bf16[3,256,2048]{2,1,0:T(8,128)(2,1)S(1)} %get-tuple-element.48.refs_4_.refs_5_, f32[6,2,128,128]{3,2,1,0:T(8,128)} %refs_6_.4, ...), custom_call_target="tpu_custom_call" | custom-call | flops 1 | bytes 1 | tf_op jit(solution)/shard_map/second_near/pallas_call | solution.py:240
  22.8 0.0 collective-permute-done.1.got_ref
  22.9 2.0 %collective-permute-start.3 = (f32[512,128]{1,0:T(8,128)S(1)}, f32[512,128]{1,0:T(8,128)S(1)}, u32[]{:S(2)}, u32[]{:S(2)}) collective-permute-start(f32[512,128]{1,0:T(8,128)S(1)} %join.1), channel_id=1, source_target_pairs={{0,2},{1,3},{2,0},{3,1},{4,6},{5,7},{6,4},{7,5},{8,10},{9,11},{10,... | collective-permute-start | bytes 786440 | tf_op jit(solution)/shard_map/ppermute | solution.py:369
  24.9 5.7 %collective-permute-done.4.refs_4_ = f32[2048,128]{1,0:T(8,128)S(1)} collective-permute-done((f32[2048,128]{1,0:T(8,128)S(1)}, f32[2048,128]{1,0:T(8,128)S(1)}, u32[]{:S(2)}, u32[]{:S(2)}) %collective-permute-start.4) | collective-permute-done | bytes 1048608 | tf_op jit(solution)/shard_map/ppermute | solution.py:330
  30.6 0.0 collective-permute-done.5.refs_9_
  30.6 2.2 %second_rest.1 = f32[512,128]{1,0:T(8,128)S(1)} custom-call(s32[24]{0:T(128)S(1)} %copy-done.3, s32[2,24]{1,0:T(2,128)S(1)} %bitcast.15, f32[4,4,24]{2,1,0:T(4,128)S(1)} %bitcast.7, f32[4,4,24]{2,1,0:T(4,128)S(1)} %bitcast.11, f32[2048,128]{1,0:T(8,128)S(1)} %collective-permute-done.4.refs_4_, bf16[3,256,2048]{2,1,0:T(8,128)(2,1)S(1)} %get-tuple-element.48.refs_4_.refs_5_, ...), custom_call_target="tpu_custom_call" | custom-call | flops 1 | bytes 1 | tf_op jit(solution)/shard_map/second_rest/pallas_call | solution.py:240
  32.8 1.9 %collective-permute-start.6 = (f32[512,128]{1,0:T(8,128)S(1)}, f32[512,128]{1,0:T(8,128)S(1)}, u32[]{:S(2)}, u32[]{:S(2)}) collective-permute-start(f32[512,128]{1,0:T(8,128)S(1)} %get-tuple-element.57), channel_id=1, source_target_pairs={{0,1},{1,0},{2,3},{3,2},{4,5},{5,4},{6,7},{7,6},{8,9},{9,8},{10,11... | collective-permute-start | bytes 786440 | tf_op jit(solution)/shard_map/ppermute | solution.py:363
  34.7 2.0 %collective-permute-start.7 = (f32[512,128]{1,0:T(8,128)S(1)}, f32[512,128]{1,0:T(8,128)S(1)}, u32[]{:S(2)}, u32[]{:S(2)}) collective-permute-start(f32[512,128]{1,0:T(8,128)S(1)} %second_rest.1), channel_id=1, source_target_pairs={{0,2},{1,3},{2,0},{3,1},{4,6},{5,7},{6,4},{7,5},{8,10},{9,11},{10,... | collective-permute-start | bytes 786440 | tf_op jit(solution)/shard_map/ppermute | solution.py:370
  36.8 0.8 %collective-permute-done.3.refs_3_ = f32[512,128]{1,0:T(8,128)S(1)} collective-permute-done((f32[512,128]{1,0:T(8,128)S(1)}, f32[512,128]{1,0:T(8,128)S(1)}, u32[]{:S(2)}, u32[]{:S(2)}) %collective-permute-start.3) | collective-permute-done | bytes 262176 | tf_op jit(solution)/shard_map/ppermute | solution.py:369
  37.5 2.2 %second_mine.1.refs_2_ = f32[512,128]{1,0:T(8,128)S(1)} custom-call(s32[24]{0:T(128)S(1)} %copy-done.3, s32[2,24]{1,0:T(2,128)S(1)} %bitcast.16, f32[4,4,24]{2,1,0:T(4,128)S(1)} %bitcast.8, f32[4,4,24]{2,1,0:T(4,128)S(1)} %bitcast.12, f32[2048,128]{1,0:T(8,128)S(1)} %collective-permute-done.4.refs_4_, ...), custom_call_target="tpu_custom_call" | custom-call | flops 1 | bytes 1 | tf_op jit(solution)/shard_map/second_mine/pallas_call | solution.py:240
  39.8 8.8 %collective-permute-done.6.refs_2_ = f32[512,128]{1,0:T(8,128)S(1)} collective-permute-done((f32[512,128]{1,0:T(8,128)S(1)}, f32[512,128]{1,0:T(8,128)S(1)}, u32[]{:S(2)}, u32[]{:S(2)}) %collective-permute-start.6) | collective-permute-done | bytes 262176 | tf_op jit(solution)/shard_map/ppermute | solution.py:363
  48.6 1.5 %finish_first.1 = (f32[2,512,128]{2,1,0:T(8,128)}, f32[32,128]{1,0:T(8,128)S(1)}) custom-call(s32[2,2]{1,0:T(2,128)} %refs_0_.9, f32[512,128]{1,0:T(8,128)S(1)} %get-tuple-element.55.refs_1_, f32[512,128]{1,0:T(8,128)S(1)} %collective-permute-done.6.refs_2_, f32[512,128]{1,0:T(8,128)S(1)} %collective-permute-done.3.refs_3_), custom_call_target="tpu_custom_call" | custom-call | flops 1 | bytes 1 | tf_op jit(solution)/shard_map/finish_first/pallas_call | solution.py:378
  50.1 0.0 collective-permute-done.7.refs_3_
  50.1 0.8 %finish_second.1 = f32[2,512,128]{2,1,0:T(8,128)} custom-call(f32[2,512,128]{2,1,0:T(8,128)} %get-tuple-element.59.refs_0_, f32[32,128]{1,0:T(8,128)S(1)} %get-tuple-element.60.refs_1_, f32[512,128]{1,0:T(8,128)S(1)} %second_mine.1.refs_2_, f32[512,128]{1,0:T(8,128)S(1)} %collective-permute-done.7.refs_3_), custom_call_target="tpu_custom_call", output_to_operand_aliasing={{}: (0, {})} | custom-call | flops 1 | bytes 1 | tf_op jit(solution)/shard_map/finish_second/pallas_call | solution.py:378
  (1 shorter events, 0.0 us)
Async XLA Ops:
  0.0 7.1 %copy-start.2 = (s32[24,2]{0,1:T(2,128)S(1)}, s32[24,2]{0,1:T(2,128)}, u32[]{:S(2)}) copy-start(s32[24,2]{0,1:T(2,128)} %param.10) | copy-start | bytes 580
  0.0 7.1 %copy-start = (f32[24,4,4]{0,2,1:T(4,128)S(1)}, f32[24,4,4]{0,2,1:T(4,128)}, u32[]{:S(2)}) copy-start(f32[24,4,4]{0,2,1:T(4,128)} %param.14) | copy-start | bytes 4612
  0.0 7.1 %copy-start.1 = (f32[24,4,4]{0,2,1:T(4,128)S(1)}, f32[24,4,4]{0,2,1:T(4,128)}, u32[]{:S(2)}) copy-start(f32[24,4,4]{0,2,1:T(4,128)} %param.15) | copy-start | bytes 4612
  0.0 7.1 %copy-start.3 = (s32[24]{0:T(128)S(1)}, s32[24]{0:T(128)}, u32[]{:S(2)}) copy-start(s32[24]{0:T(128)} %refs_0_.8) | copy-start | bytes 292
  1.9 5.1 %collective-permute-start = (f32[2048,128]{1,0:T(8,128)S(1)}, f32[2048,128]{1,0:T(8,128)S(1)}, u32[]{:S(2)}, u32[]{:S(2)}) collective-permute-start(f32[2048,128]{1,0:T(8,128)S(1)} %get-tuple-element.34.refs_4_), channel_id=1, source_target_pairs={{0,4},{4,0},{8,12},{12,8},{16,20},{20,16},{24,28},{28,24},{1,5},{5... | collective-permute-start | bytes 3145736 | tf_op jit(solution)/shard_map/ppermute | solution.py:331
  2.7 27.9 %collective-permute-start.4 = (f32[2048,128]{1,0:T(8,128)S(1)}, f32[2048,128]{1,0:T(8,128)S(1)}, u32[]{:S(2)}, u32[]{:S(2)}) collective-permute-start(f32[2048,128]{1,0:T(8,128)S(1)} %get-tuple-element.35.refs_5_), channel_id=1, source_target_pairs={{4,8},{12,16},{20,24},{8,4},{16,12},{24,20},{5,9},{13,17},{21,25},... | collective-permute-start | bytes 3145736 | tf_op jit(solution)/shard_map/ppermute | solution.py:330
  5.7 10.7 %collective-permute-start.2 = (f32[4,192,128]{2,1,0:T(8,128)S(1)}, f32[4,192,128]{2,1,0:T(8,128)S(1)}, u32[]{:S(2)}, u32[]{:S(2)}) collective-permute-start(f32[4,192,128]{2,1,0:T(8,128)S(1)} %get-tuple-element.41), channel_id=1, source_target_pairs={{0,1},{1,0},{2,3},{3,2},{4,5},{5,4},{6,7},{7,6},{8,9},{9,8},{10,11... | collective-permute-start | bytes 1179656 | tf_op jit(solution)/shard_map/ppermute | solution.py:332
  12.6 10.2 %collective-permute-start.1 = (f32[512,128]{1,0:T(8,128)S(1)}, f32[512,128]{1,0:T(8,128)S(1)}, u32[]{:S(2)}, u32[]{:S(2)}) collective-permute-start(f32[512,128]{1,0:T(8,128)S(1)} %get-tuple-element.39), channel_id=1, source_target_pairs={{0,1},{1,0},{2,3},{3,2},{4,5},{5,4},{6,7},{7,6},{8,9},{9,8},{10,11... | collective-permute-start | bytes 786440 | tf_op jit(solution)/shard_map/ppermute | solution.py:343
  12.9 17.7 %collective-permute-start.5 = (f32[2,192,128]{2,1,0:T(8,128)S(1)}, f32[2,192,128]{2,1,0:T(8,128)S(1)}, u32[]{:S(2)}, u32[]{:S(2)}) collective-permute-start(f32[2,192,128]{2,1,0:T(8,128)S(1)} %get-tuple-element.45), channel_id=1, source_target_pairs={{0,1},{1,0},{2,3},{3,2},{4,5},{5,4},{6,7},{7,6},{8,9},{9,8},{10,11... | collective-permute-start | bytes 589832 | tf_op jit(solution)/shard_map/ppermute | solution.py:344
  22.9 14.6 %collective-permute-start.3 = (f32[512,128]{1,0:T(8,128)S(1)}, f32[512,128]{1,0:T(8,128)S(1)}, u32[]{:S(2)}, u32[]{:S(2)}) collective-permute-start(f32[512,128]{1,0:T(8,128)S(1)} %join.1), channel_id=1, source_target_pairs={{0,2},{1,3},{2,0},{3,1},{4,6},{5,7},{6,4},{7,5},{8,10},{9,11},{10,... | collective-permute-start | bytes 786440 | tf_op jit(solution)/shard_map/ppermute | solution.py:369
  32.8 15.7 %collective-permute-start.6 = (f32[512,128]{1,0:T(8,128)S(1)}, f32[512,128]{1,0:T(8,128)S(1)}, u32[]{:S(2)}, u32[]{:S(2)}) collective-permute-start(f32[512,128]{1,0:T(8,128)S(1)} %get-tuple-element.57), channel_id=1, source_target_pairs={{0,1},{1,0},{2,3},{3,2},{4,5},{5,4},{6,7},{7,6},{8,9},{9,8},{10,11... | collective-permute-start | bytes 786440 | tf_op jit(solution)/shard_map/ppermute | solution.py:363
  34.7 15.3 %collective-permute-start.7 = (f32[512,128]{1,0:T(8,128)S(1)}, f32[512,128]{1,0:T(8,128)S(1)}, u32[]{:S(2)}, u32[]{:S(2)}) collective-permute-start(f32[512,128]{1,0:T(8,128)S(1)} %second_rest.1), channel_id=1, source_target_pairs={{0,2},{1,3},{2,0},{3,1},{4,6},{5,7},{6,4},{7,5},{8,10},{9,11},{10,... | collective-permute-start | bytes 786440 | tf_op jit(solution)/shard_map/ppermute | solution.py:370
